TPU v7x, 32 devices: a whole 2x2x4 slice. The times are simulated.
32 devices in a mesh: dp: 2 (over y), row: 4 (over z), col: 4 (over x, core).
Axes of the slice: x: 2, y: 2, z: 4, core: 2. Of those that a mesh axis runs over, the one named last changes fastest.
Arguments:
- inputs: bfloat16 [2, 8, 512, 2048], P(None, ('dp', 'row'), 'col'), may hold values from -6 to 6
- lengths: int32 [2, 8], P(None, ('dp', 'row')), may hold values from 128 to 512, as said below
- wqkv: bfloat16 [2048, 4096], P(('dp', 'row'), 'col'), may hold values from -0.125 to 0.125
- wo: bfloat16 [2048, 2048], P('col', ('dp', 'row')), may hold values from -0.75 to 0.75
- w1: bfloat16 [2048, 8192], P(('dp', 'row'), 'col'), may hold values from -0.125 to 0.125
- w3: bfloat16 [2048, 8192], P(('dp', 'row'), 'col'), may hold values from -0.125 to 0.125
- w2: bfloat16 [8192, 2048], P('col', ('dp', 'row')), may hold values from -0.0625 to 0.0625
- attn_gain: bfloat16 [2048], P(('dp', 'row')), may hold values from 0.099609375 to 1.8984375
- ffn_gain: bfloat16 [2048], P(('dp', 'row')), may hold values from 0.099609375 to 1.8984375
- cotangent: bfloat16 [2, 8, 512, 2048], P(None, ('dp', 'row'), 'col'), may hold values from -6 to 6
Outputs:
- outputs: bfloat16 [2, 8, 512, 2048], P(None, ('dp', 'row'), 'col')
- input_grad: bfloat16 [2, 8, 512, 2048], P(None, ('dp', 'row'), 'col')
- attn_gain_grad: float32 [2048], P(('dp', 'row'))
- ffn_gain_grad: float32 [2048], P(('dp', 'row'))
- wqkv_grad: float32 [2048, 4096], P(('dp', 'row'), 'col')
- wo_grad: float32 [2048, 2048], P('col', ('dp', 'row'))
- w1_grad: float32 [2048, 8192], P(('dp', 'row'), 'col')
- w3_grad: float32 [2048, 8192], P(('dp', 'row'), 'col')
- w2_grad: float32 [8192, 2048], P('col', ('dp', 'row'))
Inputs may be any that keep to these rules, and one draw needn't show every extreme that they name: `lengths`: in every slot one of the 2 micro-batches has length exactly 512; the others lie from 128 to 512.
All inputs are finite; a program needn't handle non-finite values.
Results may differ from a plain program's by a relative error of at most 0.018.
Values may be sent and summed in bfloat16 or wider, within the bound.
No kernel may reach another device: no remote copies, remote signals or barrier semaphores. Data moves between devices by JAX's collectives and lax.ppermute only.
A program may use at most 256 MiB of HBM per device.

v0:
```python
import jax
import jax.numpy as jnp
from jax import lax
from jax.sharding import PartitionSpec as P

HEAD_SIZE = 128
QUERY_PER_GROUP = 2


EPS = 1e-05
THETA = 1000000.0
NEGATIVE = -1e30


def rope_tables(token_rows, head):
    places = jnp.arange(token_rows, dtype=jnp.float32)
    freqs = THETA ** (-jnp.arange(head // 2, dtype=jnp.float32) * 2.0 / head)
    angles = places[:, None] * freqs[None, :]
    return (jnp.cos(angles), jnp.sin(angles))


def rotate(values, cosine, sine):
    half = values.shape[-1] // 2
    first_half = values[..., :half]
    second_half = values[..., half:]
    cos_view = cosine[:, None, None, :]
    sin_view = sine[:, None, None, :]
    return jnp.concatenate(
        [
            first_half * cos_view - second_half * sin_view,
            second_half * cos_view + first_half * sin_view,
        ],
        axis=-1,
    )


def unrotate(grads, cosine, sine):
    half = grads.shape[-1] // 2
    first_half = grads[..., :half]
    second_half = grads[..., half:]
    cos_view = cosine[:, None, None, :]
    sin_view = sine[:, None, None, :]
    return jnp.concatenate(
        [
            first_half * cos_view + second_half * sin_view,
            second_half * cos_view - first_half * sin_view,
        ],
        axis=-1,
    )


def rms_norm(values, gain):
    inverse = lax.rsqrt(jnp.mean(values * values, axis=-1, keepdims=True) + EPS)
    return (values * inverse * gain, inverse)


def rms_back(values, inverse, gain, upstream):
    scaled = upstream * gain
    inner = jnp.mean(scaled * values, axis=-1, keepdims=True)
    grad_in = inverse * scaled - values * (inverse * inverse * inverse) * inner
    grad_gain = jnp.sum(upstream * values * inverse, axis=0)
    return (grad_in, grad_gain)


def contract_rows(left, right):
    return lax.dot_general(
        left, right, (((0,), (0,)), ((), ())), preferred_element_type=jnp.float32
    )


def contract_cols(left, right):
    return lax.dot_general(
        left, right, (((1,), (1,)), ((), ())), preferred_element_type=jnp.float32
    )


def score_block(query_block, keys, start, length, score_scale):
    block = query_block.shape[0]
    key_pos = jnp.arange(keys.shape[0], dtype=jnp.int32)
    query_pos = start + jnp.arange(block, dtype=jnp.int32)
    scores = (
        jnp.einsum("qgrd,kgd->grqk", query_block, keys, preferred_element_type=jnp.float32)
        * score_scale
    )
    allowed = (key_pos[None, :] <= query_pos[:, None]) & (key_pos[None, :] < length)
    return jnp.where(allowed, scores, NEGATIVE)


def attend(query, keys, values, length, score_scale):
    token_rows = query.shape[0]
    block = min(token_rows, 512)
    count = token_rows // block

    def one_block(index):
        start = index * block
        scores = score_block(query, keys, start, length, score_scale)
        highest = jnp.max(scores, axis=-1, keepdims=True)
        expo = jnp.exp(scores - highest)
        total = jnp.sum(expo, axis=-1, keepdims=True)
        probs = (expo / total).astype(jnp.bfloat16)
        attended = jnp.einsum("grqk,kgd->qgrd", probs, values, preferred_element_type=jnp.float32)
        return (attended.astype(jnp.bfloat16), highest[..., 0] + jnp.log(total[..., 0]))

    attended, log_totals = lax.map(one_block, jnp.arange(count, dtype=jnp.int32))
    return (attended.reshape(query.shape), log_totals)


def attend_back(query, keys, values, log_totals, grad_out, length, score_scale):
    token_rows = query.shape[0]
    block = min(token_rows, 512)
    count = token_rows // block

    def one_block(carry, index):
        keys_acc, values_acc = carry
        start = index * block
        scores = score_block(query, keys, start, length, score_scale)
        probs = jnp.exp(scores - log_totals[index][..., None])
        grad_probs = jnp.einsum(
            "qgrd,kgd->grqk", grad_out, values, preferred_element_type=jnp.float32
        )
        values_acc = values_acc + jnp.einsum(
            "grqk,qgrd->kgd",
            probs.astype(jnp.bfloat16),
            grad_out,
            preferred_element_type=jnp.float32,
        )
        inner = jnp.sum(probs * grad_probs, axis=-1, keepdims=True)
        grad_scores = (probs * (grad_probs - inner)).astype(jnp.bfloat16)
        query_grad = (
            jnp.einsum("grqk,kgd->qgrd", grad_scores, keys, preferred_element_type=jnp.float32)
            * score_scale
        )
        keys_acc = (
            keys_acc
            + jnp.einsum("grqk,qgrd->kgd", grad_scores, query, preferred_element_type=jnp.float32)
            * score_scale
        )
        return ((keys_acc, values_acc), query_grad)

    empty = jnp.zeros(keys.shape, jnp.float32)
    (keys_grad, values_grad), query_grad = lax.scan(
        one_block, (empty, empty), jnp.arange(count, dtype=jnp.int32)
    )
    return (query_grad.reshape(query.shape), keys_grad, values_grad)


def fetch(wqkv, wo, w1, w3, w2, attn_gain, ffn_gain):
    return (
        lax.all_gather(wqkv, ("dp", "row"), axis=0, tiled=True),
        lax.all_gather(wo, ("dp", "row"), axis=1, tiled=True),
        lax.all_gather(jnp.stack((w1, w3)), ("dp", "row"), axis=1, tiled=True),
        lax.all_gather(w2, ("dp", "row"), axis=1, tiled=True),
        lax.all_gather(jnp.stack((attn_gain, ffn_gain)), ("dp", "row"), axis=1, tiled=True),
    )


def reduce_grads(totals):
    qkv_acc, out_acc, pair_acc, down_acc, gain_acc = totals
    gain_acc = lax.psum(gain_acc, "col")
    return (
        lax.psum_scatter(
            qkv_acc.astype(jnp.bfloat16), ("dp", "row"), scatter_dimension=0, tiled=True
        ).astype(jnp.float32),
        lax.psum_scatter(
            out_acc.astype(jnp.bfloat16), ("dp", "row"), scatter_dimension=1, tiled=True
        ).astype(jnp.float32),
        lax.psum_scatter(
            pair_acc.astype(jnp.bfloat16), ("dp", "row"), scatter_dimension=1, tiled=True
        ).astype(jnp.float32),
        lax.psum_scatter(
            down_acc.astype(jnp.bfloat16), ("dp", "row"), scatter_dimension=1, tiled=True
        ).astype(jnp.float32),
        lax.psum_scatter(
            gain_acc.astype(jnp.bfloat16), ("dp", "row"), scatter_dimension=1, tiled=True
        ).astype(jnp.float32),
    )


def body(inputs, lengths, wqkv, wo, w1, w3, w2, attn_gain, ffn_gain, cotangent):
    col_index = lax.axis_index("col")
    local_rows = inputs.shape[2]
    token_rows = local_rows * lax.axis_size("col")
    model_width = wqkv.shape[0] * lax.axis_size(("dp", "row"))
    groups = wqkv.shape[1] // ((QUERY_PER_GROUP + 2) * HEAD_SIZE)
    cosine, sine = rope_tables(token_rows, HEAD_SIZE)
    score_scale = HEAD_SIZE ** (-0.5)
    totals = (
        jnp.zeros((model_width, wqkv.shape[1]), jnp.float32),
        jnp.zeros((wo.shape[0], model_width), jnp.float32),
        jnp.zeros((2, model_width, w1.shape[1]), jnp.float32),
        jnp.zeros((w2.shape[0], model_width), jnp.float32),
        jnp.zeros((2, model_width), jnp.float32),
    )
    shards = None
    results = []
    source_grads = []
    for micro in range(inputs.shape[0]):
        gathered = fetch(wqkv, wo, w1, w3, w2, attn_gain, ffn_gain)
        qkv_w, out_w, pair_w, down_w, gains = gathered
        gain_attn = gains[0].astype(jnp.float32)
        gain_ffn = gains[1].astype(jnp.float32)
        length = lengths[micro, 0]
        qkv_acc, out_acc, pair_acc, down_acc, gain_acc = totals
        source = inputs[micro, 0].astype(jnp.float32)
        first_normed, inverse1 = rms_norm(source, gain_attn)
        attn_rows = lax.all_gather(first_normed.astype(jnp.bfloat16), "col", axis=0, tiled=True)
        projected_rows = jnp.dot(attn_rows, qkv_w, preferred_element_type=jnp.float32).reshape(
            token_rows, groups, QUERY_PER_GROUP + 2, HEAD_SIZE
        )
        query = rotate(projected_rows[:, :, :QUERY_PER_GROUP], cosine, sine).astype(jnp.bfloat16)
        keys = rotate(projected_rows[:, :, QUERY_PER_GROUP : QUERY_PER_GROUP + 1], cosine, sine)[
            :, :, 0
        ].astype(jnp.bfloat16)
        values = projected_rows[:, :, QUERY_PER_GROUP + 1].astype(jnp.bfloat16)
        attended, log_totals = attend(query, keys, values, length, score_scale)
        attended_flat = attended.reshape(token_rows, -1)
        residual = source + lax.psum_scatter(
            jnp.dot(attended_flat, out_w, preferred_element_type=jnp.float32),
            "col",
            scatter_dimension=0,
            tiled=True,
        )
        normed2, inverse2 = rms_norm(residual, gain_ffn)
        ffn_rows = lax.all_gather(normed2.astype(jnp.bfloat16), "col", axis=0, tiled=True)
        gate_up = jnp.einsum("ld,gdf->lgf", ffn_rows, pair_w, preferred_element_type=jnp.float32)
        gate_val = gate_up[:, 0]
        up_val = gate_up[:, 1]
        sigma = jax.nn.sigmoid(gate_val)
        swish = gate_val * sigma
        hidden = (swish * up_val).astype(jnp.bfloat16)
        result = residual + lax.psum_scatter(
            jnp.dot(hidden, down_w, preferred_element_type=jnp.float32).astype(jnp.bfloat16),
            "col",
            scatter_dimension=0,
            tiled=True,
        ).astype(jnp.float32)
        results.append(result.astype(jnp.bfloat16))
        positions = col_index * local_rows + jnp.arange(local_rows, dtype=jnp.int32)
        valid = (positions < length).astype(jnp.float32)[:, None]
        upstream = cotangent[micro, 0].astype(jnp.float32) * valid
        piece = lax.all_gather(upstream.astype(jnp.bfloat16), "col", axis=0, tiled=True)
        down_sum = down_acc
        down_sum = down_sum + contract_rows(hidden, piece)
        hidden_grad = contract_cols(piece, down_w)
        down_acc, hidden_grad = (down_sum, hidden_grad)
        grad_gate = hidden_grad * up_val * sigma * (1.0 + gate_val * (1.0 - sigma))
        grad_up = hidden_grad * swish
        grad_pair = jnp.stack((grad_gate, grad_up), axis=1).astype(jnp.bfloat16)
        pair_acc = pair_acc + jnp.einsum(
            "ld,lgf->gdf", ffn_rows, grad_pair, preferred_element_type=jnp.float32
        )
        normed2_grad = lax.psum_scatter(
            jnp.einsum("lgf,gdf->ld", grad_pair, pair_w, preferred_element_type=jnp.float32),
            "col",
            scatter_dimension=0,
            tiled=True,
        )
        residual_in, gain2_grad = rms_back(residual, inverse2, gain_ffn, normed2_grad)
        residual_grad = upstream + residual_in
        attn_piece = lax.all_gather(residual_grad.astype(jnp.bfloat16), "col", axis=0, tiled=True)
        out_sum = out_acc
        out_sum = out_sum + contract_rows(attended_flat, attn_piece)
        attended_grad = contract_cols(attn_piece, out_w)
        out_acc, attended_grad = (out_sum, attended_grad)
        grad_out = attended_grad.astype(jnp.bfloat16).reshape(query.shape)
        query_grad, keys_grad, values_grad = attend_back(
            query, keys, values, log_totals, grad_out, length, score_scale
        )
        query_grad = unrotate(query_grad, cosine, sine)
        keys_grad = unrotate(keys_grad[:, :, None], cosine, sine)
        grad_proj = (
            jnp.concatenate((query_grad, keys_grad, values_grad[:, :, None]), axis=2)
            .reshape(token_rows, -1)
            .astype(jnp.bfloat16)
        )
        qkv_acc = qkv_acc + contract_rows(attn_rows, grad_proj)
        normed1_grad = lax.psum_scatter(
            contract_cols(grad_proj, qkv_w), "col", scatter_dimension=0, tiled=True
        )
        source_in, gain1_grad = rms_back(source, inverse1, gain_attn, normed1_grad)
        source_grads.append((residual_grad + source_in).astype(jnp.bfloat16))
        gain_acc = gain_acc + jnp.stack((gain1_grad, gain2_grad))
        totals = (qkv_acc, out_acc, pair_acc, down_acc, gain_acc)
    shards = reduce_grads(totals)
    qkv_shard, out_shard, pair_shard, down_shard, gain_shard = shards
    outputs = jnp.stack(results)[:, None]
    input_grad = jnp.stack(source_grads)[:, None]
    return (
        outputs,
        input_grad,
        gain_shard[0],
        gain_shard[1],
        qkv_shard,
        out_shard,
        pair_shard[0],
        pair_shard[1],
        down_shard,
    )


def solution(mesh):
    in_specs = (
        P(None, ("dp", "row"), "col", None),
        P(None, ("dp", "row")),
        P(("dp", "row"), "col"),
        P("col", ("dp", "row")),
        P(("dp", "row"), "col"),
        P(("dp", "row"), "col"),
        P("col", ("dp", "row")),
        P(("dp", "row")),
        P(("dp", "row")),
        P(None, ("dp", "row"), "col", None),
    )
    out_specs = (
        P(None, ("dp", "row"), "col", None),
        P(None, ("dp", "row"), "col", None),
        P(("dp", "row")),
        P(("dp", "row")),
        P(("dp", "row"), "col"),
        P("col", ("dp", "row")),
        P(("dp", "row"), "col"),
        P(("dp", "row"), "col"),
        P("col", ("dp", "row")),
    )
    return jax.shard_map(body, mesh=mesh, in_specs=in_specs, out_specs=out_specs, check_vma=False)
```

profile of v0, /device:TPU:0, one launch (start us, length us, event | category | flops | bytes accessed | tf_op | source)
XLA Modules:
  0.0 1812.3 jit_solution(6051224787211087116)
XLA Ops:
  8.6 22.3 %all_gather.44 = bf16[2,2048]{1,0:T(2,128)(2,1)S(1)} all-gather(bf16[2,256]{1,0:T(2,128)(2,1)S(1)} %pad_maximum_fusion.15), channel_id=1, replica_groups=mesh['dp'=2,'row'=4,'col'=4] {'dp','row'}, dimensions={1}, use_global_device_ids=true | all-gather | bytes 9216 | tf_op jit(solution)/shard_map/all_gather | solution.py:153
  40.2 15.2 all-gather.13.cloned.1.call-done
  55.4 75.6 %all-gather.15.cloned.1.call-done = bf16[2048,1024]{1,0:T(8,128)(2,1)} async-done(((bf16[256,1024]{1,0:T(8,128)(2,1)}), bf16[2048,1024]{1,0:T(8,128)(2,1)}) %all-gather.15.cloned.1.call-update) | async-done | bytes 4194320 | tf_op jit(solution)/shard_map/all_gather | solution.py:149
  137.5 16.5 all-gather.25.cloned.1.call-done
  165.2 41.7 %all-gather.17.cloned.1.call-done = bf16[512,2048]{1,0:T(8,128)(2,1)} async-done(((bf16[512,256]{1,0:T(8,128)(2,1)}), bf16[512,2048]{1,0:T(8,128)(2,1)}) %all-gather.17.cloned.1.call-update) | async-done | bytes 2097168 | tf_op jit(solution)/shard_map/all_gather | solution.py:150
  211.9 12.2 reduce-scatter.20.cloned.1.call-start
  232.5 22.2 %reduce-scatter.16.cloned.1.call-done = f32[128,2048]{1,0:T(8,128)} async-done(((f32[512,2048]{1,0:T(8,128)}), f32[128,2048]{1,0:T(8,128)}) %reduce-scatter.16.cloned.1.call-update) | async-done | bytes 1048592 | tf_op jit(solution)/shard_map/reduce_scatter | solution.py:217
  254.7 47.1 %reduce-scatter.20.cloned.1.call-done = f32[128,2048]{1,0:T(8,128)} async-done(((f32[512,2048]{1,0:T(8,128)}), f32[128,2048]{1,0:T(8,128)}) %reduce-scatter.20.cloned.1.call-update) | async-done | bytes 1048592 | tf_op jit(solution)/shard_map/reduce_scatter | solution.py:217
  311.0 16.5 all-gather.19.cloned.1.call-done
  327.5 230.4 %all-gather.21.cloned.1.call-done = bf16[2,2048,2048]{2,1,0:T(8,128)(2,1)} async-done(((bf16[2,256,2048]{2,1,0:T(8,128)(2,1)}), bf16[2,2048,2048]{2,1,0:T(8,128)(2,1)}) %all-gather.21.cloned.1.call-update) | async-done | bytes 16777232 | tf_op jit(solution)/shard_map/all_gather | solution.py:151
  557.8 15.0 fusion.24
  580.8 127.3 %all-gather.23.cloned.1.call-done = bf16[2048,2048]{1,0:T(8,128)(2,1)} async-done(((bf16[2048,256]{1,0:T(8,128)(2,1)}), bf16[2048,2048]{1,0:T(8,128)(2,1)}) %all-gather.23.cloned.1.call-update) | async-done | bytes 8388624 | tf_op jit(solution)/shard_map/all_gather | solution.py:152
  708.1 13.6 fusion.30
  723.6 13.8 convolution_bitcast_fusion.1
  737.5 42.8 %reduce-scatter.24.cloned.1.call-done = f32[128,2048]{1,0:T(8,128)} async-done(((f32[512,2048]{1,0:T(8,128)}), f32[128,2048]{1,0:T(8,128)}) %reduce-scatter.24.cloned.1.call-update) | async-done | bytes 1048592 | tf_op jit(solution)/shard_map/reduce_scatter | solution.py:252
  784.5 21.5 %all-gather.27.cloned.1.call-done = bf16[512,2048]{1,0:T(8,128)(2,1)} async-done(((bf16[128,2048]{1,0:T(8,128)(2,1)}), bf16[512,2048]{1,0:T(8,128)(2,1)}) %all-gather.27.cloned.1.call-update) | async-done | bytes 2097168 | tf_op jit(solution)/shard_map/all_gather | solution.py:224
  806.0 15.0 fusion.21
  830.8 13.6 fusion.31
  846.4 13.8 convolution_bitcast_fusion
  880.5 24.4 %reduce-scatter.28.cloned.1.call-done = f32[128,2048]{1,0:T(8,128)} async-done(((f32[512,2048]{1,0:T(8,128)}), f32[128,2048]{1,0:T(8,128)}) %reduce-scatter.28.cloned.1.call-update) | async-done | bytes 1048592 | tf_op jit(solution)/shard_map/reduce_scatter | solution.py:252
  906.4 32.3 %reduce-scatter.18.cloned.1.call-done = bf16[128,2048]{1,0:T(8,128)(2,1)} async-done(((bf16[512,2048]{1,0:T(8,128)(2,1)}), bf16[128,2048]{1,0:T(8,128)(2,1)}) %reduce-scatter.18.cloned.1.call-update) | async-done | bytes 524304 | tf_op jit(solution)/shard_map/reduce_scatter | solution.py:231
  938.8 34.0 %reduce-scatter.22.cloned.1.call-done = bf16[128,2048]{1,0:T(8,128)(2,1)} async-done(((bf16[512,2048]{1,0:T(8,128)(2,1)}), bf16[128,2048]{1,0:T(8,128)(2,1)}) %reduce-scatter.22.cloned.1.call-update) | async-done | bytes 524304 | tf_op jit(solution)/shard_map/reduce_scatter | solution.py:231
  978.2 21.8 %all-gather.31.cloned.1.call-done = bf16[512,2048]{1,0:T(8,128)(2,1)} async-done(((bf16[128,2048]{1,0:T(8,128)(2,1)}), bf16[512,2048]{1,0:T(8,128)(2,1)}) %all-gather.31.cloned.1.call-update) | async-done | bytes 2097168 | tf_op jit(solution)/shard_map/all_gather | solution.py:260
  1009.9 14.8 all-gather.35.cloned.1.call-done
  1086.3 19.9 %fusion.13 = f32[2,2048,2048]{2,1,0:T(8,128)} fusion(bf16[512,1,2048]{2,0,1:T(8,128)(2,1)} %copy-done.71, bf16[512,1,2048]{2,0,1:T(8,128)(2,1)} %copy-done.70, bf16[512,2048]{1,0:T(8,128)(2,1)} %all-gather.19.cloned.1.call-done), kind=kOutput, calls=%fused_computation.47 | convolution fusion | flops 8592031744 | bytes 39845888 | tf_op jit(solution)/shard_map/ld,lgf->gdf/dot_general | solution.py:249
  1106.2 25.1 %reduce-scatter.30.cloned.1.call-done = f32[128,2048]{1,0:T(8,128)} async-done(((f32[512,2048]{1,0:T(8,128)}), f32[128,2048]{1,0:T(8,128)}) %reduce-scatter.30.cloned.1.call-update) | async-done | bytes 1048592 | tf_op jit(solution)/shard_map/reduce_scatter | solution.py:277
  1144.9 20.9 %fusion = bf16[2,2048,2048]{1,2,0:T(8,128)(2,1)} fusion(f32[2,2048,2048]{2,1,0:T(8,128)} %fusion.13, bf16[512,1,2048]{2,0,1:T(8,128)(2,1)} %copy-done.69, bf16[512,1,2048]{2,0,1:T(8,128)(2,1)} %copy-done.68, bf16[512,2048]{1,0:T(8,128)(2,1)} %all-gather.27.cloned.1.call-done), kind=kOutput, calls=%fused_computation.1 | convolution fusion | flops 8608808960 | bytes 56623104 | tf_op jit(solution)/shard_map/ld,lgf->gdf/dot_general | solution.py:249
  1168.3 35.2 %reduce-scatter.34.cloned.1.call-done = bf16[512,256]{1,0:T(8,128)(2,1)} async-done(((bf16[512,2048]{1,0:T(8,128)(2,1)}), bf16[512,256]{1,0:T(8,128)(2,1)}) %reduce-scatter.34.cloned.1.call-update) | async-done | bytes 262160 | tf_op jit(solution)/shard_map/reduce_scatter | solution.py:164
  1205.3 150.3 %reduce-scatter.38.cloned.1.call-done = bf16[2048,256]{1,0:T(8,128)(2,1)} async-done(((bf16[2048,2048]{1,0:T(8,128)(2,1)}), bf16[2048,256]{1,0:T(8,128)(2,1)}) %reduce-scatter.38.cloned.1.call-update) | async-done | bytes 1048592 | tf_op jit(solution)/shard_map/reduce_scatter | solution.py:170
  1358.2 88.3 %reduce-scatter.32.cloned.1.call-done = bf16[256,1024]{1,0:T(8,128)(2,1)} async-done(((bf16[2048,1024]{1,0:T(8,128)(2,1)}), bf16[256,1024]{1,0:T(8,128)(2,1)}) %reduce-scatter.32.cloned.1.call-update) | async-done | bytes 524304 | tf_op jit(solution)/shard_map/reduce_scatter | solution.py:161
  1451.9 60.1 %reduce-scatter.40.cloned.1.call-done = bf16[256,2]{1,0:T(8,128)(2,1)} async-done(((bf16[2048,2]{1,0:T(8,128)(2,1)}), bf16[256,2]{1,0:T(8,128)(2,1)}) %reduce-scatter.40.cloned.1.call-update) | async-done | bytes 1040
  1513.5 283.8 %reduce-scatter.36.cloned.1.call-done = bf16[2,256,2048]{1,2,0:T(8,128)(2,1)} async-done(((bf16[2,2048,2048]{1,2,0:T(8,128)(2,1)}), bf16[2,256,2048]{1,2,0:T(8,128)(2,1)}) %reduce-scatter.36.cloned.1.call-update) | async-done | bytes 2097168 | tf_op jit(solution)/shard_map/reduce_scatter | solution.py:167
  (280 shorter events, 210.3 us)
Async XLA Ops:
  7.2 48.2 %all-gather.13.cloned.1.call-start = ((), (), s32[]{:S(2)}) async-start(), calls=%async_computation.13 | async-start | bytes 2621440 | tf_op jit(solution)/shard_map/all_gather | solution.py:206
  35.4 95.6 %all-gather.15.cloned.1.call-start = ((), (), s32[]{:S(2)}) async-start(), calls=%async_computation.14 | async-start | bytes 4718592 | tf_op jit(solution)/shard_map/all_gather | solution.py:149
  36.2 117.8 %all-gather.25.cloned.1.call-start = ((), (), s32[]{:S(2)}) async-start(), calls=%async_computation.21 | async-start | bytes 2621440 | tf_op jit(solution)/shard_map/all_gather | solution.py:206
  36.9 170.1 %all-gather.17.cloned.1.call-start = ((), (), s32[]{:S(2)}) async-start(), calls=%async_computation.15 | async-start | bytes 2359296 | tf_op jit(solution)/shard_map/all_gather | solution.py:150
  37.5 217.2 %reduce-scatter.16.cloned.1.call-start = ((), (), s32[]{:S(2)}) async-start(), calls=%async_computation.16 | async-start | bytes 5242880 | tf_op jit(solution)/shard_map/reduce_scatter | solution.py:217
  39.3 120.9 %copy-start.14 = (f32[512,64]{0,1:T(8,128)}, f32[512,64]{0,1:T(8,128)S(1)}, u32[]{:S(2)}) copy-start(f32[512,64]{0,1:T(8,128)S(1)} %get-tuple-element.226) | copy-start | bytes 393220
  39.3 120.9 %copy-start.16 = (f32[512,64]{0,1:T(8,128)}, f32[512,64]{0,1:T(8,128)S(1)}, u32[]{:S(2)}) copy-start(f32[512,64]{0,1:T(8,128)S(1)} %get-tuple-element.227) | copy-start | bytes 393220
  211.9 89.9 %reduce-scatter.20.cloned.1.call-start = ((), (), s32[]{:S(2)}) async-start(), calls=%async_computation.22 | async-start | bytes 5242880 | tf_op jit(solution)/shard_map/reduce_scatter | solution.py:217
  232.5 95.0 %all-gather.19.cloned.1.call-start = ((), (), s32[]{:S(2)}) async-start(), calls=%async_computation.17 | async-start | bytes 2621440 | tf_op jit(solution)/shard_map/all_gather | solution.py:224
  304.7 253.1 %all-gather.21.cloned.1.call-start = ((), (), s32[]{:S(2)}) async-start(), calls=%async_computation.18 | async-start | bytes 18874368 | tf_op jit(solution)/shard_map/all_gather | solution.py:151
  307.8 272.9 %all-gather.29.cloned.1.call-start = ((), (), s32[]{:S(2)}) async-start(), calls=%async_computation.25 | async-start | bytes 2621440 | tf_op jit(solution)/shard_map/all_gather | solution.py:241
  310.3 397.7 %all-gather.23.cloned.1.call-start = ((), (), s32[]{:S(2)}) async-start(), calls=%async_computation.19 | async-start | bytes 9437184 | tf_op jit(solution)/shard_map/all_gather | solution.py:152
  310.9 469.3 %reduce-scatter.24.cloned.1.call-start = ((), (), s32[]{:S(2)}) async-start(), calls=%async_computation.26 | async-start | bytes 5242880 | tf_op jit(solution)/shard_map/reduce_scatter | solution.py:252
  737.4 68.6 %all-gather.27.cloned.1.call-start = ((), (), s32[]{:S(2)}) async-start(), calls=%async_computation.23 | async-start | bytes 2621440 | tf_op jit(solution)/shard_map/all_gather | solution.py:224
  783.3 47.6 %all-gather.33.cloned.1.call-start = ((), (), s32[]{:S(2)}) async-start(), calls=%async_computation.29 | async-start | bytes 2621440 | tf_op jit(solution)/shard_map/all_gather | solution.py:241
  784.0 120.9 %reduce-scatter.28.cloned.1.call-start = ((), (), s32[]{:S(2)}) async-start(), calls=%async_computation.30 | async-start | bytes 5242880 | tf_op jit(solution)/shard_map/reduce_scatter | solution.py:252
  860.3 78.5 %reduce-scatter.18.cloned.1.call-start = ((), (), s32[]{:S(2)}) async-start(), calls=%async_computation.20 | async-start | bytes 2621440 | tf_op jit(solution)/shard_map/reduce_scatter | solution.py:231
  870.3 102.4 %reduce-scatter.22.cloned.1.call-start = ((), (), s32[]{:S(2)}) async-start(), calls=%async_computation.24 | async-start | bytes 2621440 | tf_op jit(solution)/shard_map/reduce_scatter | solution.py:231
  880.4 92.3 %copy-start.10 = (f32[128,2048]{1,0:T(8,128)S(1)}, f32[128,2048]{1,0:T(8,128)}, u32[]{:S(2)}) copy-start(f32[128,2048]{1,0:T(8,128)} %reduce-scatter.24.cloned.1.call-done) | copy-start | bytes 3145732
  880.4 119.6 %all-gather.31.cloned.1.call-start = ((), (), s32[]{:S(2)}) async-start(), calls=%async_computation.27 | async-start | bytes 2621440 | tf_op jit(solution)/shard_map/all_gather | solution.py:260
  977.3 47.4 %all-gather.35.cloned.1.call-start = ((), (), s32[]{:S(2)}) async-start(), calls=%async_computation.31 | async-start | bytes 2621440 | tf_op jit(solution)/shard_map/all_gather | solution.py:260
  977.9 128.3 %reduce-scatter.26.cloned.1.call-start = ((), (), s32[]{:S(2)}) async-start(), calls=%async_computation.28 | async-start | bytes 5242880 | tf_op jit(solution)/shard_map/reduce_scatter | solution.py:277
  1039.6 91.7 %reduce-scatter.30.cloned.1.call-start = ((), (), s32[]{:S(2)}) async-start(), calls=%async_computation.32 | async-start | bytes 5242880 | tf_op jit(solution)/shard_map/reduce_scatter | solution.py:277
  1049.5 153.9 %reduce-scatter.34.cloned.1.call-start = ((), (), s32[]{:S(2)}) async-start(), calls=%async_computation.34 | async-start | bytes 2359296 | tf_op jit(solution)/shard_map/reduce_scatter | solution.py:164
  1055.6 299.9 %reduce-scatter.38.cloned.1.call-start = ((), (), s32[]{:S(2)}) async-start(), calls=%async_computation.36 | async-start | bytes 9437184 | tf_op jit(solution)/shard_map/reduce_scatter | solution.py:170
  1076.1 370.5 %reduce-scatter.32.cloned.1.call-start = ((), (), s32[]{:S(2)}) async-start(), calls=%async_computation.33 | async-start | bytes 4718592 | tf_op jit(solution)/shard_map/reduce_scatter | solution.py:161
  1086.3 425.8 %reduce-scatter.40.cloned.1.call-start = ((), (), s32[]{:S(2)}) async-start(), calls=%async_computation.37 | async-start | bytes 589824
  1144.7 652.6 %reduce-scatter.36.cloned.1.call-start = ((), (), s32[]{:S(2)}) async-start(), calls=%async_computation.35 | async-start | bytes 18874368 | tf_op jit(solution)/shard_map/reduce_scatter | solution.py:167
  1165.8 282.9 %copy-start.8 = (f32[128,2048]{1,0:T(8,128)S(1)}, f32[128,2048]{1,0:T(8,128)}, u32[]{:S(2)}) copy-start(f32[128,2048]{1,0:T(8,128)} %reduce-scatter.26.cloned.1.call-done) | copy-start | bytes 3145732
  1165.8 282.9 %copy-start.9 = (f32[128,2048]{1,0:T(8,128)S(1)}, f32[128,2048]{1,0:T(8,128)}, u32[]{:S(2)}) copy-start(f32[128,2048]{1,0:T(8,128)} %reduce-scatter.30.cloned.1.call-done) | copy-start | bytes 3145732
  1165.8 282.9 %copy-start.59 = (f32[128]{0:T(128)S(1)}, f32[128]{0:T(128)}, u32[]{:S(2)}) copy-start(f32[128]{0:T(128)} %get-tuple-element.218) | copy-start | bytes 1540
  1165.9 282.9 %copy-start.60 = (f32[128]{0:T(128)S(1)}, f32[128]{0:T(128)}, u32[]{:S(2)}) copy-start(f32[128]{0:T(128)} %get-tuple-element.237) | copy-start | bytes 1540
  (65 other events, 802.2 us)
Sparse Core Ops, SparseCore 0:
  35.5 19.8 all-gather.12
  57.5 73.4 all-gather.14
  133.1 20.8 all-gather.24
  155.8 51.0 all-gather.16
  212.0 42.6 reduce-scatter.15
  257.3 44.5 reduce-scatter.19
  304.8 22.5 all-gather.18
  330.2 227.6 all-gather.20
  560.0 20.7 all-gather.28
  582.6 125.4 all-gather.22
  737.5 42.6 reduce-scatter.23
  783.4 22.5 all-gather.26
  808.2 22.5 all-gather.32
  860.4 44.5 reduce-scatter.27
  907.3 31.4 reduce-scatter.17
  941.3 31.3 reduce-scatter.21
  977.4 22.5 all-gather.30
  1002.0 22.5 all-gather.34
  1039.7 44.4 reduce-scatter.25
  1086.8 44.4 reduce-scatter.29
  1135.4 68.0 reduce-scatter.33
  1207.1 148.3 reduce-scatter.37
  1359.6 86.9 reduce-scatter.31
  1450.3 61.6 reduce-scatter.39
  1516.3 280.9 reduce-scatter.35
where the time goes:
time: 1820 us; the launch traced here: 1810 us
  waiting for transfers between devices  1450 us (80%)
  matrix products  229 us (13%)
  other arithmetic  46.4 us (3%)
  blocking collectives  32.4 us (2%)
  local copies, waits for them, and re-layouts  25.3 us (1%)
    reduce_scatter x1, waiting for transfers between devices, reduce_grads(): lax.psum_scatter(pair_acc.astype(jnp.bfloat16), ('dp', 'row'), scatter_di...  284 us
    all_gather x1, waiting for transfers between devices, fetch(): lax.all_gather(jnp.stack((w1, w3)), ('dp', 'row'), axis=1, tiled=True)  230 us
    reduce_scatter x1, waiting for transfers between devices, reduce_grads(): lax.psum_scatter(down_acc.astype(jnp.bfloat16), ('dp', 'row'), scatter_di...  150 us
    all_gather x1, waiting for transfers between devices, fetch(): lax.all_gather(w2, ('dp', 'row'), axis=1, tiled=True)  127 us
    reduce_scatter x1, waiting for transfers between devices, reduce_grads(): lax.psum_scatter(qkv_acc.astype(jnp.bfloat16), ('dp', 'row'), scatter_dim...  88.3 us
    all_gather x1, waiting for transfers between devices, fetch(): lax.all_gather(wqkv, ('dp', 'row'), axis=0, tiled=True)  75.6 us
    reduce_scatter x2, waiting for transfers between devices, body(): lax.psum_scatter(jnp.dot(attended_flat, out_w, preferred_element_type=jnp...  69.3 us
    reduce_scatter x2, waiting for transfers between devices, body(): lax.psum_scatter(jnp.einsum('lgf,gdf->ld', grad_pair, pair_w, preferred_e...  67.2 us
  transfers between devices with their start and end apart: 25, of which 24 were waited for; matrix products, arithmetic and copies ran while one was open for 10% of the time, Pallas kernels for 0%

commit v1 on v0

v1 whole, which is shorter than its diff:
```python
import jax
import jax.numpy as jnp
from jax import lax
from jax.sharding import PartitionSpec as P

HEAD_SIZE = 128
QUERY_PER_GROUP = 2
EPS = 1e-05
THETA = 1000000.0
NEGATIVE = -1e30
CHUNKS = 4
BF = jnp.bfloat16
F32 = jnp.float32


def xchg(value, axis, bit):
    size = lax.axis_size(axis)
    return lax.ppermute(value, axis, [(i, i ^ bit) for i in range(size)])


def dot(left, right, left_dim, right_dim):
    return lax.dot_general(
        left, right, (((left_dim,), (right_dim,)), ((), ())), preferred_element_type=F32
    )


def gather_tokens(own):
    over_x = xchg(own, "col", 2)
    over_y = xchg(own, "dp", 1)
    first = xchg(over_y[:1], "col", 2)
    second = xchg(over_x[1:], "dp", 1)
    diagonal = jnp.concatenate((first, second), axis=0)
    blocks = []
    for block in (own, over_x, over_y, diagonal):
        blocks.extend((block, xchg(block, "col", 1)))
    return jnp.stack(blocks).reshape((2, 4) + own.shape)


def add(left, right):
    return left.astype(F32) + right.astype(F32)


def scatter_tokens(parts):
    parts = parts.reshape((2, 2, 2) + parts.shape[2:])
    quad = add(parts[:, :, 0], xchg(parts[:, :, 1], "col", 1)).astype(BF)
    first, second = quad[:, :, 0], quad[:, :, 1]
    first = add(first[:, 0], xchg(first[:, 1], "col", 2)).astype(BF)
    second = add(second[0], xchg(second[1], "dp", 1)).astype(BF)
    first = add(first[0], xchg(first[1], "dp", 1))
    second = add(second[0], xchg(second[1], "col", 2))
    return jnp.stack((first, second))


def dp_groups():
    size = lax.axis_size("dp")
    return [[i for i in range(size) if i % 2 == low] for low in (0, 1)]


def gather_weight(halves):
    low = lax.axis_index("dp") % 2
    mine = jnp.where(low == 0, halves[0], halves[1])
    sent = jnp.where(low == 0, halves[1], halves[0])
    came = xchg(sent, "dp", 1)
    pair = jnp.where(low == 0, jnp.stack((mine, came)), jnp.stack((came, mine)))
    full = lax.all_gather(pair, "row", axis=1, tiled=True)
    if lax.axis_size("dp") > 2:
        full = lax.all_gather(full, "dp", axis=0, tiled=True, axis_index_groups=dp_groups())
    return full.reshape(-1, full.shape[-1])


def scatter_weight(grad):
    low = lax.axis_index("dp") % 2
    size = lax.axis_size("dp")
    grad = grad.reshape(size, -1, grad.shape[-1])
    if size > 2:
        grad = lax.psum_scatter(
            grad, "dp", scatter_dimension=0, tiled=True, axis_index_groups=dp_groups()
        )
    pair = lax.psum_scatter(grad, "row", scatter_dimension=1, tiled=True)
    mine = jnp.where(low == 0, pair[0], pair[1])
    sent = jnp.where(low == 0, pair[1], pair[0])
    came = xchg(sent, "dp", 1)
    return jnp.where(low == 0, jnp.stack((mine, came)), jnp.stack((came, mine))).astype(F32)


def gather_gains(gains):
    blocks = gains[None]
    rows, size = lax.axis_size("row"), lax.axis_size("dp")
    bit = 1
    while bit < rows:
        blocks = jnp.concatenate((blocks, xchg(blocks, "row", bit)))
        bit *= 2
    bit = 1
    while bit < size:
        blocks = jnp.concatenate((blocks, xchg(blocks, "dp", bit)))
        bit *= 2
    me = lax.axis_index("dp") * rows + lax.axis_index("row")
    order = jnp.arange(rows * size, dtype=jnp.int32) ^ me
    return jnp.take(blocks, order, axis=0).transpose(1, 0, 2).reshape(gains.shape[0], -1)


def scatter_gain(grad):
    rows, size = lax.axis_size("row"), lax.axis_size("dp")
    bit = 1
    while bit < lax.axis_size("col"):
        grad = grad + xchg(grad, "col", bit)
        bit *= 2
    me = lax.axis_index("dp") * rows + lax.axis_index("row")
    order = jnp.arange(rows * size, dtype=jnp.int32) ^ me
    blocks = jnp.take(grad.reshape(rows * size, -1), order, axis=0)
    bit = size // 2
    while bit:
        half = blocks.shape[0] // 2
        blocks = blocks[:half] + xchg(blocks[half:], "dp", bit)
        bit //= 2
    bit = rows // 2
    while bit:
        half = blocks.shape[0] // 2
        blocks = blocks[:half] + xchg(blocks[half:], "row", bit)
        bit //= 2
    return blocks[0]


def rope_tables(positions):
    freqs = THETA ** (-jnp.arange(HEAD_SIZE // 2, dtype=F32) * 2.0 / HEAD_SIZE)
    angles = positions.astype(F32)[:, None] * freqs[None, :]
    return jnp.cos(angles)[:, None, None, :], jnp.sin(angles)[:, None, None, :]


def rotate(values, cosine, sine):
    half = HEAD_SIZE // 2
    first, second = values[..., :half], values[..., half:]
    return jnp.concatenate(
        (first * cosine - second * sine, second * cosine + first * sine), axis=-1
    )


def rms_norm(values, gain):
    inverse = lax.rsqrt(jnp.mean(values * values, axis=-1, keepdims=True) + EPS)
    return values * inverse * gain, inverse


def rms_back(values, inverse, gain, upstream):
    scaled = upstream * gain
    inner = jnp.mean(scaled * values, axis=-1, keepdims=True)
    grad_in = inverse * scaled - values * (inverse * inverse * inverse) * inner
    grad_gain = jnp.sum(upstream * values * inverse, axis=(0, 1))
    return grad_in, grad_gain


def score(query, keys, allowed):
    scores = jnp.einsum("sqgrd,skgd->sgrqk", query, keys, preferred_element_type=F32)
    return jnp.where(allowed, scores * HEAD_SIZE ** (-0.5), NEGATIVE)


def attend(query, keys, values, allowed):
    scores = score(query, keys, allowed)
    highest = jnp.max(scores, axis=-1, keepdims=True)
    expo = jnp.exp(scores - highest)
    total = jnp.sum(expo, axis=-1, keepdims=True)
    probs = (expo / total).astype(BF)
    attended = jnp.einsum("sgrqk,skgd->sqgrd", probs, values, preferred_element_type=F32)
    return attended.astype(BF), highest + jnp.log(total)


def attend_back(query, keys, values, log_totals, grad_out, allowed):
    scale = HEAD_SIZE ** (-0.5)
    probs = jnp.exp(score(query, keys, allowed) - log_totals)
    grad_probs = jnp.einsum("sqgrd,skgd->sgrqk", grad_out, values, preferred_element_type=F32)
    values_grad = jnp.einsum(
        "sgrqk,sqgrd->skgd", probs.astype(BF), grad_out, preferred_element_type=F32
    )
    inner = jnp.sum(probs * grad_probs, axis=-1, keepdims=True)
    grad_scores = (probs * (grad_probs - inner)).astype(BF)
    query_grad = jnp.einsum("sgrqk,skgd->sqgrd", grad_scores, keys, preferred_element_type=F32)
    keys_grad = jnp.einsum("sgrqk,sqgrd->skgd", grad_scores, query, preferred_element_type=F32)
    return query_grad * scale, keys_grad * scale, values_grad


def body(inputs, lengths, wqkv, wo, w1, w3, w2, attn_gain, ffn_gain, cotangent):
    micro, _, rows, width = inputs.shape
    cols = lax.axis_size("col")
    block = (2, cols, micro, rows)
    tokens = 2 * cols * micro * rows
    sequences = 2 * micro
    places = cols * rows
    me = lax.axis_index("col")
    groups = wqkv.shape[1] // ((QUERY_PER_GROUP + 2) * HEAD_SIZE) // 2
    hidden_units = w1.shape[1] // 2
    cut = hidden_units // CHUNKS

    def by_sequence(flat):
        return flat.reshape(block + (-1,)).transpose(0, 2, 1, 3, 4).reshape(sequences, places, -1)

    def by_token(per_sequence):
        return (
            per_sequence.reshape(2, micro, cols, rows, -1)
            .transpose(0, 2, 1, 3, 4)
            .reshape(tokens, -1)
        )

    gains = gather_gains(jnp.stack((attn_gain, ffn_gain))).astype(F32)
    gain_attn, gain_ffn = gains[0], gains[1]
    d = wqkv.shape[0]
    qkv_w = gather_weight(wqkv.reshape(d, 2, -1).transpose(1, 0, 2))
    out_w = gather_weight(wo.reshape(2, -1, d).transpose(0, 2, 1))
    ffn_halves = jnp.concatenate(
        (
            w1.reshape(d, 2, CHUNKS, cut).transpose(1, 2, 0, 3),
            w3.reshape(d, 2, CHUNKS, cut).transpose(1, 2, 0, 3),
            w2.reshape(2, CHUNKS, cut, d).transpose(0, 1, 3, 2),
        ),
        axis=-1,
    )

    source = inputs[:, 0].astype(F32)
    normed1, inverse1 = rms_norm(source, gain_attn)
    attn_rows = gather_tokens(normed1.astype(BF)).reshape(tokens, width)
    all_lengths = jnp.stack((lengths, xchg(lengths, "dp", 1))).reshape(sequences)
    positions = (
        (jnp.arange(cols, dtype=jnp.int32) ^ me)[:, None] * rows
        + jnp.arange(rows, dtype=jnp.int32)[None, :]
    ).reshape(places)
    cosine, sine = rope_tables(positions)
    allowed = (positions[None, None, :] <= positions[None, :, None]) & (
        positions[None, None, :] < all_lengths[:, None, None]
    )
    allowed = allowed[:, None, None]
    projected = by_sequence(dot(attn_rows, qkv_w, 1, 0)).reshape(
        sequences, places, groups, QUERY_PER_GROUP + 2, HEAD_SIZE
    )
    query = rotate(projected[:, :, :, :QUERY_PER_GROUP], cosine, sine).astype(BF)
    keys = rotate(
        projected[:, :, :, QUERY_PER_GROUP : QUERY_PER_GROUP + 1], cosine, sine
    )[:, :, :, 0].astype(BF)
    values = projected[:, :, :, QUERY_PER_GROUP + 1].astype(BF)
    attended, log_totals = attend(query, keys, values, allowed)
    attended = by_token(attended)
    residual = source + scatter_tokens(
        dot(attended, out_w, 1, 1).astype(BF).reshape(block + (width,))
    )

    normed2, inverse2 = rms_norm(residual, gain_ffn)
    ffn_rows = gather_tokens(normed2.astype(BF)).reshape(tokens, width)
    own_places = me * rows + jnp.arange(rows, dtype=jnp.int32)
    valid = (own_places[None, :] < lengths).astype(F32)[:, :, None]
    upstream = cotangent[:, 0].astype(F32) * valid
    piece = gather_tokens(upstream.astype(BF)).reshape(tokens, width)
    hiddens, grad_pairs, pair_ws, down_ws, ffn_grads = [], [], [], [], []
    for chunk in range(CHUNKS):
        weights = gather_weight(ffn_halves[:, chunk])
        pair_w, down_w = weights[:, : 2 * cut], weights[:, 2 * cut :]
        gate_up = dot(ffn_rows, pair_w, 1, 0)
        gate_val, up_val = gate_up[:, :cut], gate_up[:, cut:]
        sigma = jax.nn.sigmoid(gate_val)
        swish = gate_val * sigma
        hidden = (swish * up_val).astype(BF)
        hidden_grad = dot(piece, down_w, 1, 0)
        grad_gate = hidden_grad * up_val * sigma * (1.0 + gate_val * (1.0 - sigma))
        grad_up = hidden_grad * swish
        grad_pair = jnp.concatenate((grad_gate, grad_up), axis=1).astype(BF)
        grads = jnp.concatenate(
            (dot(ffn_rows, grad_pair, 0, 0).astype(BF), dot(piece, hidden, 0, 0).astype(BF)),
            axis=1,
        )
        ffn_grads.append(scatter_weight(grads))
        hiddens.append(hidden)
        grad_pairs.append(grad_pair)
        pair_ws.append(pair_w)
        down_ws.append(down_w)
    normed2_grad = dot(
        jnp.concatenate(grad_pairs, axis=1), jnp.concatenate(pair_ws, axis=1), 1, 1
    )
    normed2_grad = scatter_tokens(normed2_grad.astype(BF).reshape(block + (width,)))
    ffn_out = dot(jnp.concatenate(hiddens, axis=1), jnp.concatenate(down_ws, axis=1), 1, 1)
    result = residual + scatter_tokens(ffn_out.astype(BF).reshape(block + (width,)))

    residual_in, gain2_grad = rms_back(residual, inverse2, gain_ffn, normed2_grad)
    residual_grad = upstream + residual_in
    attn_piece = gather_tokens(residual_grad.astype(BF)).reshape(tokens, width)
    out_grad = dot(attn_piece, attended, 0, 0).astype(BF)
    grad_out = by_sequence(dot(attn_piece, out_w, 1, 0).astype(BF)).reshape(query.shape)
    query_grad, keys_grad, values_grad = attend_back(
        query, keys, values, log_totals, grad_out, allowed
    )
    query_grad = rotate(query_grad, cosine, -sine)
    keys_grad = rotate(keys_grad[:, :, :, None], cosine, -sine)
    grad_proj = by_token(
        jnp.concatenate((query_grad, keys_grad, values_grad[:, :, :, None]), axis=3).astype(BF)
    )
    qkv_grad = dot(attn_rows, grad_proj, 0, 0).astype(BF)
    normed1_grad = scatter_tokens(dot(grad_proj, qkv_w, 1, 1).astype(BF).reshape(block + (width,)))
    source_in, gain1_grad = rms_back(source, inverse1, gain_attn, normed1_grad)
    source_grad = (residual_grad + source_in).astype(BF)

    qkv_shard = scatter_weight(qkv_grad).transpose(1, 0, 2).reshape(wqkv.shape)
    out_shard = scatter_weight(out_grad).transpose(0, 2, 1).reshape(wo.shape)
    ffn = jnp.stack(ffn_grads, axis=1)
    gate_shard = ffn[..., :cut].transpose(2, 0, 1, 3).reshape(w1.shape)
    up_shard = ffn[..., cut : 2 * cut].transpose(2, 0, 1, 3).reshape(w3.shape)
    down_shard = ffn[..., 2 * cut :].transpose(0, 1, 3, 2).reshape(w2.shape)
    return (
        result.astype(BF)[:, None],
        source_grad[:, None],
        scatter_gain(gain1_grad),
        scatter_gain(gain2_grad),
        qkv_shard,
        out_shard,
        gate_shard,
        up_shard,
        down_shard,
    )


def solution(mesh):
    tokens = P(None, ("dp", "row"), "col", None)
    in_specs = (
        tokens,
        P(None, ("dp", "row")),
        P(("dp", "row"), "col"),
        P("col", ("dp", "row")),
        P(("dp", "row"), "col"),
        P(("dp", "row"), "col"),
        P("col", ("dp", "row")),
        P(("dp", "row")),
        P(("dp", "row")),
        tokens,
    )
    out_specs = (
        tokens,
        tokens,
        P(("dp", "row")),
        P(("dp", "row")),
        P(("dp", "row"), "col"),
        P("col", ("dp", "row")),
        P(("dp", "row"), "col"),
        P(("dp", "row"), "col"),
        P("col", ("dp", "row")),
    )
    return jax.shard_map(body, mesh=mesh, in_specs=in_specs, out_specs=out_specs, check_vma=False)
```

time: 1820 us -> 868 us (0.48)
  waiting for transfers between devices: 1450 us -> 253 us
  local copies, waits for them, and re-layouts: 25.3 us -> 201 us
  other arithmetic: 46.4 us -> 117 us
  starting transfers between devices: 14.7 us -> 76.4 us
  matrix products: 229 us -> 196 us
  blocking collectives: 32.4 us -> 0 us
    reduce_scatter x12 -> x6, waiting for transfers between devices: 785 us -> 0.01 us  [scatter_weight(): pair = lax.psum_scatter(grad, 'row', scatter_dimension=1, tiled=True)]
    all_gather x12 -> x6, waiting for transfers between devices: 599 us -> 0.03 us  [gather_weight(): full = lax.all_gather(pair, 'row', axis=1, tiled=True)]
    ppermute x0 -> x78, waiting for transfers between devices: none -> 253 us  [xchg(): return lax.ppermute(value, axis, [(i, i ^ bit) for i in range(size)])]
    ppermute x0 -> x78, starting transfers between devices: none -> 75.7 us  [xchg(): return lax.ppermute(value, axis, [(i, i ^ bit) for i in range(size)])]
    unnamed x26 -> x12, waiting for transfers between devices: 64 us -> 0.2 us
    slice x2 -> x30, local copies, waits for them, and re-layouts: 1.18 us -> 48.3 us  [the longest x8 18.8 us: body(): pair_w, down_w = (weights[:, :2 * cut], weights[:, 2 * cut:])]
    unnamed x148 -> x257, local copies, waits for them, and re-layouts: 21.3 us -> 64.7 us
    dot_general x36 -> x30, matrix products: 229 us -> 196 us  [the longest x24 181 us: dot(): lax.dot_general(left, right, (((left_dim,), (right_dim,)), ((), ())), pre...]
  transfers between devices with their start and end apart: 25 -> 90, of which waited for: 24 -> 38; matrix products, arithmetic and copies ran while one was open for 10% -> 58% of each run, Pallas kernels for 0% -> 0%
where the time goes in v1:
time: 868 us; the launch traced here: 860 us
  waiting for transfers between devices  253 us (29%)
  local copies, waits for them, and re-layouts  201 us (23%)
  matrix products  196 us (23%)
  other arithmetic  117 us (13%)
  starting transfers between devices  76.4 us (9%)
  between operations  16.4 us (2%)
    ppermute x78, waiting for transfers between devices, xchg(): return lax.ppermute(value, axis, [(i, i ^ bit) for i in range(size)])  253 us
    dot_general x24, matrix products, dot(): lax.dot_general(left, right, (((left_dim,), (right_dim,)), ((), ())), pre...  181 us
    ppermute x78, starting transfers between devices, xchg(): return lax.ppermute(value, axis, [(i, i ^ bit) for i in range(size)])  75.7 us
    unnamed x257, local copies, waits for them, and re-layouts  64.7 us
    convert_element_type x4, other arithmetic, scatter_tokens(): quad = add(parts[:, :, 0], xchg(parts[:, :, 1], 'col', 1)).astype(BF)  19.3 us
    all_gather x4, local copies, waits for them, and re-layouts, gather_weight(): full = lax.all_gather(pair, 'row', axis=1, tiled=True)  19.2 us
    slice x8, local copies, waits for them, and re-layouts, body(): pair_w, down_w = (weights[:, :2 * cut], weights[:, 2 * cut:])  18.8 us
  transfers between devices with their start and end apart: 90, of which 38 were waited for; matrix products, arithmetic and copies ran while one was open for 58% of the time, Pallas kernels for 0%

profile of v1, /device:TPU:0, one launch (start us, length us, event | category | flops | bytes accessed | tf_op | source)
XLA Modules:
  0.0 860.2 jit_solution(9855906772768413814)
XLA Ops:
  11.5 6.3 collective-permute-done.11
  30.3 7.4 collective-permute-done.27
  40.2 6.9 collective-permute-done.28
  74.8 17.8 %collective-permute-done.6 = bf16[2,128,2048]{2,1,0:T(8,128)(2,1)S(1)} collective-permute-done((bf16[2,128,2048]{2,1,0:T(8,128)(2,1)}, bf16[2,128,2048]{2,1,0:T(8,128)(2,1)S(1)}, u32[]{:S(2)}, u32[]{:S(2)}) %collective-permute-start.6) | collective-permute-done | bytes 1048608 | tf_op jit(solution)/shard_map/ppermute | solution.py:18
  98.7 7.3 collective-permute-done.8
  111.9 7.7 convolution_bitcast_fusion
  127.6 8.2 fusion.173
  174.2 29.0 %collective-permute-done.30 = bf16[256,768]{0,1:T(8,128)(2,1)S(1)} collective-permute-done((bf16[256,768]{0,1:T(8,128)(2,1)}, bf16[256,768]{0,1:T(8,128)(2,1)S(1)}, u32[]{:S(2)}, u32[]{:S(2)}) %collective-permute-start.30) | collective-permute-done | bytes 393248 | tf_op jit(solution)/shard_map/ppermute | solution.py:18
  229.0 21.1 %collective-permute-done.15 = bf16[2,128,2048]{2,1,0:T(8,128)(2,1)S(1)} collective-permute-done((bf16[2,128,2048]{2,1,0:T(8,128)(2,1)S(1)}, bf16[2,128,2048]{2,1,0:T(8,128)(2,1)S(1)}, u32[]{:S(2)}, u32[]{:S(2)}) %collective-permute-start.15) | collective-permute-done | bytes 1048608 | tf_op jit(solution)/shard_map/ppermute | solution.py:18
  254.6 9.6 %collective-permute-done.16 = bf16[128,2048]{1,0:T(8,128)(2,1)S(1)} collective-permute-done((bf16[128,2048]{1,0:T(8,128)(2,1)S(1)}, bf16[128,2048]{1,0:T(8,128)(2,1)S(1)}, u32[]{:S(2)}, u32[]{:S(2)}) %collective-permute-start.16) | collective-permute-done | bytes 524320 | tf_op jit(solution)/shard_map/ppermute | solution.py:18
  283.1 9.7 %collective-permute-done.22 = bf16[2,128,2048]{2,1,0:T(8,128)(2,1)} collective-permute-done((bf16[2,128,2048]{2,1,0:T(8,128)(2,1)}, bf16[2,128,2048]{2,1,0:T(8,128)(2,1)}, u32[]{:S(2)}, u32[]{:S(2)}) %collective-permute-start.22) | collective-permute-done | bytes 1048608 | tf_op jit(solution)/shard_map/ppermute | solution.py:18
  315.6 7.4 constant_dynamic-update-slice_fusion.13
  325.3 7.2 fusion.165
  335.1 6.7 convolution_convert_fusion.11
  383.0 7.4 constant_dynamic-update-slice_fusion.11
  392.0 6.1 convolution_convert_fusion.10
  409.6 9.5 %fusion.163 = f32[2048,512]{0,1:T(8,128)} fusion(bf16[2048,2048]{1,0:T(8,128)(2,1)} %bitcast.694, bf16[2048,768]{1,0:T(8,128)(2,1)S(1)} %bitcast.645), kind=kOutput, calls=%fused_computation.414 | convolution fusion | flops 4294967296 | bytes 14680064 | tf_op jit(solution)/shard_map/dot_general | solution.py:22
  419.1 8.7 %constant_dynamic-update-slice_fusion.9 = (bf16[2048,2048]{0,1:T(8,128)(2,1)}, bf16[2048,256]{0,1:T(8,128)(2,1)S(1)}, f32[2048,256]{0,1:T(8,128)S(1)}) fusion(bf16[2048,2048]{0,1:T(8,128)(2,1)} %get-tuple-element.31, f32[2048,512]{0,1:T(8,128)} %fusion.163, bf16[2048,2048]{1,0:T(8,128)(2,1)} %bitcast.115, bf16[2048,768]{1,0:T(8,128)(2,1)S(1)} %bitcast.646), kind=kOutput, calls=%fused_computation.352 | convolution fusion | flops 2152726528 | bytes 17825792 | tf_op jit(solution)/shard_map/dot_general | solution.py:22
  430.2 7.1 fusion.161
  439.9 6.7 convolution_convert_fusion.9
  457.9 9.6 %constant_dynamic-update-slice_fusion.7 = (bf16[2048,2048]{0,1:T(8,128)(2,1)}, bf16[2048,256]{0,1:T(8,128)(2,1)}, f32[2048,256]{0,1:T(8,128)}) fusion(bf16[2048,2048]{0,1:T(8,128)(2,1)} %get-tuple-element.27, f32[2048,512]{0,1:T(8,128)} %copy-done.24, bf16[2048,2048]{1,0:T(8,128)(2,1)} %bitcast.115, bf16[2048,768]{1,0:T(8,128)(2,1)S(1)} %bitcast.642), kind=kOutput, calls=%fused_computation.350 | convolution fusion | flops 2152726528 | bytes 17825792 | tf_op jit(solution)/shard_map/dot_general | solution.py:22
  472.8 22.6 %fusion.15 = bf16[2048,2048]{1,0:T(8,128)(2,1)S(1)} fusion(bf16[2048,2048]{0,1:T(8,128)(2,1)} %get-tuple-element.23, bf16[2048,512]{1,0:T(8,128)(2,1)} %slice.594, bf16[2048,512]{1,0:T(8,128)(2,1)S(1)} %copy-done.55, bf16[2048,512]{1,0:T(8,128)(2,1)S(1)} %copy-done.54, bf16[2048,512]{1,0:T(8,128)(2,1)S(1)} %copy-done.53), kind=kOutput, calls=%fused_computation.28 | convolution fusion | flops 17217617920 | bytes 25165824 | tf_op jit(solution)/shard_map/dot_general | solution.py:22
  500.5 11.8 %convolution_convert_fusion.1 = bf16[2048,2048]{1,0:T(8,128)(2,1)S(1)} fusion(bf16[2048,256]{0,1:T(8,128)(2,1)} %get-tuple-element.119, bf16[2048,256]{0,1:T(8,128)(2,1)} %copy-done.62, bf16[2048,256]{0,1:T(8,128)(2,1)S(1)} %copy-done.59, bf16[2048,256]{0,1:T(8,128)(2,1)} %copy-done.60, bf16[2048,256]{1,0:T(8,128)(2,1)} %slice.600, ...), kind=kOutput, calls=%fused_computation.30 | convolution fusion | flops 8627683328 | bytes 16777216 | tf_op jit(solution)/shard_map/dot_general | solution.py:22
  546.4 17.1 %collective-permute-done.45 = bf16[2,128,2048]{2,1,0:T(8,128)(2,1)S(1)} collective-permute-done((bf16[2,128,2048]{2,1,0:T(8,128)(2,1)S(1)}, bf16[2,128,2048]{2,1,0:T(8,128)(2,1)S(1)}, u32[]{:S(2)}, u32[]{:S(2)}) %collective-permute-start.45) | collective-permute-done | bytes 1048608 | tf_op jit(solution)/shard_map/ppermute | solution.py:18
  566.8 19.2 %collective-permute-done.32 = bf16[2,128,2048]{2,1,0:T(8,128)(2,1)S(1)} collective-permute-done((bf16[2,128,2048]{2,1,0:T(8,128)(2,1)S(1)}, bf16[2,128,2048]{2,1,0:T(8,128)(2,1)S(1)}, u32[]{:S(2)}, u32[]{:S(2)}) %collective-permute-start.32) | collective-permute-done | bytes 1048608 | tf_op jit(solution)/shard_map/ppermute | solution.py:18
  589.2 9.4 %collective-permute-done.46 = bf16[128,2048]{1,0:T(8,128)(2,1)S(1)} collective-permute-done((bf16[128,2048]{1,0:T(8,128)(2,1)S(1)}, bf16[128,2048]{1,0:T(8,128)(2,1)S(1)}, u32[]{:S(2)}, u32[]{:S(2)}) %collective-permute-start.46) | collective-permute-done | bytes 524320 | tf_op jit(solution)/shard_map/ppermute | solution.py:18
  613.4 17.0 %collective-permute-done.68 = f32[2048]{0:T(1024)S(1)} collective-permute-done((f32[2048]{0:T(1024)S(1)}, f32[2048]{0:T(1024)S(1)}, u32[]{:S(2)}, u32[]{:S(2)}) %collective-permute-start.68) | collective-permute-done | bytes 8224 | tf_op jit(solution)/shard_map/ppermute | solution.py:18
  655.0 6.9 convolution_convert_fusion.13
  719.4 6.0 collective-permute-done.75
  727.6 6.9 convolution_convert_fusion.12
  746.0 9.5 %convolution_convert_fusion.7 = bf16[2048,512]{1,0:T(8,128)(2,1)} fusion(bf16[2048,2048]{1,0:T(8,128)(2,1)} %bitcast.710, bf16[2048,512]{1,0:T(8,128)(2,1)S(1)} %bitcast.661), kind=kOutput, calls=%fused_computation.84 | convolution fusion | flops 4296015872 | bytes 12582912 | tf_op jit(solution)/shard_map/dot_general | solution.py:22
  796.5 16.4 %collective-permute-done.60 = bf16[2,128,2048]{2,1,0:T(8,128)(2,1)} collective-permute-done((bf16[2,128,2048]{2,1,0:T(8,128)(2,1)}, bf16[2,128,2048]{2,1,0:T(8,128)(2,1)}, u32[]{:S(2)}, u32[]{:S(2)}) %collective-permute-start.60) | collective-permute-done | bytes 1048608 | tf_op jit(solution)/shard_map/ppermute | solution.py:18
  (654 shorter events, 493.6 us)
Async XLA Ops:
  7.2 104.7 %all-gather.7.cloned.1.call-start = ((), (), s32[]{:S(2)}) async-start(), calls=%async_computation.6 | async-start | bytes 2621440 | tf_op jit(solution)/shard_map/all_gather | solution.py:65
  18.7 140.3 %all-gather.9.cloned.1.call-start = ((), (), s32[]{:S(2)}) async-start(), calls=%async_computation.7 | async-start | bytes 1310720 | tf_op jit(solution)/shard_map/all_gather | solution.py:65
  24.7 248.5 %all-gather.11.cloned.1.call-start = ((), (), s32[]{:S(2)}) async-start(), calls=%async_computation.8 | async-start | bytes 3932160 | tf_op jit(solution)/shard_map/all_gather | solution.py:65
  38.7 239.4 %all-gather.13.cloned.1.call-start = ((), (), s32[]{:S(2)}) async-start(), calls=%async_computation.9 | async-start | bytes 3932160 | tf_op jit(solution)/shard_map/all_gather | solution.py:65
  48.1 314.3 %all-gather.15.cloned.1.call-start = ((), (), s32[]{:S(2)}) async-start(), calls=%async_computation.10 | async-start | bytes 3932160 | tf_op jit(solution)/shard_map/all_gather | solution.py:65
  65.6 29.8 %collective-permute-start.3 = (bf16[2,128,2048]{2,1,0:T(8,128)(2,1)}, bf16[2,128,2048]{2,1,0:T(8,128)(2,1)}, u32[]{:S(2)}, u32[]{:S(2)}) collective-permute-start(bf16[2,128,2048]{2,1,0:T(8,128)(2,1)} %fusion.63), channel_id=1, source_target_pairs={{0,1},{1,0},{2,3},{3,2},{4,5},{5,4},{6,7},{7,6},{8,9},{9,8},{10,11... | collective-permute-start | bytes 3145736 | tf_op jit(solution)/shard_map/ppermute | solution.py:18
  65.6 27.6 %collective-permute-start.4 = (bf16[2,128,2048]{2,1,0:T(8,128)(2,1)}, bf16[2,128,2048]{2,1,0:T(8,128)(2,1)S(1)}, u32[]{:S(2)}, u32[]{:S(2)}) collective-permute-start(bf16[2,128,2048]{2,1,0:T(8,128)(2,1)} %fusion.63), channel_id=1, source_target_pairs={{0,2},{1,3},{2,0},{3,1},{4,6},{5,7},{6,4},{7,5},{8,10},{9,11},{10,... | collective-permute-start | bytes 3145736 | tf_op jit(solution)/shard_map/ppermute | solution.py:18
  74.8 298.0 %all-gather.17.cloned.1.call-start = ((), (), s32[]{:S(2)}) async-start(), calls=%async_computation.11 | async-start | bytes 3932160 | tf_op jit(solution)/shard_map/all_gather | solution.py:65
  167.7 52.3 %collective-permute-start.14 = (bf16[2,2,2,128,2048]{4,3,1,2,0:T(8,128)(2,1)}, bf16[2,2,2,128,2048]{4,3,1,2,0:T(8,128)(2,1)}, u32[]{:S(2)}, u32[]{:S(2)}) collective-permute-start(bf16[2,2,2,128,2048]{4,3,1,2,0:T(8,128)(2,1)} %bitcast.616), channel_id=1, source_target_pairs={{0,1},{1,0},{2,3},{3,2},{4,5},{5,4},{6,7},{7,6},{8,9},{9,8},{10,11... | collective-permute-start | bytes 12582920 | tf_op jit(solution)/shard_map/ppermute | solution.py:18
  169.5 34.8 %collective-permute-start.39 = (bf16[2,128,2048]{2,1,0:T(8,128)(2,1)}, bf16[2,128,2048]{2,1,0:T(8,128)(2,1)S(1)}, u32[]{:S(2)}, u32[]{:S(2)}) collective-permute-start(bf16[2,128,2048]{2,1,0:T(8,128)(2,1)} %fusion.59), channel_id=1, source_target_pairs={{0,16},{16,0},{1,17},{17,1},{2,18},{18,2},{3,19},{19,3},{4,20},{20... | collective-permute-start | bytes 3145736 | tf_op jit(solution)/shard_map/ppermute | solution.py:18
  170.9 34.9 %collective-permute-start.37 = (bf16[2,128,2048]{2,1,0:T(8,128)(2,1)}, bf16[2,128,2048]{2,1,0:T(8,128)(2,1)}, u32[]{:S(2)}, u32[]{:S(2)}) collective-permute-start(bf16[2,128,2048]{2,1,0:T(8,128)(2,1)} %fusion.59), channel_id=1, source_target_pairs={{0,2},{1,3},{2,0},{3,1},{4,6},{5,7},{6,4},{7,5},{8,10},{9,11},{10,... | collective-permute-start | bytes 3145736 | tf_op jit(solution)/shard_map/ppermute | solution.py:18
  172.4 36.1 %collective-permute-start.36 = (bf16[2,128,2048]{2,1,0:T(8,128)(2,1)}, bf16[2,128,2048]{2,1,0:T(8,128)(2,1)}, u32[]{:S(2)}, u32[]{:S(2)}) collective-permute-start(bf16[2,128,2048]{2,1,0:T(8,128)(2,1)} %fusion.59), channel_id=1, source_target_pairs={{0,1},{1,0},{2,3},{3,2},{4,5},{5,4},{6,7},{7,6},{8,9},{9,8},{10,11... | collective-permute-start | bytes 3145736 | tf_op jit(solution)/shard_map/ppermute | solution.py:18
  172.4 30.8 %collective-permute-start.30 = (bf16[256,768]{0,1:T(8,128)(2,1)}, bf16[256,768]{0,1:T(8,128)(2,1)S(1)}, u32[]{:S(2)}, u32[]{:S(2)}) collective-permute-start(bf16[256,768]{0,1:T(8,128)(2,1)} %get-tuple-element.63), channel_id=1, source_target_pairs={{0,16},{16,0},{1,17},{17,1},{2,18},{18,2},{3,19},{19,3},{4,20},{20... | collective-permute-start | bytes 1179656 | tf_op jit(solution)/shard_map/ppermute | solution.py:18
  204.2 498.5 %reduce-scatter.11.cloned.1.call-start = ((), (), s32[]{:S(2)}) async-start(), calls=%async_computation.14 | async-start | bytes 3932160 | tf_op jit(solution)/shard_map/reduce_scatter | solution.py:79
  208.5 45.0 %collective-permute-start.40 = (bf16[2,128,2048]{2,1,0:T(8,128)(2,1)S(1)}, bf16[2,128,2048]{2,1,0:T(8,128)(2,1)S(1)}, u32[]{:S(2)}, u32[]{:S(2)}) collective-permute-start(bf16[2,128,2048]{2,1,0:T(8,128)(2,1)S(1)} %collective-permute-done.39), channel_id=1, source_target_pairs={{0,1},{1,0},{2,3},{3,2},{4,5},{5,4},{6,7},{7,6},{8,9},{9,8},{10,11... | collective-permute-start | bytes 3145736 | tf_op jit(solution)/shard_map/ppermute | solution.py:18
  219.9 52.3 %collective-permute-start.43 = (bf16[2,128,2048]{2,1,0:T(8,128)(2,1)S(1)}, bf16[2,128,2048]{2,1,0:T(8,128)(2,1)S(1)}, u32[]{:S(2)}, u32[]{:S(2)}) collective-permute-start(bf16[2,128,2048]{2,1,0:T(8,128)(2,1)S(1)} %constant_dynamic-update-slice_fusion.4), channel_id=1, source_target_pairs={{0,1},{1,0},{2,3},{3,2},{4,5},{5,4},{6,7},{7,6},{8,9},{9,8},{10,11... | collective-permute-start | bytes 3145736 | tf_op jit(solution)/shard_map/ppermute | solution.py:18
  353.1 352.6 %reduce-scatter.13.cloned.1.call-start = ((), (), s32[]{:S(2)}) async-start(), calls=%async_computation.15 | async-start | bytes 3932160 | tf_op jit(solution)/shard_map/reduce_scatter | solution.py:79
  419.1 289.7 %reduce-scatter.15.cloned.1.call-start = ((), (), s32[]{:S(2)}) async-start(), calls=%async_computation.16 | async-start | bytes 3932160 | tf_op jit(solution)/shard_map/reduce_scatter | solution.py:79
  467.5 244.3 %reduce-scatter.17.cloned.1.call-start = ((), (), s32[]{:S(2)}) async-start(), calls=%async_computation.17 | async-start | bytes 3932160 | tf_op jit(solution)/shard_map/reduce_scatter | solution.py:79
  499.9 31.7 %collective-permute-start.44 = (bf16[2,2,2,128,2048]{4,3,1,2,0:T(8,128)(2,1)}, bf16[2,2,2,128,2048]{4,3,1,2,0:T(8,128)(2,1)}, u32[]{:S(2)}, u32[]{:S(2)}) collective-permute-start(bf16[2,2,2,128,2048]{4,3,1,2,0:T(8,128)(2,1)} %bitcast.614), channel_id=1, source_target_pairs={{0,1},{1,0},{2,3},{3,2},{4,5},{5,4},{6,7},{7,6},{8,9},{9,8},{10,11... | collective-permute-start | bytes 12582920 | tf_op jit(solution)/shard_map/ppermute | solution.py:18
  531.4 250.5 %reduce-scatter.9.cloned.1.call-start = ((), (), s32[]{:S(2)}) async-start(), calls=%async_computation.13 | async-start | bytes 1310720 | tf_op jit(solution)/shard_map/reduce_scatter | solution.py:79
  544.5 41.5 %collective-permute-start.32 = (bf16[2,128,2048]{2,1,0:T(8,128)(2,1)S(1)}, bf16[2,128,2048]{2,1,0:T(8,128)(2,1)S(1)}, u32[]{:S(2)}, u32[]{:S(2)}) collective-permute-start(bf16[2,128,2048]{2,1,0:T(8,128)(2,1)S(1)} %slice_bitcast_fusion.17), channel_id=1, source_target_pairs={{0,2},{1,3},{2,0},{3,1},{4,6},{5,7},{6,4},{7,5},{8,10},{9,11},{10,... | collective-permute-start | bytes 3145736 | tf_op jit(solution)/shard_map/ppermute | solution.py:18
  545.9 42.1 %collective-permute-start.34 = (bf16[2,128,2048]{2,1,0:T(8,128)(2,1)S(1)}, bf16[2,128,2048]{2,1,0:T(8,128)(2,1)S(1)}, u32[]{:S(2)}, u32[]{:S(2)}) collective-permute-start(bf16[2,128,2048]{2,1,0:T(8,128)(2,1)S(1)} %slice_bitcast_fusion.15), channel_id=1, source_target_pairs={{0,16},{16,0},{1,17},{17,1},{2,18},{18,2},{3,19},{19,3},{4,20},{20... | collective-permute-start | bytes 3145736 | tf_op jit(solution)/shard_map/ppermute | solution.py:18
  564.0 34.6 %collective-permute-start.46 = (bf16[128,2048]{1,0:T(8,128)(2,1)S(1)}, bf16[128,2048]{1,0:T(8,128)(2,1)S(1)}, u32[]{:S(2)}, u32[]{:S(2)}) collective-permute-start(bf16[128,2048]{1,0:T(8,128)(2,1)S(1)} %slice_bitcast_fusion.29), channel_id=1, source_target_pairs={{0,16},{16,0},{1,17},{17,1},{2,18},{18,2},{3,19},{19,3},{4,20},{20... | collective-permute-start | bytes 1572872 | tf_op jit(solution)/shard_map/ppermute | solution.py:18
  566.0 32.9 %collective-permute-start.48 = (bf16[128,2048]{1,0:T(8,128)(2,1)S(1)}, bf16[128,2048]{1,0:T(8,128)(2,1)S(1)}, u32[]{:S(2)}, u32[]{:S(2)}) collective-permute-start(bf16[128,2048]{1,0:T(8,128)(2,1)S(1)} %slice_bitcast_fusion.27), channel_id=1, source_target_pairs={{0,2},{1,3},{2,0},{3,1},{4,6},{5,7},{6,4},{7,5},{8,10},{9,11},{10,... | collective-permute-start | bytes 1572872 | tf_op jit(solution)/shard_map/ppermute | solution.py:18
  602.7 28.9 %collective-permute-start.52 = (bf16[2,128,2048]{2,1,0:T(8,128)(2,1)}, bf16[2,128,2048]{2,1,0:T(8,128)(2,1)}, u32[]{:S(2)}, u32[]{:S(2)}) collective-permute-start(bf16[2,128,2048]{2,1,0:T(8,128)(2,1)} %fusion.60), channel_id=1, source_target_pairs={{0,16},{16,0},{1,17},{17,1},{2,18},{18,2},{3,19},{19,3},{4,20},{20... | collective-permute-start | bytes 3145736 | tf_op jit(solution)/shard_map/ppermute | solution.py:18
  603.7 30.4 %collective-permute-start.50 = (bf16[2,128,2048]{2,1,0:T(8,128)(2,1)}, bf16[2,128,2048]{2,1,0:T(8,128)(2,1)}, u32[]{:S(2)}, u32[]{:S(2)}) collective-permute-start(bf16[2,128,2048]{2,1,0:T(8,128)(2,1)} %fusion.60), channel_id=1, source_target_pairs={{0,2},{1,3},{2,0},{3,1},{4,6},{5,7},{6,4},{7,5},{8,10},{9,11},{10,... | collective-permute-start | bytes 3145736 | tf_op jit(solution)/shard_map/ppermute | solution.py:18
  605.0 31.7 %collective-permute-start.49 = (bf16[2,128,2048]{2,1,0:T(8,128)(2,1)}, bf16[2,128,2048]{2,1,0:T(8,128)(2,1)}, u32[]{:S(2)}, u32[]{:S(2)}) collective-permute-start(bf16[2,128,2048]{2,1,0:T(8,128)(2,1)} %fusion.60), channel_id=1, source_target_pairs={{0,1},{1,0},{2,3},{3,2},{4,5},{5,4},{6,7},{7,6},{8,9},{9,8},{10,11... | collective-permute-start | bytes 3145736 | tf_op jit(solution)/shard_map/ppermute | solution.py:18
  702.2 53.4 %collective-permute-start.57 = (bf16[2,2,2,128,2048]{4,3,0,1,2:T(8,128)(2,1)}, bf16[2,2,2,128,2048]{4,3,0,1,2:T(8,128)(2,1)}, u32[]{:S(2)}, u32[]{:S(2)}) collective-permute-start(bf16[2,2,2,128,2048]{4,3,0,1,2:T(8,128)(2,1)} %bitcast.613), channel_id=1, source_target_pairs={{0,1},{1,0},{2,3},{3,2},{4,5},{5,4},{6,7},{7,6},{8,9},{9,8},{10,11... | collective-permute-start | bytes 12582920 | tf_op jit(solution)/shard_map/ppermute | solution.py:18
  713.9 27.4 %collective-permute-start.77 = (bf16[256,768]{1,0:T(8,128)(2,1)}, bf16[256,768]{1,0:T(8,128)(2,1)}, u32[]{:S(2)}, u32[]{:S(2)}) collective-permute-start(bf16[256,768]{1,0:T(8,128)(2,1)} %get-tuple-element.89), channel_id=1, source_target_pairs={{0,16},{16,0},{1,17},{17,1},{2,18},{18,2},{3,19},{19,3},{4,20},{20... | collective-permute-start | bytes 1179656 | tf_op jit(solution)/shard_map/ppermute | solution.py:18
  734.5 82.9 %reduce-scatter.7.cloned.1.call-start = ((), (), s32[]{:S(2)}) async-start(), calls=%async_computation.12 | async-start | bytes 2621440 | tf_op jit(solution)/shard_map/reduce_scatter | solution.py:79
  794.6 29.6 %collective-permute-start.59 = (bf16[128,2048]{1,0:T(8,128)(2,1)}, bf16[128,2048]{1,0:T(8,128)(2,1)}, u32[]{:S(2)}, u32[]{:S(2)}) collective-permute-start(bf16[128,2048]{1,0:T(8,128)(2,1)} %slice_bitcast_fusion.25), channel_id=1, source_target_pairs={{0,16},{16,0},{1,17},{17,1},{2,18},{18,2},{3,19},{19,3},{4,20},{20... | collective-permute-start | bytes 1572872 | tf_op jit(solution)/shard_map/ppermute | solution.py:18
  (168 other events, 1838.9 us)
Sparse Core Ops, SparseCore 0:
  18.8 47.4 all-gather.6
  67.9 26.6 all-gather.8
  96.2 62.9 all-gather.10
  160.5 61.5 all-gather.12
  224.2 61.5 all-gather.14
  287.8 61.5 all-gather.16
  353.3 59.4 reduce-scatter.10
  419.2 59.7 reduce-scatter.12
  481.4 60.2 reduce-scatter.14
  543.8 60.2 reduce-scatter.16
  734.6 26.6 reduce-scatter.8
  763.6 42.5 reduce-scatter.6

commit v2 on v1

v2 whole, which is shorter than its diff:
```python
import jax
import jax.numpy as jnp
from jax import lax
from jax.experimental import pallas as pl
from jax.experimental.pallas import tpu as pltpu
from jax.sharding import PartitionSpec as P

HEAD_SIZE = 128
QUERY_PER_GROUP = 2
EPS = 1e-05
THETA = 1000000.0
NEGATIVE = -1e30
CHUNKS = 2
BF = jnp.bfloat16
F32 = jnp.float32


def xchg(value, axis, bit):
    size = lax.axis_size(axis)
    return lax.ppermute(value, axis, [(i, i ^ bit) for i in range(size)])


def dot(left, right, left_dim, right_dim):
    return lax.dot_general(
        left, right, (((left_dim,), (right_dim,)), ((), ())), preferred_element_type=F32
    )


def start_gather(owns):
    return [(own, xchg(own, "col", 2), xchg(own, "dp", 1)) for own in owns]


def cross(started):
    return [
        (*blocks, xchg(blocks[1], "dp", 1) if stream % 2 else xchg(blocks[2], "col", 2))
        for stream, blocks in enumerate(started)
    ]


def both_cores(crossed):
    return [
        [item for block in blocks for item in (block, xchg(block, "col", 1))] for blocks in crossed
    ]


def end_gather(started):
    return both_cores(cross(started))


def fenced(started, order):
    came = len(started[0]) - 1
    values = order.fence(*[value for blocks in started for value in blocks[1:]])
    return [(blocks[0], *values[came * m : came * (m + 1)]) for m, blocks in enumerate(started)]


def scatter_core(halves):
    return [xchg(send, "col", 1) for _, send in halves]


def scatter_first(halves, came, order):
    parts = []
    for stream, (keep, _) in enumerate(halves):
        kept, sent = fold(keep, came[stream], (0, 1) if stream % 2 else (0, 2), order)
        parts.append((kept, xchg(sent, "dp", 1) if stream % 2 else xchg(sent, "col", 2)))
    return parts


def scatter_second(parts, order):
    terms = []
    for stream, (keep, came) in enumerate(parts):
        kept, sent = fold(keep, came, (0,), order)
        terms.append((kept, xchg(sent, "col", 2) if stream % 2 else xchg(sent, "dp", 1)))
    return terms


def scatter_tokens(halves, order):
    return scatter_second(scatter_first(halves, scatter_core(halves), order), order)


def dp_groups():
    size = lax.axis_size("dp")
    return [[i for i in range(size) if i % 2 == low] for low in (0, 1)]


def gather_weight(mine, sent, low, order):
    pair = paired(mine, xchg(sent, "dp", 1), low, order)
    full = lax.all_gather(pair, "row", axis=1, tiled=True)
    if lax.axis_size("dp") > 2:
        full = lax.all_gather(full, "dp", axis=0, tiled=True, axis_index_groups=dp_groups())
    return full.reshape(-1, full.shape[-1])


def start_scatter(grad):
    size, rows = lax.axis_size("dp"), lax.axis_size("row")
    grad = grad.reshape((size, rows) + grad.shape[1:])
    if size > 2:
        grad = lax.psum_scatter(
            grad, "dp", scatter_dimension=0, tiled=True, axis_index_groups=dp_groups()
        )
    return grad


def end_scatter(pair):
    sent = lax.dynamic_index_in_dim(pair, 1 - lax.axis_index("dp") % 2, 0, keepdims=False)
    return pair, xchg(sent, "dp", 1)


def scatter_weight(grad):
    grad = start_scatter(grad)
    grad = grad.reshape(2, -1, grad.shape[-1])
    return end_scatter(lax.psum_scatter(grad, "row", scatter_dimension=1, tiled=True))


class Chain:
    def __init__(self, grad):
        self.grad = start_scatter(grad)
        self.rows = lax.axis_size("row")
        self.step = 1
        self.came = ()
        far = self.rows - 1
        self.send(self.block(far), self.block(-far))

    def place(self, offset):
        return jnp.clip(lax.axis_index("row") + offset, 0, self.rows - 1).astype(jnp.int32)

    def block(self, offset):
        return lax.dynamic_index_in_dim(self.grad, self.place(offset), 1, keepdims=False)

    def send(self, up, down):
        far = self.rows - self.step
        self.came = (
            lax.ppermute(up, "row", [(i, i + 1) for i in range(self.step)]),
            lax.ppermute(down, "row", [(i, i - 1) for i in range(far, self.rows)]),
        )

    def advance(self, order):
        self.step += 1
        far = self.rows - self.step
        places = jnp.stack((self.place(far), self.place(-far)))
        _, _, n, d = self.grad.shape
        part = pl.BlockSpec((1, n, d), lambda p, at: (p, 0, 0))

        def picked(which):
            return pl.BlockSpec((1, 1, n, d), lambda p, at: (p, at[which], 0, 0))

        def kernel(at_ref, up_ref, down_ref, first_ref, second_ref, *out_refs):
            if far:
                out_refs[0][...] = add(first_ref[0], up_ref[...]).astype(BF)
                out_refs[1][...] = add(second_ref[0], down_ref[...]).astype(BF)
            else:
                out_refs[0][...] = (add(first_ref[0], up_ref[...]) + down_ref[...].astype(F32)).astype(BF)

        count = 2 if far else 1
        outs = order.call(
            kernel,
            (2,),
            [part, part, picked(0), picked(1)],
            [part] * count,
            [shaped(2, n, d)] * count,
            (places, *self.came, self.grad, self.grad),
            prefetch=1,
            moved=24 * n * d,
        )
        if far:
            self.send(*outs)
            return None
        return end_scatter(outs[0])


def sum_over_col(value):
    return sum([xchg(value, "col", mask) for mask in range(1, lax.axis_size("col"))], value)


def rope_tables(positions):
    freqs = THETA ** (-jnp.arange(HEAD_SIZE // 2, dtype=F32) * 2.0 / HEAD_SIZE)
    angles = positions.astype(F32)[:, None] * freqs[None, :]
    cosine, sine = jnp.cos(angles), jnp.sin(angles)
    return jnp.concatenate((cosine, cosine), axis=1), jnp.concatenate((-sine, sine), axis=1)


class Order:
    def __init__(self):
        self.last = ()

    def wait(self, *values):
        self.last = self.last + values

    def fence(self, *values):
        return self.call(
            lambda *refs: None,
            (1,),
            [pl.BlockSpec(memory_space=pl.ANY)] * len(values),
            [pl.BlockSpec(memory_space=pl.ANY)] * len(values),
            [shaped(*value.shape, dtype=value.dtype) for value in values],
            values,
            aliases={i: i for i in range(len(values))},
        )

    def call(
        self, kernel, grid, in_specs, out_specs, out_shape, args, scratch=(), flops=0, moved=0, prefetch=0, aliases=None
    ):
        last = [token for token in self.last if all(token is not arg for arg in args)]
        tokens = len(last)
        count = len(args)

        def run(*refs):
            kernel(*refs[:count], *refs[count + tokens :])

        outs = pl.pallas_call(
            run,
            grid_spec=pltpu.PrefetchScalarGridSpec(
                num_scalar_prefetch=prefetch,
                grid=grid,
                in_specs=list(in_specs) + [pl.BlockSpec(memory_space=pl.ANY)] * tokens,
                out_specs=out_specs,
                scratch_shapes=list(scratch),
            ),
            out_shape=out_shape,
            input_output_aliases=aliases or {},
            compiler_params=pltpu.CompilerParams(vmem_limit_bytes=56 * 2**20),
            cost_estimate=pl.CostEstimate(flops=flops, bytes_accessed=moved, transcendentals=0),
        )(*args, *last)
        self.last = (outs[0] if isinstance(outs, (list, tuple)) else outs,)
        return outs


def shaped(*shape, dtype=BF):
    return jax.ShapeDtypeStruct(shape, dtype)


def whole(shape):
    return pl.BlockSpec(shape, lambda *_: (0,) * len(shape))


SCALARS = pl.BlockSpec(memory_space=pltpu.SMEM)


def prepare_attn_kernel(low_ref, qkv_ref, out_ref, gain_ref, mine_ref, sent_ref):
    wide = qkv_ref.shape[1] // 2
    tall = out_ref.shape[0] // 2
    for part, ref in ((low_ref[0], mine_ref), (1 - low_ref[0], sent_ref)):
        columns = qkv_ref[:, pl.ds(pl.multiple_of(part * wide, wide), wide)]
        ref[:, :wide] = (columns.astype(F32) * gain_ref[...]).astype(BF)
        ref[:, wide:] = out_ref[pl.ds(pl.multiple_of(part * tall, tall), tall), :].T


def prepare_attn(low, wqkv, wo, gain, order):
    d = wqkv.shape[0]
    out = shaped(d, wqkv.shape[1] // 2 + wo.shape[0] // 2)
    return order.call(
        prepare_attn_kernel,
        (1,),
        [SCALARS] + [whole(item.shape) for item in (wqkv, wo, gain)],
        [whole(out.shape)] * 2,
        [out, out],
        (low, wqkv, wo, gain),
        moved=4 * (wqkv.size + wo.size),
    )


def prepare_ffn_kernel(chunks, cut, low_ref, w1_ref, w3_ref, w2_ref, gain_ref, *refs):
    units = w1_ref.shape[1] // 2
    gain = gain_ref[...]
    for at, chunk in enumerate(chunks):
        for part, ref in ((low_ref[0], refs[2 * at]), (1 - low_ref[0], refs[2 * at + 1])):
            place = pl.ds(pl.multiple_of(part * units + chunk * cut, cut), cut)
            ref[:, :cut] = (w1_ref[:, place].astype(F32) * gain).astype(BF)
            ref[:, cut : 2 * cut] = (w3_ref[:, place].astype(F32) * gain).astype(BF)
            ref[:, 2 * cut :] = w2_ref[place, :].T


def prepare_ffn(chunks, cut, low, w1, w3, w2, gain, order):
    out = shaped(w1.shape[0], 3 * cut)
    outs = order.call(
        lambda *refs: prepare_ffn_kernel(chunks, cut, *refs),
        (1,),
        [SCALARS] + [whole(item.shape) for item in (w1, w3, w2, gain)],
        [whole(out.shape)] * (2 * len(chunks)),
        [out] * (2 * len(chunks)),
        (low, w1, w3, w2, gain),
        moved=12 * w1.size,
    )
    return [(outs[2 * i], outs[2 * i + 1]) for i in range(len(chunks))]


def paired_kernel(low_ref, mine_ref, came_ref, out_ref):
    out_ref[pl.ds(low_ref[0], 1)] = mine_ref[...][None]
    out_ref[pl.ds(1 - low_ref[0], 1)] = came_ref[...][None]


def paired(mine, came, low, order):
    out = shaped(2, *mine.shape)
    return order.call(
        paired_kernel,
        (1,),
        [SCALARS, whole(mine.shape), whole(mine.shape)],
        whole(out.shape),
        out,
        (low, mine, came),
        moved=8 * mine.size,
    )


def inverse_rms(values):
    return lax.rsqrt(jnp.mean(values * values, axis=-1, keepdims=True) + EPS)


def by_rows(kernel, ins, outs, order, scalars=None):
    def spec(item):
        lead = item.shape[:-2]
        block = lead + (item.shape[-2] // 4, item.shape[-1])
        return pl.BlockSpec(block, lambda l: (0,) * len(lead) + (l, 0))

    extra = [] if scalars is None else [scalars]
    return order.call(
        kernel,
        (4,),
        [SCALARS] * len(extra) + [spec(item) for item in ins],
        [spec(item) for item in outs],
        outs,
        (*extra, *ins),
        moved=4 * sum(item.size for item in (*ins, *outs)),
    )


def first_norm(inputs, order):
    def kernel(in_ref, *out_refs):
        for m, ref in enumerate(out_refs):
            values = in_ref[m].astype(F32)
            ref[...] = (values * inverse_rms(values)).astype(BF)

    return by_rows(kernel, [inputs], [shaped(*inputs.shape[1:])] * inputs.shape[0], order)


def masked(cotangent, scalars, order):
    def kernel(scalar_ref, in_ref, *out_refs):
        for m, ref in enumerate(out_refs):
            rows = ref.shape[0]
            place = scalar_ref[0] + pl.program_id(0) * rows
            places = place + lax.broadcasted_iota(jnp.int32, ref.shape, 0)
            valid = places < scalar_ref[1 + m]
            ref[...] = jnp.where(valid, in_ref[m].astype(F32), 0.0).astype(BF)

    return by_rows(kernel, [cotangent], [shaped(*cotangent.shape[1:])] * cotangent.shape[0], order, scalars)


def fold(keep, came, kept, order):
    others = [i for i in range(keep.shape[0]) if i not in kept]
    shape = (len(kept),) + keep.shape[1:]

    def kernel(keep_ref, came_ref, kept_ref, sent_ref):
        for at, (mine, other) in enumerate(zip(kept, others)):
            sent_ref[at] = add(keep_ref[other], came_ref[other]).astype(BF)
            kept_ref[at] = add(keep_ref[mine], came_ref[mine])

    return by_rows(kernel, [keep, came], [shaped(*shape, dtype=F32), shaped(*shape)], order)


def add(left, right):
    return left.astype(F32) + right.astype(F32)


def total_of(refs):
    return add(refs[0][0], refs[1][0])


def second_norm(inputs, terms, order):
    micro = inputs.shape[0]

    def kernel(in_ref, *refs):
        for m in range(micro):
            values = in_ref[m].astype(F32) + total_of(refs[2 * m : 2 * m + 2])
            refs[2 * micro + m][...] = (values * inverse_rms(values)).astype(BF)
            refs[3 * micro + m][...] = values

    shape = inputs.shape[1:]
    outs = by_rows(
        kernel,
        [inputs] + [item for pair in terms for item in pair],
        [shaped(*shape)] * micro + [shaped(*shape, dtype=F32)] * micro,
        order,
    )
    return outs[:micro], outs[micro:]


def finished(residual, terms, order):
    micro = len(residual)

    def kernel(*refs):
        for m in range(micro):
            refs[-1][m] = (refs[3 * m][...] + total_of(refs[3 * m + 1 : 3 * m + 3])).astype(BF)

    ins = [item for m in range(micro) for item in (residual[m], *terms[m])]
    return by_rows(kernel, ins, [shaped(micro, *residual[0].shape)], order)[0]


def norm_back(values, scaled):
    inverse = inverse_rms(values)
    inner = jnp.mean(scaled * values, axis=-1, keepdims=True)
    return inverse * scaled - values * (inverse * inverse * inverse) * inner


def second_norm_back(residual, upstream, terms, order):
    micro = len(residual)

    def kernel(*refs):
        outs = refs[4 * micro :]
        for m in range(micro):
            residual_ref, upstream_ref = refs[4 * m : 4 * m + 2]
            grad = upstream_ref[...].astype(F32) + norm_back(
                residual_ref[...], total_of(refs[4 * m + 2 : 4 * m + 4])
            )
            outs[m][...] = grad.astype(BF)
            outs[micro + m][...] = grad

    ins = [item for m in range(micro) for item in (residual[m], upstream[m], *terms[m])]
    shape = residual[0].shape
    outs = by_rows(
        kernel, ins, [shaped(*shape)] * micro + [shaped(*shape, dtype=F32)] * micro, order
    )
    return outs[:micro], outs[micro:]


def first_norm_back(inputs, upstream, terms, order):
    micro = inputs.shape[0]

    def kernel(in_ref, *refs):
        for m in range(micro):
            upstream_ref = refs[3 * m]
            grad = upstream_ref[...] + norm_back(
                in_ref[m].astype(F32), total_of(refs[3 * m + 1 : 3 * m + 3])
            )
            refs[-1][m] = grad.astype(BF)

    ins = [inputs] + [item for m in range(micro) for item in (upstream[m], *terms[m])]
    return by_rows(kernel, ins, [shaped(*inputs.shape)], order)[0]


def head_probs(query, keys, me, length, rows):
    places = query.shape[0]
    scores = dot(query, keys, 1, 1) * HEAD_SIZE ** (-0.5)
    queried = lax.broadcasted_iota(jnp.int32, (places, places), 0)
    keyed = lax.broadcasted_iota(jnp.int32, (places, places), 1)
    queried = ((queried // rows) ^ me) * rows + queried % rows
    keyed = ((keyed // rows) ^ me) * rows + keyed % rows
    scores = jnp.where((keyed <= queried) & (keyed < length), scores, NEGATIVE)
    expo = jnp.exp(scores - jnp.max(scores, axis=-1, keepdims=True))
    return expo * (1.0 / jnp.sum(expo, axis=-1, keepdims=True))


def turn(values, cosine, sine):
    return values * cosine + pltpu.roll(values, HEAD_SIZE // 2, 1) * sine


def joined(refs):
    return jnp.concatenate([ref[...] for ref in refs], axis=0)


def put_blocks(value, y, pairs, keep_ref, send_ref):
    rows = keep_ref.shape[1]
    for x in range(pairs):
        start = 2 * x * rows
        keep_ref[y * pairs + x] = value[start : start + rows].astype(BF)
        send_ref[y * pairs + x] = value[start + rows : start + 2 * rows].astype(BF)


def head_at(index):
    return slice(index * HEAD_SIZE, (index + 1) * HEAD_SIZE)


def attend_kernel(count, groups, scalar_ref, *refs):
    blocks = refs[:count]
    cos_ref, sin_ref, w_ref, keep_ref, send_ref, q_ref, k_ref, v_ref, a_ref = refs[count:]
    rows = blocks[0].shape[0]
    cols = count // 2
    span = (QUERY_PER_GROUP + 2) * HEAD_SIZE
    cosine, sine = cos_ref[...], sin_ref[...]
    for y in (0, 1):
        projected = dot(joined(blocks[y * cols : (y + 1) * cols]), w_ref[:, : groups * span], 1, 0)
        for g in range(groups):
            part = projected[:, g * span : (g + 1) * span]
            keys = turn(part[:, -2 * HEAD_SIZE : -HEAD_SIZE], cosine, sine).astype(BF)
            values = part[:, -HEAD_SIZE:].astype(BF)
            k_ref[y, :, head_at(g)] = keys
            v_ref[y, :, head_at(g)] = values
            for r in range(QUERY_PER_GROUP):
                query = turn(part[:, head_at(r)], cosine, sine).astype(BF)
                probs = head_probs(query, keys, scalar_ref[0], scalar_ref[1 + y], rows).astype(BF)
                at = head_at(g * QUERY_PER_GROUP + r)
                q_ref[y, :, at] = query
                a_ref[y, :, at] = dot(probs, values, 1, 0).astype(BF)
        put_blocks(dot(a_ref[y], w_ref[:, groups * span :], 1, 1), y, cols // 2, keep_ref, send_ref)


def attend(blocks, scalars, cosine, sine, weights, groups, order):
    count = len(blocks)
    rows, width = blocks[0].shape
    places = count // 2 * rows
    head = groups * HEAD_SIZE
    sizes = (QUERY_PER_GROUP * head, head, head, QUERY_PER_GROUP * head)
    outs = [(count // 2, rows, width)] * 2 + [(2, places, size) for size in sizes]
    return order.call(
        lambda *refs: attend_kernel(count, groups, *refs),
        (1,),
        [SCALARS] + [whole(item.shape) for item in (*blocks, cosine, sine, weights)],
        [whole(shape) for shape in outs],
        [jax.ShapeDtypeStruct(shape, BF) for shape in outs],
        flops=4 * places * weights.size + 16 * places * places * QUERY_PER_GROUP * head,
        moved=8 * places * width + 2 * weights.size,
        args=(scalars, *blocks, cosine, sine, weights,),
    )


def attend_back_kernel(count, groups, scalar_ref, *refs):
    pieces = refs[:count]
    cos_ref, sin_ref, w_ref, q_ref, k_ref, v_ref, keep_ref, send_ref, grad_ref = refs[count:]
    rows = pieces[0].shape[0]
    cols = count // 2
    span = (QUERY_PER_GROUP + 2) * HEAD_SIZE
    scale = HEAD_SIZE ** (-0.5)
    cosine, sine = cos_ref[...], -sin_ref[...]
    for y in (0, 1):
        piece = joined(pieces[y * cols : (y + 1) * cols])
        grad_out = dot(piece, w_ref[:, groups * span :], 1, 0).astype(BF)
        parts = []
        for g in range(groups):
            keys, values = k_ref[y, :, head_at(g)], v_ref[y, :, head_at(g)]
            keys_grad, values_grad = 0.0, 0.0
            for r in range(QUERY_PER_GROUP):
                at = head_at(g * QUERY_PER_GROUP + r)
                query, upstream = q_ref[y, :, at], grad_out[:, at]
                probs = head_probs(query, keys, scalar_ref[0], scalar_ref[1 + y], rows)
                grad_probs = dot(upstream, values, 1, 1)
                values_grad = values_grad + dot(probs.astype(BF), upstream, 0, 0)
                inner = jnp.sum(probs * grad_probs, axis=-1, keepdims=True)
                grad_scores = (probs * (grad_probs - inner)).astype(BF)
                parts.append(turn(dot(grad_scores, keys, 1, 0) * scale, cosine, sine))
                keys_grad = keys_grad + dot(grad_scores, query, 0, 0)
            parts.extend((turn(keys_grad * scale, cosine, sine), values_grad))
        grad_proj = jnp.concatenate([part.astype(BF) for part in parts], axis=1)
        grad_ref[y] = grad_proj
        put_blocks(dot(grad_proj, w_ref[:, : groups * span], 1, 1), y, cols // 2, keep_ref, send_ref)


def attend_back(pieces, scalars, cosine, sine, weights, saved, groups, order):
    count = len(pieces)
    rows, width = pieces[0].shape
    places = count // 2 * rows
    span = groups * (QUERY_PER_GROUP + 2) * HEAD_SIZE
    outs = [(count // 2, rows, width)] * 2 + [(2, places, span)]
    return order.call(
        lambda *refs: attend_back_kernel(count, groups, *refs),
        (1,),
        [SCALARS] + [whole(item.shape) for item in (*pieces, cosine, sine, weights, *saved)],
        [whole(shape) for shape in outs],
        [jax.ShapeDtypeStruct(shape, BF) for shape in outs],
        flops=4 * places * weights.size + 48 * places * places * groups * HEAD_SIZE,
        moved=8 * places * width + 2 * weights.size,
        args=(scalars, *pieces, cosine, sine, weights, *saved,),
    )


def units_kernel(count, cut, *refs):
    rows_refs, piece_refs = refs[:count], refs[count : 2 * count]
    w_ref, pair_ref, hidden_ref = refs[2 * count :]
    gate_up = dot(joined(rows_refs), w_ref[:, : 2 * cut], 1, 0)
    hidden_grad = dot(joined(piece_refs), w_ref[:, 2 * cut :], 1, 0)
    gate, up = gate_up[:, :cut], gate_up[:, cut:]
    sigma = 1.0 / (1.0 + jnp.exp(-gate))
    swish = gate * sigma
    hidden_ref[...] = (swish * up).astype(BF).reshape(hidden_ref.shape)
    pair_ref[..., :cut] = (
        (hidden_grad * up * sigma * (1.0 + gate * (1.0 - sigma))).astype(BF).reshape(hidden_ref.shape)
    )
    pair_ref[..., cut:] = (hidden_grad * swish).astype(BF).reshape(hidden_ref.shape)


def units(rows, pieces, weights, order):
    count = len(rows)
    places, width = rows[0].shape
    cut = weights.shape[1] // 3
    part = places // 4
    block = pl.BlockSpec((part, width), lambda l: (l, 0))
    return order.call(
        lambda *refs: units_kernel(count, cut, *refs),
        (4,),
        [block] * (2 * count) + [whole(weights.shape)],
        [pl.BlockSpec((count, part, size), lambda l: (0, l, 0)) for size in (2 * cut, cut)],
        [shaped(count, places, size) for size in (2 * cut, cut)],
        flops=2 * count * places * weights.size,
        moved=4 * count * places * width,
        args=(*rows, *pieces, weights),
    )


def grads_kernel(counts, *refs):
    grad_ref = refs[-1]
    size = grad_ref.shape[2]
    start = at = 0
    lefts = refs[sum(n for n, _ in counts) :]
    for n, k in counts:
        rows = joined(refs[start : start + n])
        left = jnp.concatenate([ref[...] for ref in lefts[:k]], axis=0)
        start, lefts = start + n, lefts[k:]
        product = dot(left, rows, 0, 0).astype(BF)
        for block in range(grad_ref.shape[0]):
            grad_ref[block, at : at + product.shape[0]] = product[:, block * size : (block + 1) * size]
        at += product.shape[0]


def weight_grads(products, owners, order, total=None, into=None):
    rows = [block for blocks, _ in products for block in blocks]
    lefts = [left for _, items in products for left in items]
    counts = [(len(blocks), len(items)) for blocks, items in products]
    places, width = rows[0].shape
    tile = width // 4
    part = sum(items[0].shape[1] for _, items in products)
    total = total or part
    at = 0 if into is None else total // part - 1
    tokens = len(products[0][0]) * places
    args = (*rows, *lefts) + (() if into is None else (into,))
    return order.call(
        lambda *refs: grads_kernel(counts, *refs),
        (4,),
        [pl.BlockSpec((places, tile), lambda t: (0, t))] * len(rows)
        + [whole(left.shape) for left in lefts]
        + [pl.BlockSpec(memory_space=pl.ANY)] * (into is not None),
        pl.BlockSpec((owners // 4, part, width // owners), lambda t: (t, at, 0)),
        shaped(owners, total, width // owners),
        flops=2 * tokens * part * width,
        moved=2 * len(products) * tokens * width,
        args=args,
        aliases={} if into is None else {len(args) - 1: 0},
    )


def back_kernel(count, lo, split, added, *refs):
    lefts, weights = refs[:count], refs[count : 2 * count]
    refs = refs[2 * count :]
    total = refs[0][...] if added else None
    refs = refs[1:] if added else refs
    for left, weight in zip(lefts, weights):
        value = left[...].reshape(-1, left.shape[-1])
        product = dot(value, weight[:, lo : lo + value.shape[1]], 1, 1)
        total = product if total is None else total + product
    if split:
        put_blocks(total, 0, refs[0].shape[0], *refs)
    else:
        refs[0][...] = total


def back(lefts, weights, lo, order, before=None, stream=None):
    count, places, depth = lefts[0].shape
    width = weights[0].shape[0]
    added, split = before is not None, stream is not None
    first = 2 * stream if split else 0
    half = pl.BlockSpec((2, places, width), lambda t: (t, 0, 0))
    flat = pl.BlockSpec((4 * places, width), lambda t: (first + t, 0))
    halves = shaped(4, places, width)
    steps = 2 if split else count // 4
    return order.call(
        lambda *refs: back_kernel(len(lefts), lo, split, added, *refs),
        (steps,),
        [pl.BlockSpec((4, places, depth), lambda t: (first + t, 0, 0))] * len(lefts)
        + [whole(weights[0].shape)] * len(weights)
        + ([flat] if added else []),
        [half, half] if split else flat,
        [halves, halves] if split else shaped(count * places, width, dtype=F32),
        flops=8 * steps * places * depth * width * len(lefts),
        moved=16 * steps * places * width,
        args=(*lefts, *weights, *((before,) if added else ())),
    )


def finish_ffn_kernel(count, cut, low_ref, *refs):
    pairs, cames = refs[:count], refs[count : 2 * count]
    w1_ref, w3_ref, gain_ref, grad1_ref, grad3_ref, grad2_ref, sum_ref = refs[2 * count :]
    units = w1_ref.shape[1] // 2
    gain, total = gain_ref[...], 0.0
    for chunk in range(count):
        for part, value in (
            (low_ref[0], pairs[chunk][low_ref[0]]),
            (1 - low_ref[0], cames[chunk][...]),
        ):
            place = pl.ds(pl.multiple_of(part * units + chunk * cut, cut), cut)
            value = value.astype(F32)
            first, second = value[:cut].T, value[cut : 2 * cut].T
            grad2_ref[place, :] = value[2 * cut :]
            grad1_ref[:, place] = first * gain
            grad3_ref[:, place] = second * gain
            product = first * w1_ref[:, place].astype(F32) + second * w3_ref[:, place].astype(F32)
            total = total + jnp.sum(product, axis=1, keepdims=True)
    sum_ref[...] = as_row(total)


def as_row(column):
    return jnp.broadcast_to(column, (column.shape[0], 128)).T[:1]


def finish_ffn(low, parts, w1, w3, w2, gain, order):
    count = len(parts)
    args = [pair for pair, _ in parts] + [came for _, came in parts] + [w1, w3, gain]
    outs = [shaped(*shape, dtype=F32) for shape in (w1.shape, w3.shape, w2.shape, gain.shape[::-1])]
    return order.call(
        lambda *refs: finish_ffn_kernel(count, parts[0][1].shape[0] // 3, *refs),
        (1,),
        [SCALARS] + [whole(item.shape) for item in args],
        [whole(item.shape) for item in outs],
        outs,
        (low, *args),
        moved=24 * w1.size,
    )


def finish_attn_kernel(low_ref, pair_ref, came_ref, w_ref, gain_ref, grad_ref, out_ref, sum_ref):
    wide = w_ref.shape[1] // 2
    tall = out_ref.shape[0] // 2
    gain, total = gain_ref[...], 0.0
    for part, value in ((low_ref[0], pair_ref[low_ref[0]]), (1 - low_ref[0], came_ref[...])):
        columns = pl.ds(pl.multiple_of(part * wide, wide), wide)
        value = value.astype(F32)
        first = value[:wide].T
        grad_ref[:, columns] = first * gain
        out_ref[pl.ds(pl.multiple_of(part * tall, tall), tall), :] = value[wide:]
        total = total + jnp.sum(first * w_ref[:, columns].astype(F32), axis=1, keepdims=True)
    sum_ref[...] = as_row(total)


def finish_attn(low, part, wqkv, wo, gain, order):
    args = [*part, wqkv, gain]
    outs = [shaped(*shape, dtype=F32) for shape in (wqkv.shape, wo.shape, gain.shape[::-1])]
    return order.call(
        finish_attn_kernel,
        (1,),
        [SCALARS] + [whole(item.shape) for item in args],
        [whole(item.shape) for item in outs],
        outs,
        (low, *args),
        moved=12 * wqkv.size,
    )


def body(inputs, lengths, wqkv, wo, w1, w3, w2, attn_gain, ffn_gain, cotangent):
    micro, _, rows, width = inputs.shape
    cols = lax.axis_size("col")
    places = cols * rows
    me = lax.axis_index("col")
    groups = wqkv.shape[1] // ((QUERY_PER_GROUP + 2) * HEAD_SIZE) // 2
    cut = w1.shape[1] // 2 // CHUNKS
    d = wqkv.shape[0]
    owners = width // d
    streams = range(micro)
    inputs, cotangent = inputs[:, 0], cotangent[:, 0]
    order = Order()
    low = (lax.axis_index("dp") % 2).astype(jnp.int32)[None]
    attn_gain, ffn_gain = attn_gain.astype(F32)[:, None], ffn_gain.astype(F32)[:, None]

    def prepared(*chunks):
        return prepare_ffn(chunks, cut, low, w1, w3, w2, ffn_gain, order)

    mine, sent = prepare_attn(low, wqkv, wo, attn_gain, order)
    normed1 = first_norm(inputs, order)
    attn_w = gather_weight(mine, sent, low, order)
    attn_rows = cross(fenced(start_gather(normed1), order))
    ffn_parts = prepared(0)
    attn_rows = both_cores(fenced(attn_rows, order))
    own_scalars = jnp.concatenate(((me * rows).astype(jnp.int32)[None], lengths.reshape(micro)))
    upstream = masked(cotangent, own_scalars, order)
    pieces = start_gather(upstream)
    ffn_ws = [gather_weight(*ffn_parts[0], low, order)]

    positions = (
        (jnp.arange(cols, dtype=jnp.int32) ^ me)[:, None] * rows
        + jnp.arange(rows, dtype=jnp.int32)[None, :]
    ).reshape(places)
    cosine, sine = rope_tables(positions)
    other_lengths = xchg(lengths, "dp", 1)
    scalars = [
        jnp.concatenate((me.astype(jnp.int32)[None], lengths[m], other_lengths[m])) for m in streams
    ]

    def run_attend(m):
        return attend(attn_rows[m], scalars[m], cosine, sine, attn_w, groups, order)

    ahead = [run_attend(0)]
    pieces = end_gather(fenced(pieces, order))
    ahead.append(run_attend(1))
    order.wait(*sum(pieces, []))
    halves = [item[:2] for item in ahead]
    terms = scatter_first(halves, scatter_core(halves), order)
    ffn_parts += prepared(1)
    terms = scatter_second(terms, order)
    normed2, residual = second_norm(inputs, terms, order)
    ffn_rows = start_gather(normed2)
    ffn_ws += [gather_weight(*ffn_parts[1], low, order)]
    ffn_rows = end_gather(ffn_rows)
    all_rows, all_pieces = sum(ffn_rows, []), sum(pieces, [])

    pairs, hiddens = [], []

    def run_units(chunk):
        pair, hidden = units(all_rows, all_pieces, ffn_ws[chunk], order)
        pairs.append(pair)
        hiddens.append(hidden)

    def pair_grads(chunk):
        left = pairs[chunk].reshape(-1, 2 * cut)
        return weight_grads([(all_rows, [left])], owners, order, total=3 * cut)

    def hidden_grads(chunk, into):
        left = hiddens[chunk].reshape(-1, cut)
        return weight_grads([(all_pieces, [left])], owners, order, total=3 * cut, into=into)

    run_units(0)
    ffn_grads = [scatter_weight(hidden_grads(0, pair_grads(0)))]
    early = back(pairs, ffn_ws[:1], 0, order)
    run_units(1)
    halves = [
        back(pairs[1:], ffn_ws[1:], 0, order, before=early, stream=m) for m in streams
    ]
    terms = scatter_first(halves, scatter_core(halves), order)
    part = pair_grads(1)
    terms = scatter_second(terms, order)
    ffn_grads.append(scatter_weight(hidden_grads(1, part)))
    attn_up, residual_grad = second_norm_back(residual, upstream, terms, order)
    attn_pieces = start_gather(attn_up)
    halves = [back(hiddens, ffn_ws, 2 * cut, order, stream=0)]
    attn_pieces = end_gather(fenced(attn_pieces, order))
    halves.append(back(hiddens, ffn_ws, 2 * cut, order, stream=1))
    terms = scatter_first(halves, scatter_core(halves), order)

    keep, send, grad_proj = zip(
        *[
            attend_back(attn_pieces[m], scalars[m], cosine, sine, attn_w, ahead[m][2:5], groups, order)
            for m in streams
        ]
    )
    halves = list(zip(keep, send))
    came = scatter_core(halves)
    order.wait(ffn_grads[0][1])
    attn_grads = weight_grads(
        [
            (sum(attn_rows, []), [grad_proj[m].reshape(2 * places, -1) for m in streams]),
            (sum(attn_pieces, []), [ahead[m][5].reshape(2 * places, -1) for m in streams]),
        ],
        owners,
        order,
    )
    chain = Chain(attn_grads)
    last_terms = scatter_first(halves, came, order)
    chain.advance(order)
    terms = scatter_second(terms, order)
    last_terms = scatter_second(last_terms, order)
    chain.advance(order)
    order.wait(ffn_grads[1][1])
    result = finished(residual, terms, order)
    source_grad = first_norm_back(inputs, residual_grad, last_terms, order)
    attn_part = chain.advance(order)
    w1_grad, w3_grad, w2_grad, ffn_sum = finish_ffn(low, ffn_grads, w1, w3, w2, ffn_gain, order)
    ffn_sum = sum_over_col(ffn_sum)[0]
    wqkv_grad, wo_grad, attn_sum = finish_attn(low, attn_part, wqkv, wo, attn_gain, order)
    attn_sum = sum_over_col(attn_sum)[0]
    return (
        result[:, None],
        source_grad[:, None],
        attn_sum,
        ffn_sum,
        wqkv_grad,
        wo_grad,
        w1_grad,
        w3_grad,
        w2_grad,
    )


def solution(mesh):
    tokens = P(None, ("dp", "row"), "col", None)
    in_specs = (
        tokens,
        P(None, ("dp", "row")),
        P(("dp", "row"), "col"),
        P("col", ("dp", "row")),
        P(("dp", "row"), "col"),
        P(("dp", "row"), "col"),
        P("col", ("dp", "row")),
        P(("dp", "row")),
        P(("dp", "row")),
        tokens,
    )
    out_specs = (
        tokens,
        tokens,
        P(("dp", "row")),
        P(("dp", "row")),
        P(("dp", "row"), "col"),
        P("col", ("dp", "row")),
        P(("dp", "row"), "col"),
        P(("dp", "row"), "col"),
        P("col", ("dp", "row")),
    )
    return jax.shard_map(body, mesh=mesh, in_specs=in_specs, out_specs=out_specs, check_vma=False)
```

time: 868 us -> 733 us (0.84)
  Pallas kernels: 0 us -> 340 us
  matrix products: 196 us -> 0 us
  local copies, waits for them, and re-layouts: 201 us -> 37 us
  other arithmetic: 117 us -> 10.7 us
  waiting for transfers between devices: 253 us -> 230 us
  starting transfers between devices: 76.4 us -> 88 us
    pallas_call x0 -> x53, Pallas kernels: none -> 340 us  [call(): pl.pallas_call(run, grid_spec=pltpu.PrefetchScalarGridSpec(num_scalar_pre...]
    dot_general x30 -> x0, matrix products: 196 us -> none  [the longest x24 181 us: dot(): lax.dot_general(left, right, (((left_dim,), (right_dim,)), ((), ())), pre...]
    slice x30 -> x2, local copies, waits for them, and re-layouts: 48.3 us -> 1.16 us  [the longest x1 0.58 us: body(): other_lengths[m]]
    convert_element_type x22 -> x0, other arithmetic: 41.7 us -> none  [the longest x4 19.3 us: scatter_tokens(): quad = add(parts[:, :, 0], xchg(parts[:, :, 1], 'col', 1)).astype(BF)]
    unnamed x257 -> x182, local copies, waits for them, and re-layouts: 64.7 us -> 26.6 us
    ppermute x78 -> x93, waiting for transfers between devices: 253 us -> 219 us  [xchg(): return lax.ppermute(value, axis, [(i, i ^ bit) for i in range(size)])]
    reshape x12 -> x0, local copies, waits for them, and re-layouts: 22.3 us -> none  [the longest x4 16.9 us: scatter_weight(): grad = grad.reshape(size, -1, grad.shape[-1])]
    another operation x18 -> x3, other arithmetic: 22.6 us -> 1.83 us  [advance(): places = jnp.stack((self.place(far), self.place(-far)))]
  transfers between devices with their start and end apart: 90 -> 104, of which waited for: 38 -> 48; matrix products, arithmetic and copies ran while one was open for 58% -> 2% of each run, Pallas kernels for 0% -> 46%
where the time goes in v2:
time: 733 us; the launch traced here: 720 us
  Pallas kernels  340 us (46%)
  waiting for transfers between devices  230 us (31%)
  starting transfers between devices  88 us (12%)
  local copies, waits for them, and re-layouts  37 us (5%)
  between operations  14.8 us (2%)
  other arithmetic  10.7 us (1%)
    pallas_call x53, Pallas kernels, call(): pl.pallas_call(run, grid_spec=pltpu.PrefetchScalarGridSpec(num_scalar_pre...  340 us
    ppermute x93, waiting for transfers between devices, xchg(): return lax.ppermute(value, axis, [(i, i ^ bit) for i in range(size)])  219 us
    ppermute x93, starting transfers between devices, xchg(): return lax.ppermute(value, axis, [(i, i ^ bit) for i in range(size)])  62.6 us
    unnamed x182, local copies, waits for them, and re-layouts  26.6 us
  transfers between devices with their start and end apart: 104, of which 48 were waited for; matrix products, arithmetic and copies ran while one was open for 2% of the time, Pallas kernels for 46%

profile of v2, /device:TPU:0, one launch (start us, length us, event | category | flops | bytes accessed | tf_op | source)
XLA Modules:
  0.0 720.3 jit_solution(14499906674985035205)
XLA Ops:
  31.0 10.0 %collective-permute-done.5.refs_3_ = bf16[128,2048]{1,0:T(8,128)(2,1)S(1)} collective-permute-done((bf16[128,2048]{1,0:T(8,128)(2,1)S(1)}, bf16[128,2048]{1,0:T(8,128)(2,1)S(1)}, u32[]{:S(2)}, u32[]{:S(2)}) %collective-permute-start.5) | collective-permute-done | bytes 524320 | tf_op jit(solution)/shard_map/ppermute | solution.py:20
  42.7 7.8 %collective-permute-done.3.refs_1_ = bf16[128,2048]{1,0:T(8,128)(2,1)} collective-permute-done((bf16[128,2048]{1,0:T(8,128)(2,1)S(1)}, bf16[128,2048]{1,0:T(8,128)(2,1)}, u32[]{:S(2)}, u32[]{:S(2)}) %collective-permute-start.3) | collective-permute-done | bytes 524320 | tf_op jit(solution)/shard_map/ppermute | solution.py:20
  59.9 8.5 %collective-permute-done.7.refs_2_ = bf16[128,2048]{1,0:T(8,128)(2,1)S(1)} collective-permute-done((bf16[128,2048]{1,0:T(8,128)(2,1)}, bf16[128,2048]{1,0:T(8,128)(2,1)S(1)}, u32[]{:S(2)}, u32[]{:S(2)}) %collective-permute-start.7) | collective-permute-done | bytes 524320 | tf_op jit(solution)/shard_map/ppermute | solution.py:20
  68.3 16.2 %collective-permute-done.8.refs_5_ = bf16[128,2048]{1,0:T(8,128)(2,1)S(1)} collective-permute-done((bf16[128,2048]{1,0:T(8,128)(2,1)S(1)}, bf16[128,2048]{1,0:T(8,128)(2,1)S(1)}, u32[]{:S(2)}, u32[]{:S(2)}) %collective-permute-start.8) | collective-permute-done | bytes 524320 | tf_op jit(solution)/shard_map/ppermute | solution.py:20
  111.4 8.8 %collective-permute-done.19.refs_1_ = bf16[128,2048]{1,0:T(8,128)(2,1)S(1)} collective-permute-done((bf16[128,2048]{1,0:T(8,128)(2,1)S(1)}, bf16[128,2048]{1,0:T(8,128)(2,1)S(1)}, u32[]{:S(2)}, u32[]{:S(2)}) %collective-permute-start.19) | collective-permute-done | bytes 524320 | tf_op jit(solution)/shard_map/ppermute | solution.py:20
  124.0 12.1 %shard_map.177 = (bf16[4,128,2048]{2,1,0:T(8,128)(2,1)}, bf16[4,128,2048]{2,1,0:T(8,128)(2,1)}, bf16[2,512,256]{2,1,0:T(8,128)(2,1)}, bf16[2,512,128]{2,1,0:T(8,...) custom-call(s32[3]{0:T(128)} %pad_add_fusion.refs_0_, ...), custom_call_target="tpu_custom_call" | custom-call | flops 4294967296 | bytes 11534336 | tf_op jit(solution)/shard_map/pallas_call | solution.py:209
  137.5 12.5 %shard_map.179 = (bf16[4,128,2048]{2,1,0:T(8,128)(2,1)}, bf16[4,128,2048]{2,1,0:T(8,128)(2,1)}, bf16[2,512,256]{2,1,0:T(8,128)(2,1)}, bf16[2,512,128]{2,1,0:T(8,...) custom-call(s32[3]{0:T(128)} %pad_add_fusion.2.refs_0_, ...), custom_call_target="tpu_custom_call" | custom-call | flops 4294967296 | bytes 11534336 | tf_op jit(solution)/shard_map/pallas_call | solution.py:209
  157.5 11.3 %collective-permute-done.25.refs_9_.refs_22_.refs_6_ = bf16[128,2048]{1,0:T(8,128)(2,1)S(1)} collective-permute-done((bf16[128,2048]{1,0:T(8,128)(2,1)S(1)}, bf16[128,2048]{1,0:T(8,128)(2,1)S(1)}, u32[]{:S(2)}, u32[]{:S(2)}) %collective-permute-start.25) | collective-permute-done | bytes 524320 | tf_op jit(solution)/shard_map/ppermute | solution.py:20
  189.2 14.5 %collective-permute-done.32.refs_1_ = bf16[2,128,2048]{2,1,0:T(8,128)(2,1)S(1)} collective-permute-done((bf16[2,128,2048]{2,1,0:T(8,128)(2,1)}, bf16[2,128,2048]{2,1,0:T(8,128)(2,1)S(1)}, u32[]{:S(2)}, u32[]{:S(2)}) %collective-permute-start.32) | collective-permute-done | bytes 1048608 | tf_op jit(solution)/shard_map/ppermute | solution.py:20
  217.1 9.9 %collective-permute-done.36.refs_4_ = bf16[1,128,2048]{2,1,0:T(8,128)(2,1)S(1)} collective-permute-done((bf16[1,128,2048]{2,1,0:T(8,128)(2,1)}, bf16[1,128,2048]{2,1,0:T(8,128)(2,1)S(1)}, u32[]{:S(2)}, u32[]{:S(2)}) %collective-permute-start.36) | collective-permute-done | bytes 524320 | tf_op jit(solution)/shard_map/ppermute | solution.py:20
  227.0 10.1 %collective-permute-done.34.refs_2_ = bf16[1,128,2048]{2,1,0:T(8,128)(2,1)S(1)} collective-permute-done((bf16[1,128,2048]{2,1,0:T(8,128)(2,1)S(1)}, bf16[1,128,2048]{2,1,0:T(8,128)(2,1)S(1)}, u32[]{:S(2)}, u32[]{:S(2)}) %collective-permute-start.34) | collective-permute-done | bytes 524320 | tf_op jit(solution)/shard_map/ppermute | solution.py:20
  250.1 10.8 %collective-permute-done.47.refs_12_ = bf16[128,2048]{1,0:T(8,128)(2,1)S(1)} collective-permute-done((bf16[128,2048]{1,0:T(8,128)(2,1)S(1)}, bf16[128,2048]{1,0:T(8,128)(2,1)S(1)}, u32[]{:S(2)}, u32[]{:S(2)}) %collective-permute-start.47) | collective-permute-done | bytes 524320 | tf_op jit(solution)/shard_map/ppermute | solution.py:20
  263.0 9.1 %collective-permute-done.40.refs_4_ = bf16[128,2048]{1,0:T(8,128)(2,1)S(1)} collective-permute-done((bf16[128,2048]{1,0:T(8,128)(2,1)S(1)}, bf16[128,2048]{1,0:T(8,128)(2,1)S(1)}, u32[]{:S(2)}, u32[]{:S(2)}) %collective-permute-start.40) | collective-permute-done | bytes 524320 | tf_op jit(solution)/shard_map/ppermute | solution.py:20
  284.6 20.0 %shard_map.187 = (bf16[16,128,1024]{2,1,0:T(8,128)(2,1)}, bf16[16,128,512]{2,1,0:T(8,128)(2,1)}) custom-call(bf16[128,2048]{1,0:T(8,128)(2,1)} %get-tuple-element.154.refs_3_.refs_0_, bf16[128,2048]{1,0:T(8,128)(2,1)} %copy-done.79, bf16[128,2048]{1,0:T(8,128)(2,1)} %copy-done.78, bf16[128,2048]{1,0:T(8,128)(2,1)} %copy-done.85, ...), custom_call_target="tpu_custom_call" | custom-call | flops 12884901888 | bytes 16777216 | tf_op jit(solution)/shard_map/pallas_call | solution.py:209
  304.6 13.7 %shard_map.188.refs_17_ = bf16[8,1536,256]{2,1,0:T(8,128)(2,1)} custom-call(bf16[128,2048]{1,0:T(8,128)(2,1)} %get-tuple-element.154.refs_3_.refs_0_, bf16[128,2048]{1,0:T(8,128)(2,1)} %copy-done.79, bf16[128,2048]{1,0:T(8,128)(2,1)} %copy-done.78, bf16[128,2048]{1,0:T(8,128)(2,1)} %copy-done.85, bf16[128,2048]{1,0:T(8,128)(2,1)} %copy-done.77, ...), custom_call_target="tpu_custom_call" | custom-call | flops 8589934592 | bytes 8388608 | tf_op jit(solution)/shard_map/pallas_call | solution.py:209
  318.3 8.9 %shard_map.189.refs_2_ = bf16[8,1536,256]{2,1,0:T(8,128)(2,1)} custom-call(bf16[128,2048]{1,0:T(8,128)(2,1)} %get-tuple-element.131.refs_3_.refs_16_.refs_0_.refs_1_, bf16[128,2048]{1,0:T(8,128)(2,1)} %copy-done.13, bf16[128,2048]{1,0:T(8,128)(2,1)} %get-tuple-element.138.refs_12_.refs_5_.refs_18_.refs_2_, ...), custom_call_target="tpu_custom_call", output_to_operand_aliasing={{}: (17, {})} | custom-call | flops 4294967296 | bytes 8388608 | tf_op jit(solution)/shard_map/pallas_call | solution.py:209
  327.3 11.9 %reduce-scatter.5.cloned.1.call-start = ((), (), s32[]{:S(2)}) async-start(), calls=%async_computation.6 | async-start | bytes 7864320 | tf_op jit(solution)/shard_map/reduce_scatter | solution.py:111
  339.2 14.6 %shard_map.190.refs_33_.refs_2_ = f32[2048,2048]{1,0:T(8,128)} custom-call(bf16[16,128,1024]{2,1,0:T(8,128)(2,1)} %get-tuple-element.158.refs_17_.refs_0_, bf16[2048,1536]{1,0:T(8,128)(2,1)} %bitcast.65, bf16[8,1536,256]{2,1,0:T(8,128)(2,1)} %shard_map.189.refs_2_), custom_call_target="tpu_custom_call" | custom-call | flops 8589934592 | bytes 16777216 | tf_op jit(solution)/shard_map/pallas_call | solution.py:209
  353.8 8.1 %all-gather.8.cloned.1.call-done = bf16[2,1024,1536]{2,1,0:T(8,128)(2,1)} async-done(((bf16[2,256,1536]{2,1,0:T(8,128)(2,1)}), bf16[2,1024,1536]{2,1,0:T(8,128)(2,1)}) %all-gather.8.cloned.1.call-update) | async-done | bytes 6291472 | tf_op jit(solution)/shard_map/all_gather | solution.py:87
  361.9 19.9 %shard_map.191 = (bf16[16,128,1024]{2,1,0:T(8,128)(2,1)}, bf16[16,128,512]{2,1,0:T(8,128)(2,1)}) custom-call(bf16[128,2048]{1,0:T(8,128)(2,1)} %get-tuple-element.154.refs_3_.refs_0_, bf16[128,2048]{1,0:T(8,128)(2,1)} %copy-done.79, bf16[128,2048]{1,0:T(8,128)(2,1)} %copy-done.78, bf16[128,2048]{1,0:T(8,128)(2,1)} %copy-done.85, ...), custom_call_target="tpu_custom_call" | custom-call | flops 12884901888 | bytes 16777216 | tf_op jit(solution)/shard_map/pallas_call | solution.py:209
  381.8 10.4 %shard_map.192 = (bf16[4,128,2048]{2,1,0:T(8,128)(2,1)}, bf16[4,128,2048]{2,1,0:T(8,128)(2,1)}) custom-call(bf16[16,128,1024]{2,1,0:T(8,128)(2,1)} %get-tuple-element.160.refs_0_, bf16[2048,1536]{1,0:T(8,128)(2,1)} %bitcast.60, f32[2048,2048]{1,0:T(8,128)} %shard_map.190.refs_33_.refs_2_), custom_call_target="tpu_custom_call" | custom-call | flops 4294967296 | bytes 8388608 | tf_op jit(solution)/shard_map/pallas_call | solution.py:209
  392.2 10.4 %shard_map.193 = (bf16[4,128,2048]{2,1,0:T(8,128)(2,1)}, bf16[4,128,2048]{2,1,0:T(8,128)(2,1)}) custom-call(bf16[16,128,1024]{2,1,0:T(8,128)(2,1)} %get-tuple-element.160.refs_0_, bf16[2048,1536]{1,0:T(8,128)(2,1)} %bitcast.61, f32[2048,2048]{1,0:T(8,128)} %shard_map.190.refs_33_.refs_2_, bf16[4,128,2048]{2,1,0:T(8,128)(2,1)} %get-tuple-element.161.refs_3_.refs_0_), custom_call_target="tpu_custom_call" | custom-call | flops 4294967296 | bytes 8388608 | tf_op jit(solution)/shard_map/pallas_call | solution.py:209
  417.7 13.8 %shard_map.196.refs_2_.refs_17_ = bf16[8,1536,256]{2,1,0:T(8,128)(2,1)} custom-call(bf16[128,2048]{1,0:T(8,128)(2,1)} %get-tuple-element.154.refs_3_.refs_0_, bf16[128,2048]{1,0:T(8,128)(2,1)} %copy-done.79, bf16[128,2048]{1,0:T(8,128)(2,1)} %copy-done.78, bf16[128,2048]{1,0:T(8,128)(2,1)} %copy-done.85, bf16[128,2048]{1,0:T(8,128)(2,1)} %copy-done.77, ...), custom_call_target="tpu_custom_call" | custom-call | flops 8589934592 | bytes 8388608 | tf_op jit(solution)/shard_map/pallas_call | solution.py:209
  446.1 9.1 %shard_map.199.refs_8_ = bf16[8,1536,256]{2,1,0:T(8,128)(2,1)} custom-call(bf16[128,2048]{1,0:T(8,128)(2,1)} %get-tuple-element.131.refs_3_.refs_16_.refs_0_.refs_1_, bf16[128,2048]{1,0:T(8,128)(2,1)} %copy-done.13, bf16[128,2048]{1,0:T(8,128)(2,1)} %get-tuple-element.138.refs_12_.refs_5_.refs_18_.refs_2_, ...), custom_call_target="tpu_custom_call", output_to_operand_aliasing={{}: (17, {})} | custom-call | flops 4294967296 | bytes 8388608 | tf_op jit(solution)/shard_map/pallas_call | solution.py:209
  458.1 10.7 %collective-permute-done.57.refs_7_ = bf16[1,128,2048]{2,1,0:T(8,128)(2,1)S(1)} collective-permute-done((bf16[1,128,2048]{2,1,0:T(8,128)(2,1)S(1)}, bf16[1,128,2048]{2,1,0:T(8,128)(2,1)S(1)}, u32[]{:S(2)}, u32[]{:S(2)}) %collective-permute-start.57) | collective-permute-done | bytes 524320 | tf_op jit(solution)/shard_map/ppermute | solution.py:20
  479.3 12.1 %shard_map.201 = (bf16[4,128,2048]{2,1,0:T(8,128)(2,1)}, bf16[4,128,2048]{2,1,0:T(8,128)(2,1)}) custom-call(bf16[16,128,512]{2,1,0:T(8,128)(2,1)} %get-tuple-element.157.refs_0_, bf16[16,128,512]{2,1,0:T(8,128)(2,1)} %get-tuple-element.159.refs_1_, bf16[2048,1536]{1,0:T(8,128)(2,1)} %bitcast.66, bf16[2048,1536]{1,0:T(8,128)(2,1)} %bitcast.62, ...), custom_call_target="tpu_custom_call" | custom-call | flops 4294967296 | bytes 8388608 | tf_op jit(solution)/shard_map/pallas_call | solution.py:209
  500.4 11.2 %shard_map.203 = (bf16[4,128,2048]{2,1,0:T(8,128)(2,1)}, bf16[4,128,2048]{2,1,0:T(8,128)(2,1)}) custom-call(bf16[16,128,512]{2,1,0:T(8,128)(2,1)} %get-tuple-element.157.refs_0_, bf16[16,128,512]{2,1,0:T(8,128)(2,1)} %get-tuple-element.159.refs_1_, bf16[2048,1536]{1,0:T(8,128)(2,1)} %bitcast.67, bf16[2048,1536]{1,0:T(8,128)(2,1)} %bitcast.63, ...), custom_call_target="tpu_custom_call" | custom-call | flops 4294967296 | bytes 8388608 | tf_op jit(solution)/shard_map/pallas_call | solution.py:209
  517.5 9.1 %collective-permute-done.67.refs_7_.refs_22_ = bf16[128,2048]{1,0:T(8,128)(2,1)} collective-permute-done((bf16[128,2048]{1,0:T(8,128)(2,1)S(1)}, bf16[128,2048]{1,0:T(8,128)(2,1)}, u32[]{:S(2)}, u32[]{:S(2)}) %collective-permute-start.67) | collective-permute-done | bytes 524320 | tf_op jit(solution)/shard_map/ppermute | solution.py:20
  544.3 14.7 %shard_map.206 = (bf16[4,128,2048]{2,1,0:T(8,128)(2,1)}, bf16[4,128,2048]{2,1,0:T(8,128)(2,1)}, bf16[2,512,512]{2,1,0:T(8,128)(2,1)}) custom-call(s32[3]{0:T(128)} %pad_add_fusion.refs_0_, bf16[128,2048]{1,0:T(8,128)(2,1)} %get-tuple-element.174.refs_4_.refs_1_.refs_16_, bf16[128,2048]{1,0:T(8,128)(2,1)} %copy-done.57, ...), custom_call_target="tpu_custom_call" | custom-call | flops 4831838208 | bytes 11534336 | tf_op jit(solution)/shard_map/pallas_call | solution.py:209
  560.0 14.9 %shard_map.207 = (bf16[4,128,2048]{2,1,0:T(8,128)(2,1)}, bf16[4,128,2048]{2,1,0:T(8,128)(2,1)}, bf16[2,512,512]{2,1,0:T(8,128)(2,1)}) custom-call(s32[3]{0:T(128)} %pad_add_fusion.2.refs_0_, bf16[128,2048]{1,0:T(8,128)(2,1)} %get-tuple-element.177.refs_1_.refs_24_, bf16[128,2048]{1,0:T(8,128)(2,1)} %copy-done.60, ...), custom_call_target="tpu_custom_call" | custom-call | flops 4831838208 | bytes 11534336 | tf_op jit(solution)/shard_map/pallas_call | solution.py:209
  576.0 12.5 %shard_map.208.refs_2_ = bf16[8,768,256]{2,1,0:T(8,128)(2,1)} custom-call(bf16[128,2048]{1,0:T(8,128)(2,1)} %get-tuple-element.119.refs_3_.refs_1_.refs_0_, bf16[128,2048]{1,0:T(8,128)(2,1)} %copy-done.53, bf16[128,2048]{1,0:T(8,128)(2,1)} %get-tuple-element.127.refs_2_.refs_3_, bf16[128,2048]{1,0:T(8,128)(2,1)} %copy-done.55, ...), custom_call_target="tpu_custom_call" | custom-call | flops 6442450944 | bytes 16777216 | tf_op jit(solution)/shard_map/pallas_call | solution.py:209
  630.3 10.0 %collective-permute-done.86.refs_1_ = bf16[2,128,2048]{2,1,0:T(8,128)(2,1)S(1)} collective-permute-done((bf16[2,128,2048]{2,1,0:T(8,128)(2,1)}, bf16[2,128,2048]{2,1,0:T(8,128)(2,1)S(1)}, u32[]{:S(2)}, u32[]{:S(2)}) %collective-permute-start.86) | collective-permute-done | bytes 1048608 | tf_op jit(solution)/shard_map/ppermute | solution.py:20
  (439 shorter events, 327.9 us)
Async XLA Ops:
  7.2 116.8 %all-gather.4.cloned.1.call-start = ((), (), s32[]{:S(2)}) async-start(), calls=%async_computation.2 | async-start | bytes 3932160 | tf_op jit(solution)/shard_map/all_gather | solution.py:87
  26.0 258.6 %all-gather.6.cloned.1.call-start = ((), (), s32[]{:S(2)}) async-start(), calls=%async_computation.3 | async-start | bytes 7864320 | tf_op jit(solution)/shard_map/all_gather | solution.py:87
  55.7 33.0 %collective-permute-start.12 = (bf16[256,1536]{1,0:T(8,128)(2,1)}, bf16[256,1536]{1,0:T(8,128)(2,1)S(1)}, u32[]{:S(2)}, u32[]{:S(2)}) collective-permute-start(bf16[256,1536]{1,0:T(8,128)(2,1)} %get-tuple-element.130), channel_id=1, source_target_pairs={{0,16},{16,0},{1,17},{17,1},{2,18},{18,2},{3,19},{19,3},{4,20},{20... | collective-permute-start | bytes 2359304 | tf_op jit(solution)/shard_map/ppermute | solution.py:20
  57.7 26.8 %collective-permute-start.8 = (bf16[128,2048]{1,0:T(8,128)(2,1)S(1)}, bf16[128,2048]{1,0:T(8,128)(2,1)S(1)}, u32[]{:S(2)}, u32[]{:S(2)}) collective-permute-start(bf16[128,2048]{1,0:T(8,128)(2,1)S(1)} %copy-done.24), channel_id=1, source_target_pairs={{0,16},{16,0},{1,17},{17,1},{2,18},{18,2},{3,19},{19,3},{4,20},{20... | collective-permute-start | bytes 1572872 | tf_op jit(solution)/shard_map/ppermute | solution.py:20
  92.4 269.5 %all-gather.8.cloned.1.call-start = ((), (), s32[]{:S(2)}) async-start(), calls=%async_computation.4 | async-start | bytes 7864320 | tf_op jit(solution)/shard_map/all_gather | solution.py:87
  102.1 34.9 %collective-permute-start.14 = (bf16[128,2048]{1,0:T(8,128)(2,1)}, bf16[128,2048]{1,0:T(8,128)(2,1)}, u32[]{:S(2)}, u32[]{:S(2)}) collective-permute-start(bf16[128,2048]{1,0:T(8,128)(2,1)} %get-tuple-element.120.refs_1_.refs_8_), channel_id=1, source_target_pairs={{0,1},{1,0},{2,3},{3,2},{4,5},{5,4},{6,7},{7,6},{8,9},{9,8},{10,11... | collective-permute-start | bytes 1572872 | tf_op jit(solution)/shard_map/ppermute | solution.py:20
  102.1 34.1 %collective-permute-start.18 = (bf16[128,2048]{1,0:T(8,128)(2,1)S(1)}, bf16[128,2048]{1,0:T(8,128)(2,1)S(1)}, u32[]{:S(2)}, u32[]{:S(2)}) collective-permute-start(bf16[128,2048]{1,0:T(8,128)(2,1)S(1)} %copy-done), channel_id=1, source_target_pairs={{0,2},{1,3},{2,0},{3,1},{4,6},{5,7},{6,4},{7,5},{8,10},{9,11},{10,... | collective-permute-start | bytes 1572872 | tf_op jit(solution)/shard_map/ppermute | solution.py:20
  109.4 28.1 %collective-permute-start.15 = (bf16[128,2048]{1,0:T(8,128)(2,1)}, bf16[128,2048]{1,0:T(8,128)(2,1)}, u32[]{:S(2)}, u32[]{:S(2)}) collective-permute-start(bf16[128,2048]{1,0:T(8,128)(2,1)} %get-tuple-element.134.refs_3_.refs_10_), channel_id=1, source_target_pairs={{0,1},{1,0},{2,3},{3,2},{4,5},{5,4},{6,7},{7,6},{8,9},{9,8},{10,11... | collective-permute-start | bytes 1572872 | tf_op jit(solution)/shard_map/ppermute | solution.py:20
  111.4 26.1 %collective-permute-start.16 = (bf16[128,2048]{1,0:T(8,128)(2,1)}, bf16[128,2048]{1,0:T(8,128)(2,1)}, u32[]{:S(2)}, u32[]{:S(2)}) collective-permute-start(bf16[128,2048]{1,0:T(8,128)(2,1)} %get-tuple-element.135.refs_5_.refs_12_), channel_id=1, source_target_pairs={{0,1},{1,0},{2,3},{3,2},{4,5},{5,4},{6,7},{7,6},{8,9},{9,8},{10,11... | collective-permute-start | bytes 1572872 | tf_op jit(solution)/shard_map/ppermute | solution.py:20
  137.0 35.3 %collective-permute-start.13 = (bf16[4,128,2048]{2,1,0:T(8,128)(2,1)}, bf16[4,128,2048]{2,1,0:T(8,128)(2,1)S(1)}, u32[]{:S(2)}, u32[]{:S(2)}) collective-permute-start(bf16[4,128,2048]{2,1,0:T(8,128)(2,1)} %get-tuple-element.133), channel_id=1, source_target_pairs={{0,1},{1,0},{2,3},{3,2},{4,5},{5,4},{6,7},{7,6},{8,9},{9,8},{10,11... | collective-permute-start | bytes 6291464 | tf_op jit(solution)/shard_map/ppermute | solution.py:20
  150.0 29.4 %collective-permute-start.33 = (bf16[4,128,2048]{2,1,0:T(8,128)(2,1)}, bf16[4,128,2048]{2,1,0:T(8,128)(2,1)}, u32[]{:S(2)}, u32[]{:S(2)}) collective-permute-start(bf16[4,128,2048]{2,1,0:T(8,128)(2,1)} %get-tuple-element.145), channel_id=1, source_target_pairs={{0,1},{1,0},{2,3},{3,2},{4,5},{5,4},{6,7},{7,6},{8,9},{9,8},{10,11... | collective-permute-start | bytes 6291464 | tf_op jit(solution)/shard_map/ppermute | solution.py:20
  183.9 26.3 %collective-permute-start.35 = (bf16[2,128,2048]{2,1,0:T(8,128)(2,1)}, bf16[2,128,2048]{2,1,0:T(8,128)(2,1)S(1)}, u32[]{:S(2)}, u32[]{:S(2)}) collective-permute-start(bf16[2,128,2048]{2,1,0:T(8,128)(2,1)} %get-tuple-element.150), channel_id=1, source_target_pairs={{0,16},{16,0},{1,17},{17,1},{2,18},{18,2},{3,19},{19,3},{4,20},{20... | collective-permute-start | bytes 3145736 | tf_op jit(solution)/shard_map/ppermute | solution.py:20
  188.6 53.7 %collective-permute-start.51 = (bf16[256,1536]{1,0:T(8,128)(2,1)}, bf16[256,1536]{1,0:T(8,128)(2,1)S(1)}, u32[]{:S(2)}, u32[]{:S(2)}) collective-permute-start(bf16[256,1536]{1,0:T(8,128)(2,1)} %get-tuple-element.156), channel_id=1, source_target_pairs={{0,16},{16,0},{1,17},{17,1},{2,18},{18,2},{3,19},{19,3},{4,20},{20... | collective-permute-start | bytes 2359304 | tf_op jit(solution)/shard_map/ppermute | solution.py:20
  245.9 286.1 %reduce-scatter.3.cloned.1.call-start = ((), (), s32[]{:S(2)}) async-start(), calls=%async_computation.5 | async-start | bytes 7864320 | tf_op jit(solution)/shard_map/reduce_scatter | solution.py:111
  327.3 323.9 %reduce-scatter.5.cloned.1.call-start = ((), (), s32[]{:S(2)}) async-start(), calls=%async_computation.6 | async-start | bytes 7864320 | tf_op jit(solution)/shard_map/reduce_scatter | solution.py:111
  491.5 39.9 %collective-permute-start.58 = (bf16[4,128,2048]{2,1,0:T(8,128)(2,1)}, bf16[4,128,2048]{2,1,0:T(8,128)(2,1)S(1)}, u32[]{:S(2)}, u32[]{:S(2)}) collective-permute-start(bf16[4,128,2048]{2,1,0:T(8,128)(2,1)} %get-tuple-element.176), channel_id=1, source_target_pairs={{0,1},{1,0},{2,3},{3,2},{4,5},{5,4},{6,7},{7,6},{8,9},{9,8},{10,11... | collective-permute-start | bytes 6291464 | tf_op jit(solution)/shard_map/ppermute | solution.py:20
  526.6 32.3 %collective-permute-start.69 = (bf16[128,2048]{1,0:T(8,128)(2,1)}, bf16[128,2048]{1,0:T(8,128)(2,1)S(1)}, u32[]{:S(2)}, u32[]{:S(2)}) collective-permute-start(bf16[128,2048]{1,0:T(8,128)(2,1)} %get-tuple-element.177.refs_1_.refs_24_), channel_id=1, source_target_pairs={{0,1},{1,0},{2,3},{3,2},{4,5},{5,4},{6,7},{7,6},{8,9},{9,8},{10,11... | collective-permute-start | bytes 1572872 | tf_op jit(solution)/shard_map/ppermute | solution.py:20
  531.4 28.6 %collective-permute-start.70 = (bf16[128,2048]{1,0:T(8,128)(2,1)}, bf16[128,2048]{1,0:T(8,128)(2,1)}, u32[]{:S(2)}, u32[]{:S(2)}) collective-permute-start(bf16[128,2048]{1,0:T(8,128)(2,1)} %get-tuple-element.183.refs_3_.refs_26_), channel_id=1, source_target_pairs={{0,1},{1,0},{2,3},{3,2},{4,5},{5,4},{6,7},{7,6},{8,9},{9,8},{10,11... | collective-permute-start | bytes 1572872 | tf_op jit(solution)/shard_map/ppermute | solution.py:20
  531.4 28.5 %collective-permute-start.71 = (bf16[128,2048]{1,0:T(8,128)(2,1)}, bf16[128,2048]{1,0:T(8,128)(2,1)}, u32[]{:S(2)}, u32[]{:S(2)}) collective-permute-start(bf16[128,2048]{1,0:T(8,128)(2,1)} %get-tuple-element.184.refs_5_.refs_28_), channel_id=1, source_target_pairs={{0,1},{1,0},{2,3},{3,2},{4,5},{5,4},{6,7},{7,6},{8,9},{9,8},{10,11... | collective-permute-start | bytes 1572872 | tf_op jit(solution)/shard_map/ppermute | solution.py:20
  531.9 28.0 %collective-permute-start.73 = (bf16[128,2048]{1,0:T(8,128)(2,1)}, bf16[128,2048]{1,0:T(8,128)(2,1)}, u32[]{:S(2)}, u32[]{:S(2)}) collective-permute-start(bf16[128,2048]{1,0:T(8,128)(2,1)} %collective-permute-done.72.refs_7_.refs_30_), channel_id=1, source_target_pairs={{0,1},{1,0},{2,3},{3,2},{4,5},{5,4},{6,7},{7,6},{8,9},{9,8},{10,11... | collective-permute-start | bytes 1572872 | tf_op jit(solution)/shard_map/ppermute | solution.py:20
  543.7 31.5 %collective-permute-start.75 = (bf16[1536,256]{1,0:T(8,128)(2,1)}, bf16[1536,256]{1,0:T(8,128)(2,1)S(1)}, u32[]{:S(2)}, u32[]{:S(2)}) collective-permute-start(bf16[1536,256]{1,0:T(8,128)(2,1)} %dynamic-slice_bitcast_fusion.3), channel_id=1, source_target_pairs={{0,16},{16,0},{1,17},{17,1},{2,18},{18,2},{3,19},{19,3},{4,20},{20... | collective-permute-start | bytes 2359304 | tf_op jit(solution)/shard_map/ppermute | solution.py:20
  559.8 35.4 %collective-permute-start.79 = (bf16[4,128,2048]{2,1,0:T(8,128)(2,1)}, bf16[4,128,2048]{2,1,0:T(8,128)(2,1)S(1)}, u32[]{:S(2)}, u32[]{:S(2)}) collective-permute-start(bf16[4,128,2048]{2,1,0:T(8,128)(2,1)} %get-tuple-element.200), channel_id=1, source_target_pairs={{0,1},{1,0},{2,3},{3,2},{4,5},{5,4},{6,7},{7,6},{8,9},{9,8},{10,11... | collective-permute-start | bytes 6291464 | tf_op jit(solution)/shard_map/ppermute | solution.py:20
  574.9 26.2 %collective-permute-start.78 = (bf16[4,128,2048]{2,1,0:T(8,128)(2,1)}, bf16[4,128,2048]{2,1,0:T(8,128)(2,1)}, u32[]{:S(2)}, u32[]{:S(2)}) collective-permute-start(bf16[4,128,2048]{2,1,0:T(8,128)(2,1)} %get-tuple-element.199), channel_id=1, source_target_pairs={{0,1},{1,0},{2,3},{3,2},{4,5},{5,4},{6,7},{7,6},{8,9},{9,8},{10,11... | collective-permute-start | bytes 6291464 | tf_op jit(solution)/shard_map/ppermute | solution.py:20
  591.6 26.4 %collective-permute-start.63 = (bf16[2,128,2048]{2,1,0:T(8,128)(2,1)}, bf16[2,128,2048]{2,1,0:T(8,128)(2,1)}, u32[]{:S(2)}, u32[]{:S(2)}) collective-permute-start(bf16[2,128,2048]{2,1,0:T(8,128)(2,1)} %get-tuple-element.181), channel_id=1, source_target_pairs={{0,2},{1,3},{2,0},{3,1},{4,6},{5,7},{6,4},{7,5},{8,10},{9,11},{10,... | collective-permute-start | bytes 3145736 | tf_op jit(solution)/shard_map/ppermute | solution.py:20
  595.2 30.5 %collective-permute-start.81 = (bf16[2,128,2048]{2,1,0:T(8,128)(2,1)}, bf16[2,128,2048]{2,1,0:T(8,128)(2,1)}, u32[]{:S(2)}, u32[]{:S(2)}) collective-permute-start(bf16[2,128,2048]{2,1,0:T(8,128)(2,1)} %get-tuple-element.206), channel_id=1, source_target_pairs={{0,16},{16,0},{1,17},{17,1},{2,18},{18,2},{3,19},{19,3},{4,20},{20... | collective-permute-start | bytes 3145736 | tf_op jit(solution)/shard_map/ppermute | solution.py:20
  601.1 39.2 %collective-permute-start.86 = (bf16[2,128,2048]{2,1,0:T(8,128)(2,1)}, bf16[2,128,2048]{2,1,0:T(8,128)(2,1)S(1)}, u32[]{:S(2)}, u32[]{:S(2)}) collective-permute-start(bf16[2,128,2048]{2,1,0:T(8,128)(2,1)} %get-tuple-element.211), channel_id=1, source_target_pairs={{0,2},{1,3},{2,0},{3,1},{4,6},{5,7},{6,4},{7,5},{8,10},{9,11},{10,... | collective-permute-start | bytes 3145736 | tf_op jit(solution)/shard_map/ppermute | solution.py:20
  607.3 39.0 %collective-permute-start.85 = (bf16[2,128,2048]{2,1,0:T(8,128)(2,1)}, bf16[2,128,2048]{2,1,0:T(8,128)(2,1)S(1)}, u32[]{:S(2)}, u32[]{:S(2)}) collective-permute-start(bf16[2,128,2048]{2,1,0:T(8,128)(2,1)} %get-tuple-element.210), channel_id=1, source_target_pairs={{0,16},{16,0},{1,17},{17,1},{2,18},{18,2},{3,19},{19,3},{4,20},{20... | collective-permute-start | bytes 3145736 | tf_op jit(solution)/shard_map/ppermute | solution.py:20
  615.3 38.6 %collective-permute-start.84 = (bf16[2,768,256]{2,1,0:T(8,128)(2,1)}, bf16[2,768,256]{2,1,0:T(8,128)(2,1)S(1)}, u32[]{:S(2)}, u32[]{:S(2)}) collective-permute-start(bf16[2,768,256]{2,1,0:T(8,128)(2,1)} %get-tuple-element.209), channel_id=1, source_target_pairs={{8,4},{12,8},{9,5},{13,9},{10,6},{14,10},{11,7},{15,11},{24,20},{2... | collective-permute-start | bytes 2359304 | tf_op jit(solution)/shard_map/ppermute | solution.py:133
  618.0 35.9 %collective-permute-start.83 = (bf16[2,768,256]{2,1,0:T(8,128)(2,1)}, bf16[2,768,256]{2,1,0:T(8,128)(2,1)}, u32[]{:S(2)}, u32[]{:S(2)}) collective-permute-start(bf16[2,768,256]{2,1,0:T(8,128)(2,1)} %get-tuple-element.203.refs_2_), channel_id=1, source_target_pairs={{0,4},{4,8},{1,5},{5,9},{2,6},{6,10},{3,7},{7,11},{16,20},{20,24},... | collective-permute-start | bytes 2359304 | tf_op jit(solution)/shard_map/ppermute | solution.py:132
  629.5 34.6 %collective-permute-start.82 = (bf16[1,128,2048]{2,1,0:T(8,128)(2,1)}, bf16[1,128,2048]{2,1,0:T(8,128)(2,1)S(1)}, u32[]{:S(2)}, u32[]{:S(2)}) collective-permute-start(bf16[1,128,2048]{2,1,0:T(8,128)(2,1)} %get-tuple-element.208), channel_id=1, source_target_pairs={{0,2},{1,3},{2,0},{3,1},{4,6},{5,7},{6,4},{7,5},{8,10},{9,11},{10,... | collective-permute-start | bytes 1572872 | tf_op jit(solution)/shard_map/ppermute | solution.py:20
  658.2 30.1 %collective-permute-start.91 = (bf16[2,768,256]{2,1,0:T(8,128)(2,1)}, bf16[2,768,256]{2,1,0:T(8,128)(2,1)S(1)}, u32[]{:S(2)}, u32[]{:S(2)}) collective-permute-start(bf16[2,768,256]{2,1,0:T(8,128)(2,1)} %get-tuple-element.219), channel_id=1, source_target_pairs={{4,0},{8,4},{12,8},{5,1},{9,5},{13,9},{6,2},{10,6},{14,10},{7,3},{... | collective-permute-start | bytes 2359304 | tf_op jit(solution)/shard_map/ppermute | solution.py:133
  659.5 28.8 %collective-permute-start.90 = (bf16[2,768,256]{2,1,0:T(8,128)(2,1)}, bf16[2,768,256]{2,1,0:T(8,128)(2,1)S(1)}, u32[]{:S(2)}, u32[]{:S(2)}) collective-permute-start(bf16[2,768,256]{2,1,0:T(8,128)(2,1)} %get-tuple-element.214.refs_6_), channel_id=1, source_target_pairs={{0,4},{4,8},{8,12},{1,5},{5,9},{9,13},{2,6},{6,10},{10,14},{3,7},{... | collective-permute-start | bytes 2359304 | tf_op jit(solution)/shard_map/ppermute | solution.py:132
  (163 other events, 1521.1 us)
Sparse Core Ops, SparseCore 0:
  26.1 64.9 all-gather.3
  92.6 115.4 all-gather.5
  246.1 115.7 all-gather.7
  364.0 108.9 reduce-scatter.2
  475.2 111.2 reduce-scatter.4

commit v3 on v2

--- a/solution.py
+++ b/solution.py
@@ -11,6 +11,8 @@
 THETA = 1000000.0
 NEGATIVE = -1e30
 CHUNKS = 2
+LARGE = int(63.5 * 2**20)
+SMALL = int(63.5 * 2**20)
 BF = jnp.bfloat16
 F32 = jnp.float32
 
@@ -26,55 +28,80 @@
     )
 
 
-def start_gather(owns):
-    return [(own, xchg(own, "col", 2), xchg(own, "dp", 1)) for own in owns]
-
-
-def cross(started):
-    return [
-        (*blocks, xchg(blocks[1], "dp", 1) if stream % 2 else xchg(blocks[2], "col", 2))
-        for stream, blocks in enumerate(started)
-    ]
-
-
-def both_cores(crossed):
-    return [
-        [item for block in blocks for item in (block, xchg(block, "col", 1))] for blocks in crossed
-    ]
-
-
-def end_gather(started):
-    return both_cores(cross(started))
-
-
-def fenced(started, order):
-    came = len(started[0]) - 1
-    values = order.fence(*[value for blocks in started for value in blocks[1:]])
-    return [(blocks[0], *values[came * m : came * (m + 1)]) for m, blocks in enumerate(started)]
-
-
-def scatter_core(halves):
-    return [xchg(send, "col", 1) for _, send in halves]
-
-
-def scatter_first(halves, came, order):
-    parts = []
-    for stream, (keep, _) in enumerate(halves):
-        kept, sent = fold(keep, came[stream], (0, 1) if stream % 2 else (0, 2), order)
-        parts.append((kept, xchg(sent, "dp", 1) if stream % 2 else xchg(sent, "col", 2)))
-    return parts
-
-
-def scatter_second(parts, order):
-    terms = []
-    for stream, (keep, came) in enumerate(parts):
-        kept, sent = fold(keep, came, (0,), order)
-        terms.append((kept, xchg(sent, "col", 2) if stream % 2 else xchg(sent, "dp", 1)))
-    return terms
-
-
-def scatter_tokens(halves, order):
-    return scatter_second(scatter_first(halves, scatter_core(halves), order), order)
+def add(left, right):
+    return left.astype(F32) + right.astype(F32)
+
+
+class Gather:
+    def __init__(self, own, rows, shared):
+        self.own, self.rows, self.shared = own, rows, shared
+        self.came = [xchg(own, "col", 2), xchg(own, "dp", 1), xchg(own, "col", 1)]
+
+    def cross(self, order):
+        over_x, over_y, core = order.fence(*self.came)
+        if self.shared:
+            first, second = halved(over_y, over_x, order)
+            diagonal = [xchg(first, "col", 2), xchg(second, "dp", 1)]
+        else:
+            diagonal = [xchg(over_y, "col", 2)]
+        self.arrays = [self.own, core, over_x, over_y]
+        self.came = [xchg(over_x, "col", 1), xchg(over_y, "col", 1)] + diagonal
+
+    def fence(self, order, *others):
+        values = order.fence(*self.came, *others)
+        self.came = values[: len(self.came)]
+        return values[len(self.came) :]
+
+    def blocks(self, order, *others):
+        own, core, over_x, over_y = self.arrays
+        core_x, core_y, *diagonal = self.came
+        values = order.fence(*[xchg(item, "col", 1) for item in diagonal], *others)
+        other, others = values[: len(diagonal)], values[len(diagonal) :]
+        each = self.own.shape[0] // self.rows // len(diagonal)
+        streams = []
+        for m in range(each * len(diagonal)):
+            found = [(item, m) for item in (own, core, over_x, core_x, over_y, core_y)]
+            which, place = divmod(m, each)
+            streams.append(found + [(diagonal[which], place), (other[which], place)])
+        return (streams, *others)
+
+
+class Scatter:
+    def __init__(self, *payloads):
+        shape = (2, 2) + payloads[0][0][0].shape[1:]
+        self.parts = [
+            [[keep.reshape(shape), came.reshape(shape)] for keep, came in parts]
+            for parts in payloads
+        ]
+        self.came = [[], []]
+
+    def send(self, picks, axes, order):
+        count = len(self.parts)
+        sums = [
+            [(item, *pick) for item in parts[m]]
+            + [(item, (1, *pick[0]), (p, *pick[1])) for item in self.came[m]]
+            for m, pick in enumerate(picks)
+            for p, parts in enumerate(self.parts)
+        ]
+        sent = folded([sums[:count], sums[count:]], order)
+        for m, (axis, bit) in enumerate(axes):
+            self.came[m].append(xchg(sent[m], axis, bit))
+
+    def first(self, order):
+        self.send((((2, 1), (0, 1)), ((1, 2), (1, 0))), (("col", 2), ("dp", 1)), order)
+
+    def second(self, order):
+        self.send((((1, 1), (1, 0)), ((1, 1), (0, 1))), (("dp", 1), ("col", 2)), order)
+
+    def terms(self):
+        return [
+            [
+                [(item, (1, 1), (0, 0)) for item in parts[m]]
+                + [(item, (1, 1, 1), (p, 0, 0)) for item in self.came[m]]
+                for m in range(2)
+            ]
+            for p, parts in enumerate(self.parts)
+        ]
 
 
 def dp_groups():
@@ -82,8 +109,8 @@
     return [[i for i in range(size) if i % 2 == low] for low in (0, 1)]
 
 
-def gather_weight(mine, sent, low, order):
-    pair = paired(mine, xchg(sent, "dp", 1), low, order)
+def gather_weight(mine, came, low, order):
+    pair = paired(mine, came, low, order)
     full = lax.all_gather(pair, "row", axis=1, tiled=True)
     if lax.axis_size("dp") > 2:
         full = lax.all_gather(full, "dp", axis=0, tiled=True, axis_index_groups=dp_groups())
@@ -152,6 +179,7 @@
 
         count = 2 if far else 1
         outs = order.call(
+            "advance",
             kernel,
             (2,),
             [part, part, picked(0), picked(1)],
@@ -187,6 +215,7 @@
 
     def fence(self, *values):
         return self.call(
+            "fence",
             lambda *refs: None,
             (1,),
             [pl.BlockSpec(memory_space=pl.ANY)] * len(values),
@@ -197,7 +226,7 @@
         )
 
     def call(
-        self, kernel, grid, in_specs, out_specs, out_shape, args, scratch=(), flops=0, moved=0, prefetch=0, aliases=None
+        self, name, kernel, grid, in_specs, out_specs, out_shape, args, scratch=(), flops=0, moved=0, prefetch=0, aliases=None, large=False
     ):
         last = [token for token in self.last if all(token is not arg for arg in args)]
         tokens = len(last)
@@ -216,8 +245,9 @@
                 scratch_shapes=list(scratch),
             ),
             out_shape=out_shape,
+            name=name,
             input_output_aliases=aliases or {},
-            compiler_params=pltpu.CompilerParams(vmem_limit_bytes=56 * 2**20),
+            compiler_params=pltpu.CompilerParams(vmem_limit_bytes=LARGE if large else SMALL),
             cost_estimate=pl.CostEstimate(flops=flops, bytes_accessed=moved, transcendentals=0),
         )(*args, *last)
         self.last = (outs[0] if isinstance(outs, (list, tuple)) else outs,)
@@ -226,6 +256,15 @@
 
 def shaped(*shape, dtype=BF):
     return jax.ShapeDtypeStruct(shape, dtype)
+
+
+def block_spec(block, shape, index):
+    _, place = block
+    return pl.BlockSpec(shape, lambda *at: (place * index(*at)[1] + index(*at)[0], index(*at)[2]))
+
+
+def arrays(blocks):
+    return [item for item, _ in blocks]
 
 
 def whole(shape):
@@ -248,6 +287,7 @@
     d = wqkv.shape[0]
     out = shaped(d, wqkv.shape[1] // 2 + wo.shape[0] // 2)
     return order.call(
+        "prepare_attn",
         prepare_attn_kernel,
         (1,),
         [SCALARS] + [whole(item.shape) for item in (wqkv, wo, gain)],
@@ -272,6 +312,7 @@
 def prepare_ffn(chunks, cut, low, w1, w3, w2, gain, order):
     out = shaped(w1.shape[0], 3 * cut)
     outs = order.call(
+        "prepare_ffn",
         lambda *refs: prepare_ffn_kernel(chunks, cut, *refs),
         (1,),
         [SCALARS] + [whole(item.shape) for item in (w1, w3, w2, gain)],
@@ -291,6 +332,7 @@
 def paired(mine, came, low, order):
     out = shaped(2, *mine.shape)
     return order.call(
+        "paired",
         paired_kernel,
         (1,),
         [SCALARS, whole(mine.shape), whole(mine.shape)],
@@ -305,93 +347,112 @@
     return lax.rsqrt(jnp.mean(values * values, axis=-1, keepdims=True) + EPS)
 
 
-def by_rows(kernel, ins, outs, order, scalars=None):
+def by_rows(kernel, ins, outs, order, scalars=None, steps=4):
     def spec(item):
-        lead = item.shape[:-2]
-        block = lead + (item.shape[-2] // 4, item.shape[-1])
-        return pl.BlockSpec(block, lambda l: (0,) * len(lead) + (l, 0))
+        item, lead, at = item if isinstance(item, tuple) else (item, item.shape[:-2], None)
+        at = at or (0,) * len(lead)
+        return pl.BlockSpec(lead + (item.shape[-2] // steps, item.shape[-1]), lambda l: at + (l, 0))
 
     extra = [] if scalars is None else [scalars]
-    return order.call(
+    args = [item[0] if isinstance(item, tuple) else item for item in ins]
+    return order.call(
+        "by_rows",
         kernel,
-        (4,),
+        (steps,),
         [SCALARS] * len(extra) + [spec(item) for item in ins],
         [spec(item) for item in outs],
         outs,
-        (*extra, *ins),
-        moved=4 * sum(item.size for item in (*ins, *outs)),
+        (*extra, *args),
+        moved=4 * sum(item.size for item in (*args, *outs)),
     )
 
 
 def first_norm(inputs, order):
-    def kernel(in_ref, *out_refs):
-        for m, ref in enumerate(out_refs):
-            values = in_ref[m].astype(F32)
-            ref[...] = (values * inverse_rms(values)).astype(BF)
-
-    return by_rows(kernel, [inputs], [shaped(*inputs.shape[1:])] * inputs.shape[0], order)
-
-
-def masked(cotangent, scalars, order):
-    def kernel(scalar_ref, in_ref, *out_refs):
-        for m, ref in enumerate(out_refs):
-            rows = ref.shape[0]
-            place = scalar_ref[0] + pl.program_id(0) * rows
-            places = place + lax.broadcasted_iota(jnp.int32, ref.shape, 0)
+    def kernel(in_ref, out_ref):
+        values = in_ref[...].astype(F32)
+        out_ref[...] = (values * inverse_rms(values)).astype(BF)
+
+    return by_rows(kernel, [inputs], [shaped(*inputs.shape)], order)[0]
+
+
+def halved(first, second, order):
+    half, width = first.shape[0] // 2, first.shape[1]
+
+    def kernel(*refs):
+        for ref, out_ref in zip(refs[:2], refs[2:]):
+            out_ref[...] = ref[...]
+
+    part = (half // 4, width)
+    out = pl.BlockSpec(part, lambda l: (l, 0))
+    return order.call(
+        "halved",
+        kernel,
+        (4,),
+        [out, pl.BlockSpec(part, lambda l: (4 + l, 0))],
+        [out] * 2,
+        [shaped(half, width)] * 2,
+        (first, second),
+        moved=8 * half * width,
+    )
+
+
+def total_of(refs):
+    values = [ref[...].astype(F32) for ref in refs]
+    return sum(value.reshape(value.shape[-2:]) for value in values)
+
+
+def folded(groups, order):
+    counts = [[len(items) for items in lists] for lists in groups]
+    total = sum(sum(sizes) for sizes in counts)
+
+    def kernel(*refs):
+        start = 0
+        for out_ref, sizes in zip(refs[total:], counts):
+            for p, size in enumerate(sizes):
+                values = [ref[...].astype(F32) for ref in refs[start : start + size]]
+                shape = out_ref.shape[1:]
+                out_ref[p] = sum(value.reshape(shape) for value in values).astype(BF)
+                start += size
+
+    outs = [shaped(len(lists), *lists[0][0][1], *lists[0][0][0].shape[-2:]) for lists in groups]
+    ins = [item for lists in groups for items in lists for item in items]
+    return by_rows(kernel, ins, outs, order, steps=2)
+
+
+def with_terms(kernel, ins, outs, terms, order):
+    count = len(ins)
+    sizes = [len(items) for items in terms]
+
+    def run(*refs):
+        start = count
+        for m, size in enumerate(sizes):
+            total = total_of(refs[start : start + size])
+            kernel(m, total, refs[:count], refs[count + sum(sizes) :])
+            start += size
+
+    return by_rows(run, [*ins, *[item for items in terms for item in items]], outs, order)
+
+
+def second_norm(inputs, terms, cotangent, scalars, order):
+    micro = inputs.shape[0]
+    count = sum(len(items) for items in terms)
+
+    def kernel(scalar_ref, in_ref, cot_ref, *refs):
+        out_ref, residual_ref = refs[count:]
+        start = 0
+        for m, items in enumerate(terms):
+            values = in_ref[m].astype(F32) + total_of(refs[start : start + len(items)])
+            start += len(items)
+            residual_ref[m] = values
+            out_ref[m] = (values * inverse_rms(values)).astype(BF)
+            first = scalar_ref[0] + pl.program_id(0) * in_ref.shape[1]
+            places = first + lax.broadcasted_iota(jnp.int32, in_ref.shape[1:], 0)
             valid = places < scalar_ref[1 + m]
-            ref[...] = jnp.where(valid, in_ref[m].astype(F32), 0.0).astype(BF)
-
-    return by_rows(kernel, [cotangent], [shaped(*cotangent.shape[1:])] * cotangent.shape[0], order, scalars)
-
-
-def fold(keep, came, kept, order):
-    others = [i for i in range(keep.shape[0]) if i not in kept]
-    shape = (len(kept),) + keep.shape[1:]
-
-    def kernel(keep_ref, came_ref, kept_ref, sent_ref):
-        for at, (mine, other) in enumerate(zip(kept, others)):
-            sent_ref[at] = add(keep_ref[other], came_ref[other]).astype(BF)
-            kept_ref[at] = add(keep_ref[mine], came_ref[mine])
-
-    return by_rows(kernel, [keep, came], [shaped(*shape, dtype=F32), shaped(*shape)], order)
-
-
-def add(left, right):
-    return left.astype(F32) + right.astype(F32)
-
-
-def total_of(refs):
-    return add(refs[0][0], refs[1][0])
-
-
-def second_norm(inputs, terms, order):
-    micro = inputs.shape[0]
-
-    def kernel(in_ref, *refs):
-        for m in range(micro):
-            values = in_ref[m].astype(F32) + total_of(refs[2 * m : 2 * m + 2])
-            refs[2 * micro + m][...] = (values * inverse_rms(values)).astype(BF)
-            refs[3 * micro + m][...] = values
-
-    shape = inputs.shape[1:]
-    outs = by_rows(
-        kernel,
-        [inputs] + [item for pair in terms for item in pair],
-        [shaped(*shape)] * micro + [shaped(*shape, dtype=F32)] * micro,
-        order,
-    )
-    return outs[:micro], outs[micro:]
-
-
-def finished(residual, terms, order):
-    micro = len(residual)
-
-    def kernel(*refs):
-        for m in range(micro):
-            refs[-1][m] = (refs[3 * m][...] + total_of(refs[3 * m + 1 : 3 * m + 3])).astype(BF)
-
-    ins = [item for m in range(micro) for item in (residual[m], *terms[m])]
-    return by_rows(kernel, ins, [shaped(micro, *residual[0].shape)], order)[0]
+            out_ref[micro + m] = jnp.where(valid, cot_ref[m].astype(F32), 0.0).astype(BF)
+
+    outs = [shaped(2 * micro, *inputs.shape[1:]), shaped(*inputs.shape, dtype=F32)]
+    ins = [inputs, cotangent, *[item for items in terms for item in items]]
+    return by_rows(kernel, ins, outs, order, scalars)
 
 
 def norm_back(values, scaled):
@@ -401,39 +462,33 @@
 
 
 def second_norm_back(residual, upstream, terms, order):
-    micro = len(residual)
-
-    def kernel(*refs):
-        outs = refs[4 * micro :]
+    def kernel(m, total, ins, outs):
+        grad = ins[1][m].astype(F32) + norm_back(ins[0][m], total)
+        outs[0][m] = grad.astype(BF)
+        outs[1][m] = grad
+
+    outs = [shaped(*residual.shape), shaped(*residual.shape, dtype=F32)]
+    return with_terms(kernel, [residual, upstream], outs, terms, order)
+
+
+def finished(inputs, upstream, residual, terms, order):
+    micro = inputs.shape[0]
+    sizes = [[len(items) for items in payload] for payload in terms]
+
+    def kernel(in_ref, up_ref, residual_ref, *refs):
+        grad_ref, out_ref = refs[-2:]
+        start = 0
         for m in range(micro):
-            residual_ref, upstream_ref = refs[4 * m : 4 * m + 2]
-            grad = upstream_ref[...].astype(F32) + norm_back(
-                residual_ref[...], total_of(refs[4 * m + 2 : 4 * m + 4])
-            )
-            outs[m][...] = grad.astype(BF)
-            outs[micro + m][...] = grad
-
-    ins = [item for m in range(micro) for item in (residual[m], upstream[m], *terms[m])]
-    shape = residual[0].shape
-    outs = by_rows(
-        kernel, ins, [shaped(*shape)] * micro + [shaped(*shape, dtype=F32)] * micro, order
-    )
-    return outs[:micro], outs[micro:]
-
-
-def first_norm_back(inputs, upstream, terms, order):
-    micro = inputs.shape[0]
-
-    def kernel(in_ref, *refs):
+            total = total_of(refs[start : start + sizes[0][m]])
+            start += sizes[0][m]
+            grad_ref[m] = (up_ref[m] + norm_back(in_ref[m].astype(F32), total)).astype(BF)
         for m in range(micro):
-            upstream_ref = refs[3 * m]
-            grad = upstream_ref[...] + norm_back(
-                in_ref[m].astype(F32), total_of(refs[3 * m + 1 : 3 * m + 3])
-            )
-            refs[-1][m] = grad.astype(BF)
-
-    ins = [inputs] + [item for m in range(micro) for item in (upstream[m], *terms[m])]
-    return by_rows(kernel, ins, [shaped(*inputs.shape)], order)[0]
+            total = total_of(refs[start : start + sizes[1][m]])
+            start += sizes[1][m]
+            out_ref[m] = (residual_ref[m] + total).astype(BF)
+
+    ins = [inputs, upstream, residual] + [item for payload in terms for items in payload for item in items]
+    return by_rows(kernel, ins, [shaped(*inputs.shape)] * 2, order)
 
 
 def head_probs(query, keys, me, length, rows):
@@ -492,22 +547,26 @@
         put_blocks(dot(a_ref[y], w_ref[:, groups * span :], 1, 1), y, cols // 2, keep_ref, send_ref)
 
 
-def attend(blocks, scalars, cosine, sine, weights, groups, order):
+def attend(blocks, rows, scalars, cosine, sine, weights, groups, order):
     count = len(blocks)
-    rows, width = blocks[0].shape
+    width = blocks[0][0].shape[1]
     places = count // 2 * rows
     head = groups * HEAD_SIZE
     sizes = (QUERY_PER_GROUP * head, head, head, QUERY_PER_GROUP * head)
     outs = [(count // 2, rows, width)] * 2 + [(2, places, size) for size in sizes]
     return order.call(
+        "attend",
         lambda *refs: attend_kernel(count, groups, *refs),
         (1,),
-        [SCALARS] + [whole(item.shape) for item in (*blocks, cosine, sine, weights)],
+        [SCALARS]
+        + [block_spec(block, (rows, width), lambda _: (0, 1, 0)) for block in blocks]
+        + [whole(item.shape) for item in (cosine, sine, weights)],
         [whole(shape) for shape in outs],
         [jax.ShapeDtypeStruct(shape, BF) for shape in outs],
         flops=4 * places * weights.size + 16 * places * places * QUERY_PER_GROUP * head,
         moved=8 * places * width + 2 * weights.size,
-        args=(scalars, *blocks, cosine, sine, weights,),
+        args=(scalars, *arrays(blocks), cosine, sine, weights),
+        large=True,
     )
 
 
@@ -542,21 +601,25 @@
         put_blocks(dot(grad_proj, w_ref[:, : groups * span], 1, 1), y, cols // 2, keep_ref, send_ref)
 
 
-def attend_back(pieces, scalars, cosine, sine, weights, saved, groups, order):
+def attend_back(pieces, rows, scalars, cosine, sine, weights, saved, groups, order):
     count = len(pieces)
-    rows, width = pieces[0].shape
+    width = pieces[0][0].shape[1]
     places = count // 2 * rows
     span = groups * (QUERY_PER_GROUP + 2) * HEAD_SIZE
     outs = [(count // 2, rows, width)] * 2 + [(2, places, span)]
     return order.call(
+        "attend_back",
         lambda *refs: attend_back_kernel(count, groups, *refs),
         (1,),
-        [SCALARS] + [whole(item.shape) for item in (*pieces, cosine, sine, weights, *saved)],
+        [SCALARS]
+        + [block_spec(block, (rows, width), lambda _: (0, 1, 0)) for block in pieces]
+        + [whole(item.shape) for item in (cosine, sine, weights, *saved)],
         [whole(shape) for shape in outs],
         [jax.ShapeDtypeStruct(shape, BF) for shape in outs],
         flops=4 * places * weights.size + 48 * places * places * groups * HEAD_SIZE,
         moved=8 * places * width + 2 * weights.size,
-        args=(scalars, *pieces, cosine, sine, weights, *saved,),
+        args=(scalars, *arrays(pieces), cosine, sine, weights, *saved),
+        large=True,
     )
 
 
@@ -575,21 +638,23 @@
     pair_ref[..., cut:] = (hidden_grad * swish).astype(BF).reshape(hidden_ref.shape)
 
 
-def units(rows, pieces, weights, order):
+def units(rows, pieces, places, weights, order):
     count = len(rows)
-    places, width = rows[0].shape
+    width = weights.shape[0]
     cut = weights.shape[1] // 3
     part = places // 4
-    block = pl.BlockSpec((part, width), lambda l: (l, 0))
-    return order.call(
+    return order.call(
+        "units",
         lambda *refs: units_kernel(count, cut, *refs),
         (4,),
-        [block] * (2 * count) + [whole(weights.shape)],
+        [block_spec(block, (part, width), lambda l: (l, 4, 0)) for block in (*rows, *pieces)]
+        + [whole(weights.shape)],
         [pl.BlockSpec((count, part, size), lambda l: (0, l, 0)) for size in (2 * cut, cut)],
         [shaped(count, places, size) for size in (2 * cut, cut)],
         flops=2 * count * places * weights.size,
         moved=4 * count * places * width,
-        args=(*rows, *pieces, weights),
+        args=(*arrays(rows), *arrays(pieces), weights),
+        large=True,
     )
 
 
@@ -608,21 +673,22 @@
         at += product.shape[0]
 
 
-def weight_grads(products, owners, order, total=None, into=None):
+def weight_grads(products, places, owners, order, total=None, into=None):
     rows = [block for blocks, _ in products for block in blocks]
     lefts = [left for _, items in products for left in items]
     counts = [(len(blocks), len(items)) for blocks, items in products]
-    places, width = rows[0].shape
+    width = rows[0][0].shape[1]
     tile = width // 4
     part = sum(items[0].shape[1] for _, items in products)
     total = total or part
     at = 0 if into is None else total // part - 1
     tokens = len(products[0][0]) * places
-    args = (*rows, *lefts) + (() if into is None else (into,))
-    return order.call(
+    args = (*arrays(rows), *lefts) + (() if into is None else (into,))
+    return order.call(
+        "weight_grads",
         lambda *refs: grads_kernel(counts, *refs),
         (4,),
-        [pl.BlockSpec((places, tile), lambda t: (0, t))] * len(rows)
+        [block_spec(block, (places, tile), lambda t: (0, 1, t)) for block in rows]
         + [whole(left.shape) for left in lefts]
         + [pl.BlockSpec(memory_space=pl.ANY)] * (into is not None),
         pl.BlockSpec((owners // 4, part, width // owners), lambda t: (t, at, 0)),
@@ -631,17 +697,17 @@
         moved=2 * len(products) * tokens * width,
         args=args,
         aliases={} if into is None else {len(args) - 1: 0},
-    )
-
-
-def back_kernel(count, lo, split, added, *refs):
+        large=True,
+    )
+
+
+def back_kernel(count, split, added, *refs):
     lefts, weights = refs[:count], refs[count : 2 * count]
     refs = refs[2 * count :]
     total = refs[0][...] if added else None
     refs = refs[1:] if added else refs
     for left, weight in zip(lefts, weights):
-        value = left[...].reshape(-1, left.shape[-1])
-        product = dot(value, weight[:, lo : lo + value.shape[1]], 1, 1)
+        product = dot(left[...].reshape(-1, left.shape[-1]), weight[...], 1, 1)
         total = product if total is None else total + product
     if split:
         put_blocks(total, 0, refs[0].shape[0], *refs)
@@ -659,16 +725,18 @@
     halves = shaped(4, places, width)
     steps = 2 if split else count // 4
     return order.call(
-        lambda *refs: back_kernel(len(lefts), lo, split, added, *refs),
+        "back",
+        lambda *refs: back_kernel(len(lefts), split, added, *refs),
         (steps,),
         [pl.BlockSpec((4, places, depth), lambda t: (first + t, 0, 0))] * len(lefts)
-        + [whole(weights[0].shape)] * len(weights)
+        + [pl.BlockSpec((width, depth), lambda t: (0, lo // depth))] * len(weights)
         + ([flat] if added else []),
         [half, half] if split else flat,
         [halves, halves] if split else shaped(count * places, width, dtype=F32),
         flops=8 * steps * places * depth * width * len(lefts),
         moved=16 * steps * places * width,
         args=(*lefts, *weights, *((before,) if added else ())),
+        large=True,
     )
 
 
@@ -702,6 +770,7 @@
     args = [pair for pair, _ in parts] + [came for _, came in parts] + [w1, w3, gain]
     outs = [shaped(*shape, dtype=F32) for shape in (w1.shape, w3.shape, w2.shape, gain.shape[::-1])]
     return order.call(
+        "finish_ffn",
         lambda *refs: finish_ffn_kernel(count, parts[0][1].shape[0] // 3, *refs),
         (1,),
         [SCALARS] + [whole(item.shape) for item in args],
@@ -709,6 +778,7 @@
         outs,
         (low, *args),
         moved=24 * w1.size,
+        large=True,
     )
 
 
@@ -730,6 +800,7 @@
     args = [*part, wqkv, gain]
     outs = [shaped(*shape, dtype=F32) for shape in (wqkv.shape, wo.shape, gain.shape[::-1])]
     return order.call(
+        "finish_attn",
         finish_attn_kernel,
         (1,),
         [SCALARS] + [whole(item.shape) for item in args],
@@ -758,17 +829,6 @@
     def prepared(*chunks):
         return prepare_ffn(chunks, cut, low, w1, w3, w2, ffn_gain, order)
 
-    mine, sent = prepare_attn(low, wqkv, wo, attn_gain, order)
-    normed1 = first_norm(inputs, order)
-    attn_w = gather_weight(mine, sent, low, order)
-    attn_rows = cross(fenced(start_gather(normed1), order))
-    ffn_parts = prepared(0)
-    attn_rows = both_cores(fenced(attn_rows, order))
-    own_scalars = jnp.concatenate(((me * rows).astype(jnp.int32)[None], lengths.reshape(micro)))
-    upstream = masked(cotangent, own_scalars, order)
-    pieces = start_gather(upstream)
-    ffn_ws = [gather_weight(*ffn_parts[0], low, order)]
-
     positions = (
         (jnp.arange(cols, dtype=jnp.int32) ^ me)[:, None] * rows
         + jnp.arange(rows, dtype=jnp.int32)[None, :]
@@ -778,38 +838,51 @@
     scalars = [
         jnp.concatenate((me.astype(jnp.int32)[None], lengths[m], other_lengths[m])) for m in streams
     ]
+    own_scalars = jnp.concatenate(((me * rows).astype(jnp.int32)[None], lengths.reshape(micro)))
+
+    mine, sent = prepare_attn(low, wqkv, wo, attn_gain, order)
+    normed1 = first_norm(inputs, order)
+    attn_w = gather_weight(mine, xchg(sent, "dp", 1), low, order)
+    attn_gather = Gather(normed1.reshape(-1, width), rows, False)
+    attn_gather.cross(order)
+    ((mine, sent),) = prepared(0)
+    order.wait(cosine, sine, *scalars)
+    (came,) = attn_gather.fence(order, xchg(sent, "dp", 1))
+    ffn_ws = [gather_weight(mine, came, low, order)]
+    (attn_rows,) = attn_gather.blocks(order)
+    ((mine, sent),) = prepared(1)
 
     def run_attend(m):
-        return attend(attn_rows[m], scalars[m], cosine, sine, attn_w, groups, order)
-
-    ahead = [run_attend(0)]
-    pieces = end_gather(fenced(pieces, order))
-    ahead.append(run_attend(1))
-    order.wait(*sum(pieces, []))
-    halves = [item[:2] for item in ahead]
-    terms = scatter_first(halves, scatter_core(halves), order)
-    ffn_parts += prepared(1)
-    terms = scatter_second(terms, order)
-    normed2, residual = second_norm(inputs, terms, order)
-    ffn_rows = start_gather(normed2)
-    ffn_ws += [gather_weight(*ffn_parts[1], low, order)]
-    ffn_rows = end_gather(ffn_rows)
-    all_rows, all_pieces = sum(ffn_rows, []), sum(pieces, [])
+        return attend(attn_rows[m], rows, scalars[m], cosine, sine, attn_w, groups, order)
+
+    ahead = [run_attend(0), run_attend(1)]
+    came, *sends = order.fence(xchg(sent, "dp", 1), *[item[1] for item in ahead])
+    scatter = Scatter([(item[0], xchg(send, "col", 1)) for item, send in zip(ahead, sends)])
+    ffn_ws.append(gather_weight(mine, came, low, order))
+    scatter.first(order)
+    scatter.second(order)
+    normed2, residual = second_norm(inputs, scatter.terms()[0], cotangent, own_scalars, order)
+    ffn_gather = Gather(normed2.reshape(-1, width), rows, True)
+    ffn_gather.cross(order)
+    ffn_gather.fence(order)
+    (blocks,) = ffn_gather.blocks(order)
+    all_rows, all_pieces = sum(blocks[:micro], []), sum(blocks[micro:], [])
+    upstream = (normed2, (micro,), (1,))
 
     pairs, hiddens = [], []
 
     def run_units(chunk):
-        pair, hidden = units(all_rows, all_pieces, ffn_ws[chunk], order)
+        pair, hidden = units(all_rows, all_pieces, rows, ffn_ws[chunk], order)
         pairs.append(pair)
         hiddens.append(hidden)
 
     def pair_grads(chunk):
         left = pairs[chunk].reshape(-1, 2 * cut)
-        return weight_grads([(all_rows, [left])], owners, order, total=3 * cut)
+        return weight_grads([(all_rows, [left])], rows, owners, order, total=3 * cut)
 
     def hidden_grads(chunk, into):
         left = hiddens[chunk].reshape(-1, cut)
-        return weight_grads([(all_pieces, [left])], owners, order, total=3 * cut, into=into)
+        return weight_grads([(all_pieces, [left])], rows, owners, order, total=3 * cut, into=into)
 
     run_units(0)
     ffn_grads = [scatter_weight(hidden_grads(0, pair_grads(0)))]
@@ -818,44 +891,54 @@
     halves = [
         back(pairs[1:], ffn_ws[1:], 0, order, before=early, stream=m) for m in streams
     ]
-    terms = scatter_first(halves, scatter_core(halves), order)
+    scatter = Scatter([(keep, xchg(send, "col", 1)) for keep, send in halves])
+    scatter.first(order)
     part = pair_grads(1)
-    terms = scatter_second(terms, order)
-    ffn_grads.append(scatter_weight(hidden_grads(1, part)))
-    attn_up, residual_grad = second_norm_back(residual, upstream, terms, order)
-    attn_pieces = start_gather(attn_up)
+    scatter.second(order)
+    grads = hidden_grads(1, part)
+    attn_up, residual_grad = second_norm_back(residual, upstream, scatter.terms()[0], order)
+    attn_gather = Gather(attn_up.reshape(-1, width), rows, True)
+    ffn_grads.append(scatter_weight(order.fence(grads)[0]))
     halves = [back(hiddens, ffn_ws, 2 * cut, order, stream=0)]
-    attn_pieces = end_gather(fenced(attn_pieces, order))
+    attn_gather.cross(order)
     halves.append(back(hiddens, ffn_ws, 2 * cut, order, stream=1))
-    terms = scatter_first(halves, scatter_core(halves), order)
-
-    keep, send, grad_proj = zip(
-        *[
-            attend_back(attn_pieces[m], scalars[m], cosine, sine, attn_w, ahead[m][2:5], groups, order)
-            for m in streams
-        ]
-    )
-    halves = list(zip(keep, send))
-    came = scatter_core(halves)
-    order.wait(ffn_grads[0][1])
+    attn_gather.fence(order)
+    attn_pieces, *sends = attn_gather.blocks(order, *[send for _, send in halves])
+    halves = [(keep, send) for (keep, _), send in zip(halves, sends)]
+
+    def run_back(m):
+        return attend_back(
+            attn_pieces[m], rows, scalars[m], cosine, sine, attn_w, ahead[m][2:5], groups, order
+        )
+
+    def arrived(part):
+        return part[0], order.fence(part[1])[0]
+
+    out_sent = [(keep, xchg(send, "col", 1)) for keep, send in halves]
+    behind = [run_back(0), run_back(1)]
+    pair, came = ffn_grads[0]
+    came, *values = order.fence(came, *[item for _, item in out_sent], *[item[1] for item in behind])
+    ffn_grads[0] = (pair, came)
+    out_parts = [(keep, item) for (keep, _), item in zip(out_sent, values)]
+    attn_parts = [(item[0], xchg(send, "col", 1)) for item, send in zip(behind, values[micro:])]
+    scatter = Scatter(attn_parts, out_parts)
+    scatter.first(order)
     attn_grads = weight_grads(
         [
-            (sum(attn_rows, []), [grad_proj[m].reshape(2 * places, -1) for m in streams]),
-            (sum(attn_pieces, []), [ahead[m][5].reshape(2 * places, -1) for m in streams]),
+            (sum(attn_rows, []), [item[2].reshape(2 * places, -1) for item in behind]),
+            (sum(attn_pieces, []), [item[5].reshape(2 * places, -1) for item in ahead]),
         ],
+        rows,
         owners,
         order,
     )
     chain = Chain(attn_grads)
-    last_terms = scatter_first(halves, came, order)
     chain.advance(order)
-    terms = scatter_second(terms, order)
-    last_terms = scatter_second(last_terms, order)
+    scatter.second(order)
     chain.advance(order)
-    order.wait(ffn_grads[1][1])
-    result = finished(residual, terms, order)
-    source_grad = first_norm_back(inputs, residual_grad, last_terms, order)
+    ffn_grads[1] = arrived(ffn_grads[1])
     attn_part = chain.advance(order)
+    source_grad, result = finished(inputs, residual_grad, residual, scatter.terms(), order)
     w1_grad, w3_grad, w2_grad, ffn_sum = finish_ffn(low, ffn_grads, w1, w3, w2, ffn_gain, order)
     ffn_sum = sum_over_col(ffn_sum)[0]
     wqkv_grad, wo_grad, attn_sum = finish_attn(low, attn_part, wqkv, wo, attn_gain, order)

time: 733 us -> 663 us (0.905); the launches traced: 720 us -> 658 us
  Pallas kernels: 340 us -> 291 us
  waiting for transfers between devices: 230 us -> 268 us
  starting transfers between devices: 88 us -> 62.9 us
  local copies, waits for them, and re-layouts: 37 us -> 12.6 us
    pallas_call x53 -> x52, Pallas kernels: 340 us -> 291 us  [call(): pl.pallas_call(run, grid_spec=pltpu.PrefetchScalarGridSpec(num_scalar_pre...]
    ppermute x3, waiting for transfers between devices: 2.53 us -> 32.3 us  [send(): lax.ppermute(up, 'row', [(i, i + 1) for i in range(self.step)])]
    unnamed x182 -> x12, local copies, waits for them, and re-layouts: 26.6 us -> 2.43 us
    ppermute x93 -> x58, starting transfers between devices: 62.6 us -> 43.4 us  [xchg(): return lax.ppermute(value, axis, [(i, i ^ bit) for i in range(size)])]
    reduce_scatter x2, starting transfers between devices: 12 us -> 0.73 us  [scatter_weight(): lax.psum_scatter(grad, 'row', scatter_dimension=1, tiled=True)]
    ppermute x3, waiting for transfers between devices: 0.01 us -> 10.5 us  [send(): lax.ppermute(down, 'row', [(i, i - 1) for i in range(far, self.rows)])]
    ppermute x93 -> x58, waiting for transfers between devices: 219 us -> 219 us  [xchg(): return lax.ppermute(value, axis, [(i, i ^ bit) for i in range(size)])]
  transfers between devices with their start and end apart: 104 -> 69, of which waited for: 48 -> 42; matrix products, arithmetic and copies ran while one was open for 2% -> 3% of each run, Pallas kernels for 46% -> 44%
where the time goes in v3:
time: 663 us; the launch traced here: 658 us
  Pallas kernels  291 us (44%)
  waiting for transfers between devices  268 us (40%)
  starting transfers between devices  62.9 us (9%)
  between operations  14.3 us (2%)
  local copies, waits for them, and re-layouts  12.6 us (2%)
  other arithmetic  10.1 us (2%)
    pallas_call x52, Pallas kernels, call(): pl.pallas_call(run, grid_spec=pltpu.PrefetchScalarGridSpec(num_scalar_pre...  291 us
    ppermute x58, waiting for transfers between devices, xchg(): return lax.ppermute(value, axis, [(i, i ^ bit) for i in range(size)])  219 us
    ppermute x58, starting transfers between devices, xchg(): return lax.ppermute(value, axis, [(i, i ^ bit) for i in range(size)])  43.4 us
    ppermute x3, waiting for transfers between devices, send(): lax.ppermute(up, 'row', [(i, i + 1) for i in range(self.step)])  32.3 us
    ppermute x3, starting transfers between devices, send(): lax.ppermute(up, 'row', [(i, i + 1) for i in range(self.step)])  14.8 us
  transfers between devices with their start and end apart: 69, of which 42 were waited for; matrix products, arithmetic and copies ran while one was open for 3% of the time, Pallas kernels for 44%

profile of v3, /device:TPU:0, one launch (start us, length us, event | category | flops | bytes accessed | tf_op | source)
XLA Modules:
  0.0 658.5 jit_solution(2264271873992055441)
XLA Ops:
  17.5 5.7 collective-permute-done.4.refs_2_
  29.9 22.1 %collective-permute-done.2.refs_1_ = bf16[256,2048]{1,0:T(8,128)(2,1)} collective-permute-done((bf16[256,2048]{1,0:T(8,128)(2,1)}, bf16[256,2048]{1,0:T(8,128)(2,1)}, u32[]{:S(2)}, u32[]{:S(2)}) %collective-permute-start.2) | collective-permute-done | bytes 1048608 | tf_op jit(solution)/shard_map/ppermute | solution.py:22
  66.6 13.4 %collective-permute-done.8.refs_3_ = bf16[256,1536]{1,0:T(8,128)(2,1)} collective-permute-done((bf16[256,1536]{1,0:T(8,128)(2,1)}, bf16[256,1536]{1,0:T(8,128)(2,1)}, u32[]{:S(2)}, u32[]{:S(2)}) %collective-permute-start.8) | collective-permute-done | bytes 786464 | tf_op jit(solution)/shard_map/ppermute | solution.py:22
  91.1 12.1 %attend.2 = (bf16[4,128,2048]{2,1,0:T(8,128)(2,1)}, bf16[4,128,2048]{2,1,0:T(8,128)(2,1)}, bf16[2,512,256]{2,1,0:T(8,128)(2,1)}, bf16[2,512,128]{2,1,0:T(8,128)(...) custom-call(s32[3]{0:T(128)} %get-tuple-element.244.refs_7_.refs_0_, bf16[256,2048]{1,0:T(8,128)(2,1)} %bitcast.138, ...), custom_call_target="tpu_custom_call" | custom-call | flops 4294967296 | bytes 11534336 | tf_op jit(solution)/shard_map/attend/pallas_call | solution.py:238
  103.2 12.2 %attend.3 = (bf16[4,128,2048]{2,1,0:T(8,128)(2,1)}, bf16[4,128,2048]{2,1,0:T(8,128)(2,1)}, bf16[2,512,256]{2,1,0:T(8,128)(2,1)}, bf16[2,512,128]{2,1,0:T(8,128)(...) custom-call(s32[3]{0:T(128)} %get-tuple-element.245.refs_8_.refs_0_, bf16[256,2048]{1,0:T(8,128)(2,1)} %bitcast.139, ...), custom_call_target="tpu_custom_call" | custom-call | flops 4294967296 | bytes 11534336 | tf_op jit(solution)/shard_map/attend/pallas_call | solution.py:238
  129.3 22.5 %collective-permute-done.14.refs_5_.refs_9_ = bf16[1,1,2,128,2048]{4,3,2,1,0:T(8,128)(2,1)} collective-permute-done((bf16[1,1,2,128,2048]{4,3,2,1,0:T(8,128)(2,1)}, bf16[1,1,2,128,2048]{4,3,2,1,0:T(8,128)(2,1)}, u32[]{:S(2)}, u32[]{:S(2)}) %collective-permute-start.14) | collective-permute-done | bytes 1048608 | tf_op jit(solution)/shard_map/ppermute | solution.py:22
  158.4 10.5 %collective-permute-done.16.refs_10_ = bf16[1,1,1,128,2048]{4,3,2,1,0:T(8,128)(2,1)} collective-permute-done((bf16[1,1,1,128,2048]{4,3,2,1,0:T(8,128)(2,1)}, bf16[1,1,1,128,2048]{4,3,2,1,0:T(8,128)(2,1)}, u32[]{:S(2)}, u32[]{:S(2)}) %collective-permute-start.16) | collective-permute-done | bytes 524320 | tf_op jit(solution)/shard_map/ppermute | solution.py:22
  180.4 43.9 %collective-permute-done.18.refs_1_ = bf16[512,2048]{1,0:T(8,128)(2,1)} collective-permute-done((bf16[512,2048]{1,0:T(8,128)(2,1)}, bf16[512,2048]{1,0:T(8,128)(2,1)}, u32[]{:S(2)}, u32[]{:S(2)}) %collective-permute-start.18) | collective-permute-done | bytes 2097184 | tf_op jit(solution)/shard_map/ppermute | solution.py:22
  230.8 23.4 %collective-permute-done.23.refs_3_ = bf16[256,2048]{1,0:T(8,128)(2,1)} collective-permute-done((bf16[256,2048]{1,0:T(8,128)(2,1)}, bf16[256,2048]{1,0:T(8,128)(2,1)}, u32[]{:S(2)}, u32[]{:S(2)}) %collective-permute-start.23) | collective-permute-done | bytes 1048608 | tf_op jit(solution)/shard_map/ppermute | solution.py:22
  259.9 20.0 %units.2 = (bf16[16,128,1024]{2,1,0:T(8,128)(2,1)}, bf16[16,128,512]{2,1,0:T(8,128)(2,1)}) custom-call(bf16[512,2048]{1,0:T(8,128)(2,1)} %bitcast.73, bf16[512,2048]{1,0:T(8,128)(2,1)} %get-tuple-element.139.refs_1_.refs_9_.refs_17_.refs_25_, bf16[512,2048]{1,0:T(8,128)(2,1)} %get-tuple-element.140.refs_1_.refs_2_.refs_10_.refs_18_.refs_26_, ...), custom_call_target="tpu_custom_call" | custom-call | flops 12884901888 | bytes 16777216 | tf_op jit(solution)/shard_map/units/pallas_call | solution.py:238
  280.0 13.7 %weight_grads.5.refs_17_ = bf16[8,1536,256]{2,1,0:T(8,128)(2,1)} custom-call(bf16[512,2048]{1,0:T(8,128)(2,1)} %bitcast.77, bf16[512,2048]{1,0:T(8,128)(2,1)} %get-tuple-element.139.refs_1_.refs_9_.refs_17_.refs_25_, bf16[512,2048]{1,0:T(8,128)(2,1)} %get-tuple-element.140.refs_1_.refs_2_.refs_10_.refs_18_.refs_26_, ...), custom_call_target="tpu_custom_call" | custom-call | flops 8589934592 | bytes 8388608 | tf_op jit(solution)/shard_map/weight_grads/pallas_call | solution.py:238
  293.7 9.0 %weight_grads.6.refs_2_ = bf16[8,1536,256]{2,1,0:T(8,128)(2,1)} custom-call(bf16[512,2048]{1,0:T(8,128)(2,1)} %bitcast.79, bf16[512,2048]{1,0:T(8,128)(2,1)} %get-tuple-element.139.refs_1_.refs_9_.refs_17_.refs_25_, bf16[512,2048]{1,0:T(8,128)(2,1)} %get-tuple-element.140.refs_1_.refs_2_.refs_10_.refs_18_.refs_26_, ...), custom_call_target="tpu_custom_call", output_to_operand_aliasing={{}: (17, {})} | custom-call | flops 4294967296 | bytes 8388608 | tf_op jit(solution)/shard_map/weight_grads/pallas_call | solution.py:238
  302.7 14.2 %back.5.refs_33_.refs_2_ = f32[2048,2048]{1,0:T(8,128)} custom-call(bf16[16,128,1024]{2,1,0:T(8,128)(2,1)} %get-tuple-element.150.refs_17_.refs_0_, bf16[2048,1536]{1,0:T(8,128)(2,1)} %bitcast.104, bf16[8,1536,256]{2,1,0:T(8,128)(2,1)} %weight_grads.6.refs_2_), custom_call_target="tpu_custom_call" | custom-call | flops 8589934592 | bytes 16777216 | tf_op jit(solution)/shard_map/back/pallas_call | solution.py:238
  321.9 20.0 %units.3 = (bf16[16,128,1024]{2,1,0:T(8,128)(2,1)}, bf16[16,128,512]{2,1,0:T(8,128)(2,1)}) custom-call(bf16[512,2048]{1,0:T(8,128)(2,1)} %bitcast.81, bf16[512,2048]{1,0:T(8,128)(2,1)} %get-tuple-element.139.refs_1_.refs_9_.refs_17_.refs_25_, bf16[512,2048]{1,0:T(8,128)(2,1)} %get-tuple-element.140.refs_1_.refs_2_.refs_10_.refs_18_.refs_26_, ...), custom_call_target="tpu_custom_call" | custom-call | flops 12884901888 | bytes 16777216 | tf_op jit(solution)/shard_map/units/pallas_call | solution.py:238
  341.9 9.9 %back.6 = (bf16[4,128,2048]{2,1,0:T(8,128)(2,1)}, bf16[4,128,2048]{2,1,0:T(8,128)(2,1)}) custom-call(bf16[16,128,1024]{2,1,0:T(8,128)(2,1)} %get-tuple-element.152.refs_0_, bf16[2048,1536]{1,0:T(8,128)(2,1)} %bitcast.98, f32[2048,2048]{1,0:T(8,128)} %back.5.refs_33_.refs_2_), custom_call_target="tpu_custom_call" | custom-call | flops 4294967296 | bytes 8388608 | tf_op jit(solution)/shard_map/back/pallas_call | solution.py:238
  351.8 9.8 %back.7 = (bf16[4,128,2048]{2,1,0:T(8,128)(2,1)}, bf16[4,128,2048]{2,1,0:T(8,128)(2,1)}) custom-call(bf16[16,128,1024]{2,1,0:T(8,128)(2,1)} %get-tuple-element.152.refs_0_, bf16[2048,1536]{1,0:T(8,128)(2,1)} %bitcast.99, f32[2048,2048]{1,0:T(8,128)} %back.5.refs_33_.refs_2_, bf16[4,128,2048]{2,1,0:T(8,128)(2,1)} %get-tuple-element.153.refs_3_), custom_call_target="tpu_custom_call" | custom-call | flops 4294967296 | bytes 8388608 | tf_op jit(solution)/shard_map/back/pallas_call | solution.py:238
  375.4 13.6 %weight_grads.7.refs_6_.refs_17_ = bf16[8,1536,256]{2,1,0:T(8,128)(2,1)} custom-call(bf16[512,2048]{1,0:T(8,128)(2,1)} %bitcast.85, bf16[512,2048]{1,0:T(8,128)(2,1)} %get-tuple-element.139.refs_1_.refs_9_.refs_17_.refs_25_, bf16[512,2048]{1,0:T(8,128)(2,1)} %get-tuple-element.140.refs_1_.refs_2_.refs_10_.refs_18_.refs_26_, ...), custom_call_target="tpu_custom_call" | custom-call | flops 8589934592 | bytes 8388608 | tf_op jit(solution)/shard_map/weight_grads/pallas_call | solution.py:238
  389.0 9.0 %collective-permute-done.29.refs_5_.refs_8_ = bf16[1,1,2,128,2048]{4,3,2,1,0:T(8,128)(2,1)} collective-permute-done((bf16[1,1,2,128,2048]{4,3,2,1,0:T(8,128)(2,1)}, bf16[1,1,2,128,2048]{4,3,2,1,0:T(8,128)(2,1)}, u32[]{:S(2)}, u32[]{:S(2)}) %collective-permute-start.29) | collective-permute-done | bytes 1048608 | tf_op jit(solution)/shard_map/ppermute | solution.py:22
  403.9 8.9 %weight_grads.8.refs_10_.refs_0_ = bf16[8,1536,256]{2,1,0:T(8,128)(2,1)} custom-call(bf16[512,2048]{1,0:T(8,128)(2,1)} %bitcast.87, bf16[512,2048]{1,0:T(8,128)(2,1)} %get-tuple-element.139.refs_1_.refs_9_.refs_17_.refs_25_, bf16[512,2048]{1,0:T(8,128)(2,1)} %get-tuple-element.140.refs_1_.refs_2_.refs_10_.refs_18_.refs_26_, ...), custom_call_target="tpu_custom_call", output_to_operand_aliasing={{}: (17, {})} | custom-call | flops 4294967296 | bytes 8388608 | tf_op jit(solution)/shard_map/weight_grads/pallas_call | solution.py:238
  416.2 5.8 by_rows.16
  423.3 8.8 %back.8 = (bf16[4,128,2048]{2,1,0:T(8,128)(2,1)}, bf16[4,128,2048]{2,1,0:T(8,128)(2,1)}) custom-call(bf16[16,128,512]{2,1,0:T(8,128)(2,1)} %get-tuple-element.151.refs_0_, bf16[16,128,512]{2,1,0:T(8,128)(2,1)} %get-tuple-element.161.refs_1_, bf16[2048,1536]{1,0:T(8,128)(2,1)} %bitcast.105, bf16[2048,1536]{1,0:T(8,128)(2,1)} %bitcast.100, ...), custom_call_target="tpu_custom_call" | custom-call | flops 4294967296 | bytes 8388608 | tf_op jit(solution)/shard_map/back/pallas_call | solution.py:238
  432.1 15.9 %collective-permute-done.33.refs_1_ = bf16[256,2048]{1,0:T(8,128)(2,1)} collective-permute-done((bf16[256,2048]{1,0:T(8,128)(2,1)}, bf16[256,2048]{1,0:T(8,128)(2,1)}, u32[]{:S(2)}, u32[]{:S(2)}) %collective-permute-start.33) | collective-permute-done | bytes 1048608 | tf_op jit(solution)/shard_map/ppermute | solution.py:22
  454.3 9.0 %back.9 = (bf16[4,128,2048]{2,1,0:T(8,128)(2,1)}, bf16[4,128,2048]{2,1,0:T(8,128)(2,1)}) custom-call(bf16[16,128,512]{2,1,0:T(8,128)(2,1)} %get-tuple-element.151.refs_0_, bf16[16,128,512]{2,1,0:T(8,128)(2,1)} %get-tuple-element.161.refs_1_, bf16[2048,1536]{1,0:T(8,128)(2,1)} %bitcast.106, bf16[2048,1536]{1,0:T(8,128)(2,1)} %bitcast.101, ...), custom_call_target="tpu_custom_call" | custom-call | flops 4294967296 | bytes 8388608 | tf_op jit(solution)/shard_map/back/pallas_call | solution.py:238
  473.9 14.6 %attend_back.2 = (bf16[4,128,2048]{2,1,0:T(8,128)(2,1)}, bf16[4,128,2048]{2,1,0:T(8,128)(2,1)}, bf16[2,512,512]{2,1,0:T(8,128)(2,1)}) custom-call(s32[3]{0:T(128)} %get-tuple-element.244.refs_7_.refs_0_, bf16[256,2048]{1,0:T(8,128)(2,1)} %bitcast.30.refs_1_.refs_16_.refs_24_, bf16[256,2048]{1,0:T(8,128)(2,1)} %get-tuple-element.165.refs_2_.refs_17_.refs_25_, ...), custom_call_target="tpu_custom_call" | custom-call | flops 4831838208 | bytes 11534336 | tf_op jit(solution)/shard_map/attend_back/pallas_call | solution.py:238
  488.5 14.8 %attend_back.3 = (bf16[4,128,2048]{2,1,0:T(8,128)(2,1)}, bf16[4,128,2048]{2,1,0:T(8,128)(2,1)}, bf16[2,512,512]{2,1,0:T(8,128)(2,1)}) custom-call(s32[3]{0:T(128)} %get-tuple-element.245.refs_8_.refs_0_, bf16[256,2048]{1,0:T(8,128)(2,1)} %bitcast.30.refs_1_.refs_16_.refs_24_, bf16[256,2048]{1,0:T(8,128)(2,1)} %get-tuple-element.165.refs_2_.refs_17_.refs_25_, ...), custom_call_target="tpu_custom_call" | custom-call | flops 4831838208 | bytes 11534336 | tf_op jit(solution)/shard_map/attend_back/pallas_call | solution.py:238
  518.2 12.3 %weight_grads.9.refs_5_ = bf16[8,768,256]{2,1,0:T(8,128)(2,1)} custom-call(bf16[256,2048]{1,0:T(8,128)(2,1)} %bitcast.140, bf16[256,2048]{1,0:T(8,128)(2,1)} %get-tuple-element.115.refs_2_.refs_1_.refs_9_, bf16[256,2048]{1,0:T(8,128)(2,1)} %get-tuple-element.116.refs_5_.refs_3_.refs_2_.refs_10_, ...), custom_call_target="tpu_custom_call" | custom-call | flops 6442450944 | bytes 16777216 | tf_op jit(solution)/shard_map/weight_grads/pallas_call | solution.py:238
  536.4 23.6 %collective-permute-done.48.refs_1_ = bf16[2,768,256]{2,1,0:T(8,128)(2,1)} collective-permute-done((bf16[2,768,256]{2,1,0:T(8,128)(2,1)S(1)}, bf16[2,768,256]{2,1,0:T(8,128)(2,1)}, u32[]{:S(2)}, u32[]{:S(2)}) %collective-permute-start.48) | collective-permute-done | bytes 786464 | tf_op jit(solution)/shard_map/ppermute | solution.py:159
  578.7 7.6 %collective-permute-done.52.refs_1_ = bf16[2,768,256]{2,1,0:T(8,128)(2,1)} collective-permute-done((bf16[2,768,256]{2,1,0:T(8,128)(2,1)}, bf16[2,768,256]{2,1,0:T(8,128)(2,1)}, u32[]{:S(2)}, u32[]{:S(2)}) %collective-permute-start.52) | collective-permute-done | bytes 786464 | tf_op jit(solution)/shard_map/ppermute | solution.py:159
  591.1 7.5 %collective-permute-start.54 = (bf16[2,768,256]{2,1,0:T(8,128)(2,1)}, bf16[2,768,256]{2,1,0:T(8,128)(2,1)}, u32[]{:S(2)}, u32[]{:S(2)}) collective-permute-start(bf16[2,768,256]{2,1,0:T(8,128)(2,1)} %get-tuple-element.206.refs_1_), channel_id=1, source_target_pairs={{0,4},{4,8},{8,12},{1,5},{5,9},{9,13},{2,6},{6,10},{10,14},{3,7},{... | collective-permute-start | bytes 2359304 | tf_op jit(solution)/shard_map/ppermute | solution.py:159
  602.1 10.5 %collective-permute-done.55.refs_2_ = bf16[2,768,256]{2,1,0:T(8,128)(2,1)} collective-permute-done((bf16[2,768,256]{2,1,0:T(8,128)(2,1)}, bf16[2,768,256]{2,1,0:T(8,128)(2,1)}, u32[]{:S(2)}, u32[]{:S(2)}) %collective-permute-start.55) | collective-permute-done | bytes 786464 | tf_op jit(solution)/shard_map/ppermute | solution.py:160
  626.4 7.5 %by_rows.19 = (bf16[2,128,2048]{2,1,0:T(8,128)(2,1)}, bf16[2,128,2048]{2,1,0:T(8,128)(2,1)}) custom-call(bf16[2,128,2048]{2,1,0:T(8,128)(2,1)} %bitcast.144, f32[2,128,2048]{2,1,0:T(8,128)} %get-tuple-element.162.refs_1_, f32[2,128,2048]{2,1,0:T(8,128)} %get-tuple-element.137.refs_0_.refs_2_, bf16[2,2,128,2048]{3,2,1,0:T(8,128)(2,1)} %bitcast.129, ...), custom_call_target="tpu_custom_call" | custom-call | bytes 69206016 | tf_op jit(solution)/shard_map/by_rows/pallas_call | solution.py:238
  633.9 6.9 %finish_ffn.1 = (f32[256,2048]{1,0:T(8,128)}, f32[256,2048]{1,0:T(8,128)}, f32[2048,256]{1,0:T(8,128)}, f32[1,256]{1,0:T(1,128)}) custom-call(s32[1]{0:T(128)} %bitcast.7.refs_0_, bf16[2,1536,256]{2,1,0:T(8,128)(2,1)} %reduce-scatter.3.cloned.1.call-done.refs_1_, bf16[2,1536,256]{2,1,0:T(8,128)(2,1)} %reduce-scatter.5.cloned.1.call-done.refs_2_, ...), custom_call_target="tpu_custom_call" | custom-call | bytes 12582912 | tf_op jit(solution)/shard_map/finish_ffn/pallas_call | solution.py:238
  (197 shorter events, 205.6 us)
Async XLA Ops:
  7.2 83.9 %all-gather.4.cloned.1.call-start = ((), (), s32[]{:S(2)}) async-start(), calls=%async_computation.2 | async-start | bytes 3932160 | tf_op jit(solution)/shard_map/all_gather | solution.py:114
  26.0 233.9 %all-gather.8.cloned.1.call-start = ((), (), s32[]{:S(2)}) async-start(), calls=%async_computation.4 | async-start | bytes 7864320 | tf_op jit(solution)/shard_map/all_gather | solution.py:114
  26.1 25.9 %collective-permute-start.2 = (bf16[256,2048]{1,0:T(8,128)(2,1)}, bf16[256,2048]{1,0:T(8,128)(2,1)}, u32[]{:S(2)}, u32[]{:S(2)}) collective-permute-start(bf16[256,2048]{1,0:T(8,128)(2,1)} %bitcast.136), channel_id=1, source_target_pairs={{0,16},{16,0},{1,17},{17,1},{2,18},{18,2},{3,19},{19,3},{4,20},{20... | collective-permute-start | bytes 3145736 | tf_op jit(solution)/shard_map/ppermute | solution.py:22
  27.9 25.5 %collective-permute-start.1 = (bf16[256,2048]{1,0:T(8,128)(2,1)}, bf16[256,2048]{1,0:T(8,128)(2,1)}, u32[]{:S(2)}, u32[]{:S(2)}) collective-permute-start(bf16[256,2048]{1,0:T(8,128)(2,1)} %bitcast.137), channel_id=1, source_target_pairs={{0,2},{1,3},{2,0},{3,1},{4,6},{5,7},{6,4},{7,5},{8,10},{9,11},{10,... | collective-permute-start | bytes 3145736 | tf_op jit(solution)/shard_map/ppermute | solution.py:22
  29.4 33.3 %collective-permute-start = (s32[2,1]{0,1:T(1,128)S(1)}, s32[2,1]{0,1:T(1,128)S(1)}, u32[]{:S(2)}, u32[]{:S(2)}) collective-permute-start(s32[2,1]{0,1:T(1,128)S(1)} %copy-done.3), channel_id=1, source_target_pairs={{0,16},{16,0},{1,17},{17,1},{2,18},{18,2},{3,19},{19,3},{4,20},{20... | collective-permute-start | bytes 32 | tf_op jit(solution)/shard_map/ppermute | solution.py:22
  53.5 26.5 %collective-permute-start.7 = (bf16[256,2048]{1,0:T(8,128)(2,1)}, bf16[256,2048]{1,0:T(8,128)(2,1)}, u32[]{:S(2)}, u32[]{:S(2)}) collective-permute-start(bf16[256,2048]{1,0:T(8,128)(2,1)} %get-tuple-element.117.refs_5_.refs_4_.refs_12_), channel_id=1, source_target_pairs={{0,2},{1,3},{2,0},{3,1},{4,6},{5,7},{6,4},{7,5},{8,10},{9,11},{10,... | collective-permute-start | bytes 3145736 | tf_op jit(solution)/shard_map/ppermute | solution.py:22
  55.0 25.0 %collective-permute-start.6 = (bf16[256,2048]{1,0:T(8,128)(2,1)}, bf16[256,2048]{1,0:T(8,128)(2,1)}, u32[]{:S(2)}, u32[]{:S(2)}) collective-permute-start(bf16[256,2048]{1,0:T(8,128)(2,1)} %get-tuple-element.117.refs_5_.refs_4_.refs_12_), channel_id=1, source_target_pairs={{0,1},{1,0},{2,3},{3,2},{4,5},{5,4},{6,7},{7,6},{8,9},{9,8},{10,11... | collective-permute-start | bytes 3145736 | tf_op jit(solution)/shard_map/ppermute | solution.py:22
  55.0 25.0 %collective-permute-start.5 = (bf16[256,2048]{1,0:T(8,128)(2,1)}, bf16[256,2048]{1,0:T(8,128)(2,1)}, u32[]{:S(2)}, u32[]{:S(2)}) collective-permute-start(bf16[256,2048]{1,0:T(8,128)(2,1)} %get-tuple-element.116.refs_5_.refs_3_.refs_2_.refs_10_), channel_id=1, source_target_pairs={{0,1},{1,0},{2,3},{3,2},{4,5},{5,4},{6,7},{7,6},{8,9},{9,8},{10,11... | collective-permute-start | bytes 3145736 | tf_op jit(solution)/shard_map/ppermute | solution.py:22
  82.6 239.2 %all-gather.6.cloned.1.call-start = ((), (), s32[]{:S(2)}) async-start(), calls=%async_computation.3 | async-start | bytes 7864320 | tf_op jit(solution)/shard_map/all_gather | solution.py:114
  89.4 25.9 %collective-permute-start.10 = (bf16[256,1536]{1,0:T(8,128)(2,1)}, bf16[256,1536]{1,0:T(8,128)(2,1)}, u32[]{:S(2)}, u32[]{:S(2)}) collective-permute-start(bf16[256,1536]{1,0:T(8,128)(2,1)} %get-tuple-element.126), channel_id=1, source_target_pairs={{0,16},{16,0},{1,17},{17,1},{2,18},{18,2},{3,19},{19,3},{4,20},{20... | collective-permute-start | bytes 2359304 | tf_op jit(solution)/shard_map/ppermute | solution.py:22
  118.6 352.5 %reduce-scatter.3.cloned.1.call-start = ((), (), s32[]{:S(2)}) async-start(), calls=%async_computation.5 | async-start | bytes 7864320 | tf_op jit(solution)/shard_map/reduce_scatter | solution.py:138
  126.3 25.5 %collective-permute-start.14 = (bf16[1,1,2,128,2048]{4,3,2,1,0:T(8,128)(2,1)}, bf16[1,1,2,128,2048]{4,3,2,1,0:T(8,128)(2,1)}, u32[]{:S(2)}, u32[]{:S(2)}) collective-permute-start(bf16[1,1,2,128,2048]{4,3,2,1,0:T(8,128)(2,1)} %get-tuple-element.134), channel_id=1, source_target_pairs={{0,16},{16,0},{1,17},{17,1},{2,18},{18,2},{3,19},{19,3},{4,20},{20... | collective-permute-start | bytes 3145736 | tf_op jit(solution)/shard_map/ppermute | solution.py:22
  127.9 25.2 %collective-permute-start.13 = (bf16[1,2,1,128,2048]{4,3,2,1,0:T(8,128)(2,1)}, bf16[1,2,1,128,2048]{4,3,2,1,0:T(8,128)(2,1)}, u32[]{:S(2)}, u32[]{:S(2)}) collective-permute-start(bf16[1,2,1,128,2048]{4,3,2,1,0:T(8,128)(2,1)} %get-tuple-element.133.refs_6_), channel_id=1, source_target_pairs={{0,2},{1,3},{2,0},{3,1},{4,6},{5,7},{6,4},{7,5},{8,10},{9,11},{10,... | collective-permute-start | bytes 3145736 | tf_op jit(solution)/shard_map/ppermute | solution.py:22
  175.9 48.4 %collective-permute-start.18 = (bf16[512,2048]{1,0:T(8,128)(2,1)}, bf16[512,2048]{1,0:T(8,128)(2,1)}, u32[]{:S(2)}, u32[]{:S(2)}) collective-permute-start(bf16[512,2048]{1,0:T(8,128)(2,1)} %bitcast.71), channel_id=1, source_target_pairs={{0,16},{16,0},{1,17},{17,1},{2,18},{18,2},{3,19},{19,3},{4,20},{20... | collective-permute-start | bytes 6291464 | tf_op jit(solution)/shard_map/ppermute | solution.py:22
  176.6 48.0 %collective-permute-start.17 = (bf16[512,2048]{1,0:T(8,128)(2,1)}, bf16[512,2048]{1,0:T(8,128)(2,1)}, u32[]{:S(2)}, u32[]{:S(2)}) collective-permute-start(bf16[512,2048]{1,0:T(8,128)(2,1)} %bitcast.72), channel_id=1, source_target_pairs={{0,2},{1,3},{2,0},{3,1},{4,6},{5,7},{6,4},{7,5},{8,10},{9,11},{10,... | collective-permute-start | bytes 6291464 | tf_op jit(solution)/shard_map/ppermute | solution.py:22
  224.6 30.8 %collective-permute-start.20 = (bf16[512,2048]{1,0:T(8,128)(2,1)}, bf16[512,2048]{1,0:T(8,128)(2,1)}, u32[]{:S(2)}, u32[]{:S(2)}) collective-permute-start(bf16[512,2048]{1,0:T(8,128)(2,1)} %get-tuple-element.140.refs_1_.refs_2_.refs_10_.refs_18_.refs_26_), channel_id=1, source_target_pairs={{0,1},{1,0},{2,3},{3,2},{4,5},{5,4},{6,7},{7,6},{8,9},{9,8},{10,11... | collective-permute-start | bytes 6291464 | tf_op jit(solution)/shard_map/ppermute | solution.py:22
  224.6 30.8 %collective-permute-start.21 = (bf16[512,2048]{1,0:T(8,128)(2,1)}, bf16[512,2048]{1,0:T(8,128)(2,1)}, u32[]{:S(2)}, u32[]{:S(2)}) collective-permute-start(bf16[512,2048]{1,0:T(8,128)(2,1)} %get-tuple-element.141.refs_0_.refs_4_.refs_12_.refs_20_.refs_28_), channel_id=1, source_target_pairs={{0,1},{1,0},{2,3},{3,2},{4,5},{5,4},{6,7},{7,6},{8,9},{9,8},{10,11... | collective-permute-start | bytes 6291464 | tf_op jit(solution)/shard_map/ppermute | solution.py:22
  228.9 25.4 %collective-permute-start.23 = (bf16[256,2048]{1,0:T(8,128)(2,1)}, bf16[256,2048]{1,0:T(8,128)(2,1)}, u32[]{:S(2)}, u32[]{:S(2)}) collective-permute-start(bf16[256,2048]{1,0:T(8,128)(2,1)} %get-tuple-element.143), channel_id=1, source_target_pairs={{0,16},{16,0},{1,17},{17,1},{2,18},{18,2},{3,19},{19,3},{4,20},{20... | collective-permute-start | bytes 3145736 | tf_op jit(solution)/shard_map/ppermute | solution.py:22
  230.3 25.1 %collective-permute-start.22 = (bf16[256,2048]{1,0:T(8,128)(2,1)}, bf16[256,2048]{1,0:T(8,128)(2,1)}, u32[]{:S(2)}, u32[]{:S(2)}) collective-permute-start(bf16[256,2048]{1,0:T(8,128)(2,1)} %get-tuple-element.142.refs_4_), channel_id=1, source_target_pairs={{0,2},{1,3},{2,0},{3,1},{4,6},{5,7},{6,4},{7,5},{8,10},{9,11},{10,... | collective-permute-start | bytes 3145736 | tf_op jit(solution)/shard_map/ppermute | solution.py:22
  302.7 268.0 %reduce-scatter.5.cloned.1.call-start = ((), (), s32[]{:S(2)}) async-start(), calls=%async_computation.6 | async-start | bytes 7864320 | tf_op jit(solution)/shard_map/reduce_scatter | solution.py:138
  372.5 25.5 %collective-permute-start.29 = (bf16[1,1,2,128,2048]{4,3,2,1,0:T(8,128)(2,1)}, bf16[1,1,2,128,2048]{4,3,2,1,0:T(8,128)(2,1)}, u32[]{:S(2)}, u32[]{:S(2)}) collective-permute-start(bf16[1,1,2,128,2048]{4,3,2,1,0:T(8,128)(2,1)} %get-tuple-element.158), channel_id=1, source_target_pairs={{0,16},{16,0},{1,17},{17,1},{2,18},{18,2},{3,19},{19,3},{4,20},{20... | collective-permute-start | bytes 3145736 | tf_op jit(solution)/shard_map/ppermute | solution.py:22
  373.9 25.2 %collective-permute-start.28 = (bf16[1,2,1,128,2048]{4,3,2,1,0:T(8,128)(2,1)}, bf16[1,2,1,128,2048]{4,3,2,1,0:T(8,128)(2,1)}, u32[]{:S(2)}, u32[]{:S(2)}) collective-permute-start(bf16[1,2,1,128,2048]{4,3,2,1,0:T(8,128)(2,1)} %get-tuple-element.157.refs_17_), channel_id=1, source_target_pairs={{0,2},{1,3},{2,0},{3,1},{4,6},{5,7},{6,4},{7,5},{8,10},{9,11},{10,... | collective-permute-start | bytes 3145736 | tf_op jit(solution)/shard_map/ppermute | solution.py:22
  422.1 25.9 %collective-permute-start.33 = (bf16[256,2048]{1,0:T(8,128)(2,1)}, bf16[256,2048]{1,0:T(8,128)(2,1)}, u32[]{:S(2)}, u32[]{:S(2)}) collective-permute-start(bf16[256,2048]{1,0:T(8,128)(2,1)} %bitcast.30.refs_1_.refs_16_.refs_24_), channel_id=1, source_target_pairs={{0,16},{16,0},{1,17},{17,1},{2,18},{18,2},{3,19},{19,3},{4,20},{20... | collective-permute-start | bytes 3145736 | tf_op jit(solution)/shard_map/ppermute | solution.py:22
  422.9 25.5 %collective-permute-start.32 = (bf16[256,2048]{1,0:T(8,128)(2,1)}, bf16[256,2048]{1,0:T(8,128)(2,1)}, u32[]{:S(2)}, u32[]{:S(2)}) collective-permute-start(bf16[256,2048]{1,0:T(8,128)(2,1)} %bitcast.30.refs_1_.refs_16_.refs_24_), channel_id=1, source_target_pairs={{0,2},{1,3},{2,0},{3,1},{4,6},{5,7},{6,4},{7,5},{8,10},{9,11},{10,... | collective-permute-start | bytes 3145736 | tf_op jit(solution)/shard_map/ppermute | solution.py:22
  470.6 32.7 %collective-permute-start.42 = (bf16[4,128,2048]{2,1,0:T(8,128)(2,1)}, bf16[4,128,2048]{2,1,0:T(8,128)(2,1)}, u32[]{:S(2)}, u32[]{:S(2)}) collective-permute-start(bf16[4,128,2048]{2,1,0:T(8,128)(2,1)} %get-tuple-element.182), channel_id=1, source_target_pairs={{0,1},{1,0},{2,3},{3,2},{4,5},{5,4},{6,7},{7,6},{8,9},{9,8},{10,11... | collective-permute-start | bytes 6291464 | tf_op jit(solution)/shard_map/ppermute | solution.py:22
  470.7 32.6 %collective-permute-start.43 = (bf16[4,128,2048]{2,1,0:T(8,128)(2,1)}, bf16[4,128,2048]{2,1,0:T(8,128)(2,1)}, u32[]{:S(2)}, u32[]{:S(2)}) collective-permute-start(bf16[4,128,2048]{2,1,0:T(8,128)(2,1)} %get-tuple-element.183), channel_id=1, source_target_pairs={{0,1},{1,0},{2,3},{3,2},{4,5},{5,4},{6,7},{7,6},{8,9},{9,8},{10,11... | collective-permute-start | bytes 6291464 | tf_op jit(solution)/shard_map/ppermute | solution.py:22
  473.1 30.2 %collective-permute-start.41 = (bf16[1536,256]{1,0:T(8,128)(2,1)}, bf16[1536,256]{1,0:T(8,128)(2,1)}, u32[]{:S(2)}, u32[]{:S(2)}) collective-permute-start(bf16[1536,256]{1,0:T(8,128)(2,1)} %dynamic-slice_bitcast_fusion.3), channel_id=1, source_target_pairs={{0,16},{16,0},{1,17},{17,1},{2,18},{18,2},{3,19},{19,3},{4,20},{20... | collective-permute-start | bytes 2359304 | tf_op jit(solution)/shard_map/ppermute | solution.py:22
  516.1 58.4 %collective-permute-start.47 = (bf16[2,1,2,128,2048]{4,3,2,1,0:T(8,128)(2,1)}, bf16[2,1,2,128,2048]{4,3,2,1,0:T(8,128)(2,1)}, u32[]{:S(2)}, u32[]{:S(2)}) collective-permute-start(bf16[2,1,2,128,2048]{4,3,2,1,0:T(8,128)(2,1)} %get-tuple-element.197), channel_id=1, source_target_pairs={{0,16},{16,0},{1,17},{17,1},{2,18},{18,2},{3,19},{19,3},{4,20},{20... | collective-permute-start | bytes 6291464 | tf_op jit(solution)/shard_map/ppermute | solution.py:22
  517.4 57.1 %collective-permute-start.46 = (bf16[2,2,1,128,2048]{4,3,2,1,0:T(8,128)(2,1)}, bf16[2,2,1,128,2048]{4,3,2,1,0:T(8,128)(2,1)}, u32[]{:S(2)}, u32[]{:S(2)}) collective-permute-start(bf16[2,2,1,128,2048]{4,3,2,1,0:T(8,128)(2,1)} %get-tuple-element.196.refs_36_), channel_id=1, source_target_pairs={{0,2},{1,3},{2,0},{3,1},{4,6},{5,7},{6,4},{7,5},{8,10},{9,11},{10,... | collective-permute-start | bytes 6291464 | tf_op jit(solution)/shard_map/ppermute | solution.py:22
  532.7 27.2 %collective-permute-start.48 = (bf16[2,768,256]{2,1,0:T(8,128)(2,1)S(1)}, bf16[2,768,256]{2,1,0:T(8,128)(2,1)}, u32[]{:S(2)}, u32[]{:S(2)}) collective-permute-start(bf16[2,768,256]{2,1,0:T(8,128)(2,1)S(1)} %get-tuple-element.236), channel_id=1, source_target_pairs={{0,4},{1,5},{2,6},{3,7},{16,20},{17,21},{18,22},{19,23}} | collective-permute-start | bytes 2359304 | tf_op jit(solution)/shard_map/ppermute | solution.py:159
  572.8 29.2 %collective-permute-start.56 = (bf16[1536,256]{1,0:T(8,128)(2,1)}, bf16[1536,256]{1,0:T(8,128)(2,1)}, u32[]{:S(2)}, u32[]{:S(2)}) collective-permute-start(bf16[1536,256]{1,0:T(8,128)(2,1)} %dynamic-slice_bitcast_fusion), channel_id=1, source_target_pairs={{0,16},{16,0},{1,17},{17,1},{2,18},{18,2},{3,19},{19,3},{4,20},{20... | collective-permute-start | bytes 2359304 | tf_op jit(solution)/shard_map/ppermute | solution.py:22
  600.0 26.4 %collective-permute-start.50 = (bf16[2,1,1,128,2048]{4,3,2,1,0:T(8,128)(2,1)}, bf16[2,1,1,128,2048]{4,3,2,1,0:T(8,128)(2,1)}, u32[]{:S(2)}, u32[]{:S(2)}) collective-permute-start(bf16[2,1,1,128,2048]{4,3,2,1,0:T(8,128)(2,1)} %get-tuple-element.203.refs_5_), channel_id=1, source_target_pairs={{0,16},{16,0},{1,17},{17,1},{2,18},{18,2},{3,19},{19,3},{4,20},{20... | collective-permute-start | bytes 3145736 | tf_op jit(solution)/shard_map/ppermute | solution.py:22
  (43 other events, 436.0 us)
Sparse Core Ops, SparseCore 0:
  26.1 64.9 all-gather.3
  92.6 114.0 all-gather.7
  208.3 113.5 all-gather.5
  324.0 108.9 reduce-scatter.2
  435.2 118.3 reduce-scatter.4

commit v4 on v3

--- a/solution.py
+++ b/solution.py
@@ -11,8 +11,7 @@
 THETA = 1000000.0
 NEGATIVE = -1e30
 CHUNKS = 2
-LARGE = int(63.5 * 2**20)
-SMALL = int(63.5 * 2**20)
+VMEM = 127 * 2**19
 BF = jnp.bfloat16
 F32 = jnp.float32
 
@@ -127,15 +126,29 @@
     return grad
 
 
-def end_scatter(pair):
-    sent = lax.dynamic_index_in_dim(pair, 1 - lax.axis_index("dp") % 2, 0, keepdims=False)
-    return pair, xchg(sent, "dp", 1)
+def for_partner(pair, low, order):
+    _, n, d = pair.shape
+
+    def kernel(low_ref, pair_ref, out_ref):
+        out_ref[...] = pair_ref[0]
+
+    return order.call(
+        "for_partner",
+        kernel,
+        (2,),
+        [pl.BlockSpec((1, n // 2, d), lambda t, low: (1 - low[0], t, 0))],
+        pl.BlockSpec((n // 2, d), lambda t, low: (t, 0)),
+        shaped(n, d),
+        (low, pair),
+        prefetch=1,
+        moved=4 * n * d,
+    )
 
 
 def scatter_weight(grad):
     grad = start_scatter(grad)
     grad = grad.reshape(2, -1, grad.shape[-1])
-    return end_scatter(lax.psum_scatter(grad, "row", scatter_dimension=1, tiled=True))
+    return lax.psum_scatter(grad, "row", scatter_dimension=1, tiled=True)
 
 
 class Chain:
@@ -192,7 +205,7 @@
         if far:
             self.send(*outs)
             return None
-        return end_scatter(outs[0])
+        return outs[0]
 
 
 def sum_over_col(value):
@@ -226,7 +239,7 @@
         )
 
     def call(
-        self, name, kernel, grid, in_specs, out_specs, out_shape, args, scratch=(), flops=0, moved=0, prefetch=0, aliases=None, large=False
+        self, name, kernel, grid, in_specs, out_specs, out_shape, args, scratch=(), flops=0, moved=0, prefetch=0, aliases=None
     ):
         last = [token for token in self.last if all(token is not arg for arg in args)]
         tokens = len(last)
@@ -247,7 +260,7 @@
             out_shape=out_shape,
             name=name,
             input_output_aliases=aliases or {},
-            compiler_params=pltpu.CompilerParams(vmem_limit_bytes=LARGE if large else SMALL),
+            compiler_params=pltpu.CompilerParams(vmem_limit_bytes=VMEM),
             cost_estimate=pl.CostEstimate(flops=flops, bytes_accessed=moved, transcendentals=0),
         )(*args, *last)
         self.last = (outs[0] if isinstance(outs, (list, tuple)) else outs,)
@@ -566,7 +579,6 @@
         flops=4 * places * weights.size + 16 * places * places * QUERY_PER_GROUP * head,
         moved=8 * places * width + 2 * weights.size,
         args=(scalars, *arrays(blocks), cosine, sine, weights),
-        large=True,
     )
 
 
@@ -619,7 +631,6 @@
         flops=4 * places * weights.size + 48 * places * places * groups * HEAD_SIZE,
         moved=8 * places * width + 2 * weights.size,
         args=(scalars, *arrays(pieces), cosine, sine, weights, *saved),
-        large=True,
     )
 
 
@@ -654,7 +665,6 @@
         flops=2 * count * places * weights.size,
         moved=4 * count * places * width,
         args=(*arrays(rows), *arrays(pieces), weights),
-        large=True,
     )
 
 
@@ -697,7 +707,6 @@
         moved=2 * len(products) * tokens * width,
         args=args,
         aliases={} if into is None else {len(args) - 1: 0},
-        large=True,
     )
 
 
@@ -736,7 +745,6 @@
         flops=8 * steps * places * depth * width * len(lefts),
         moved=16 * steps * places * width,
         args=(*lefts, *weights, *((before,) if added else ())),
-        large=True,
     )
 
 
@@ -778,7 +786,6 @@
         outs,
         (low, *args),
         moved=24 * w1.size,
-        large=True,
     )
 
 
@@ -796,8 +803,8 @@
     sum_ref[...] = as_row(total)
 
 
-def finish_attn(low, part, wqkv, wo, gain, order):
-    args = [*part, wqkv, gain]
+def finish_attn(low, pair, came, wqkv, wo, gain, order):
+    args = [pair, came, wqkv, gain]
     outs = [shaped(*shape, dtype=F32) for shape in (wqkv.shape, wo.shape, gain.shape[::-1])]
     return order.call(
         "finish_attn",
@@ -888,10 +895,11 @@
     ffn_grads = [scatter_weight(hidden_grads(0, pair_grads(0)))]
     early = back(pairs, ffn_ws[:1], 0, order)
     run_units(1)
-    halves = [
-        back(pairs[1:], ffn_ws[1:], 0, order, before=early, stream=m) for m in streams
-    ]
-    scatter = Scatter([(keep, xchg(send, "col", 1)) for keep, send in halves])
+    halves = [back(pairs[1:], ffn_ws[1:], 0, order, before=early, stream=0)]
+    first_came = xchg(halves[0][1], "col", 1)
+    halves.append(back(pairs[1:], ffn_ws[1:], 0, order, before=early, stream=1))
+    first_came, second_sent = order.fence(first_came, halves[1][1])
+    scatter = Scatter([(halves[0][0], first_came), (halves[1][0], xchg(second_sent, "col", 1))])
     scatter.first(order)
     part = pair_grads(1)
     scatter.second(order)
@@ -900,10 +908,11 @@
     attn_gather = Gather(attn_up.reshape(-1, width), rows, True)
     ffn_grads.append(scatter_weight(order.fence(grads)[0]))
     halves = [back(hiddens, ffn_ws, 2 * cut, order, stream=0)]
+    sent = for_partner(ffn_grads[0], low, order)
     attn_gather.cross(order)
     halves.append(back(hiddens, ffn_ws, 2 * cut, order, stream=1))
     attn_gather.fence(order)
-    attn_pieces, *sends = attn_gather.blocks(order, *[send for _, send in halves])
+    attn_pieces, sent, *sends = attn_gather.blocks(order, sent, *[send for _, send in halves])
     halves = [(keep, send) for (keep, _), send in zip(halves, sends)]
 
     def run_back(m):
@@ -911,16 +920,17 @@
             attn_pieces[m], rows, scalars[m], cosine, sine, attn_w, ahead[m][2:5], groups, order
         )
 
-    def arrived(part):
-        return part[0], order.fence(part[1])[0]
-
     out_sent = [(keep, xchg(send, "col", 1)) for keep, send in halves]
-    behind = [run_back(0), run_back(1)]
-    pair, came = ffn_grads[0]
-    came, *values = order.fence(came, *[item for _, item in out_sent], *[item[1] for item in behind])
-    ffn_grads[0] = (pair, came)
+    came = xchg(sent, "dp", 1)
+    behind = [run_back(0)]
+    first_came = xchg(behind[0][1], "col", 1)
+    behind.append(run_back(1))
+    came, first_came, second_sent, *values = order.fence(
+        came, first_came, behind[1][1], *[item for _, item in out_sent]
+    )
+    ffn_parts = [(ffn_grads[0], came)]
     out_parts = [(keep, item) for (keep, _), item in zip(out_sent, values)]
-    attn_parts = [(item[0], xchg(send, "col", 1)) for item, send in zip(behind, values[micro:])]
+    attn_parts = [(behind[0][0], first_came), (behind[1][0], xchg(second_sent, "col", 1))]
     scatter = Scatter(attn_parts, out_parts)
     scatter.first(order)
     attn_grads = weight_grads(
@@ -933,15 +943,18 @@
         order,
     )
     chain = Chain(attn_grads)
+    sent = for_partner(ffn_grads[1], low, order)
     chain.advance(order)
+    (came,) = order.fence(xchg(sent, "dp", 1))
+    ffn_parts.append((ffn_grads[1], came))
     scatter.second(order)
     chain.advance(order)
-    ffn_grads[1] = arrived(ffn_grads[1])
-    attn_part = chain.advance(order)
     source_grad, result = finished(inputs, residual_grad, residual, scatter.terms(), order)
-    w1_grad, w3_grad, w2_grad, ffn_sum = finish_ffn(low, ffn_grads, w1, w3, w2, ffn_gain, order)
+    attn_pair = chain.advance(order)
+    attn_came = xchg(for_partner(attn_pair, low, order), "dp", 1)
+    w1_grad, w3_grad, w2_grad, ffn_sum = finish_ffn(low, ffn_parts, w1, w3, w2, ffn_gain, order)
     ffn_sum = sum_over_col(ffn_sum)[0]
-    wqkv_grad, wo_grad, attn_sum = finish_attn(low, attn_part, wqkv, wo, attn_gain, order)
+    wqkv_grad, wo_grad, attn_sum = finish_attn(low, attn_pair, attn_came, wqkv, wo, attn_gain, order)
     attn_sum = sum_over_col(attn_sum)[0]
     return (
         result[:, None],

time: 663 us -> 652 us (0.983)
  waiting for transfers between devices: 268 us -> 260 us
    ppermute x3, waiting for transfers between devices: 32.3 us -> 2.92 us  [send(): lax.ppermute(up, 'row', [(i, i + 1) for i in range(self.step)])]
    reduce_scatter x2, waiting for transfers between devices: 0.01 us -> 24.6 us  [scatter_weight(): return lax.psum_scatter(grad, 'row', scatter_dimension=1, tiled=True)]
    ppermute x3, waiting for transfers between devices: 10.5 us -> 0.01 us  [send(): lax.ppermute(down, 'row', [(i, i - 1) for i in range(far, self.rows)])]
    ppermute x58, waiting for transfers between devices: 219 us -> 226 us  [xchg(): return lax.ppermute(value, axis, [(i, i ^ bit) for i in range(size)])]
    pallas_call x52 -> x56, Pallas kernels: 291 us -> 297 us  [call(): pl.pallas_call(run, grid_spec=pltpu.PrefetchScalarGridSpec(num_scalar_pre...]
  transfers between devices with their start and end apart: 69 -> 69, of which waited for: 42 -> 43; matrix products, arithmetic and copies ran while one was open for 3% -> 2% of each run, Pallas kernels for 44% -> 44%
where the time goes in v4:
time: 652 us; the launch traced here: 647 us
  Pallas kernels  297 us (46%)
  waiting for transfers between devices  260 us (40%)
  starting transfers between devices  59 us (9%)
  between operations  14.3 us (2%)
  other arithmetic  10.1 us (2%)
  local copies, waits for them, and re-layouts  6.93 us (1%)
    pallas_call x56, Pallas kernels, call(): pl.pallas_call(run, grid_spec=pltpu.PrefetchScalarGridSpec(num_scalar_pre...  297 us
    ppermute x58, waiting for transfers between devices, xchg(): return lax.ppermute(value, axis, [(i, i ^ bit) for i in range(size)])  226 us
    ppermute x58, starting transfers between devices, xchg(): return lax.ppermute(value, axis, [(i, i ^ bit) for i in range(size)])  38.9 us
    reduce_scatter x2, waiting for transfers between devices, scatter_weight(): return lax.psum_scatter(grad, 'row', scatter_dimension=1, tiled=True)  24.6 us
    ppermute x3, starting transfers between devices, send(): lax.ppermute(up, 'row', [(i, i + 1) for i in range(self.step)])  14.6 us
  transfers between devices with their start and end apart: 69, of which 43 were waited for; matrix products, arithmetic and copies ran while one was open for 2% of the time, Pallas kernels for 44%

profile of v4, /device:TPU:0, one launch (start us, length us, event | category | flops | bytes accessed | tf_op | source)
XLA Modules:
  0.0 646.8 jit_solution(13403858949719714637)
XLA Ops:
  17.5 5.7 collective-permute-done.4.refs_2_
  29.9 22.1 %collective-permute-done.2.refs_1_ = bf16[256,2048]{1,0:T(8,128)(2,1)} collective-permute-done((bf16[256,2048]{1,0:T(8,128)(2,1)}, bf16[256,2048]{1,0:T(8,128)(2,1)}, u32[]{:S(2)}, u32[]{:S(2)}) %collective-permute-start.2) | collective-permute-done | bytes 1048608 | tf_op jit(solution)/shard_map/ppermute | solution.py:21
  66.6 13.4 %collective-permute-done.8.refs_3_ = bf16[256,1536]{1,0:T(8,128)(2,1)} collective-permute-done((bf16[256,1536]{1,0:T(8,128)(2,1)}, bf16[256,1536]{1,0:T(8,128)(2,1)}, u32[]{:S(2)}, u32[]{:S(2)}) %collective-permute-start.8) | collective-permute-done | bytes 786464 | tf_op jit(solution)/shard_map/ppermute | solution.py:21
  91.1 12.1 %attend.2 = (bf16[4,128,2048]{2,1,0:T(8,128)(2,1)}, bf16[4,128,2048]{2,1,0:T(8,128)(2,1)}, bf16[2,512,256]{2,1,0:T(8,128)(2,1)}, bf16[2,512,128]{2,1,0:T(8,128)(...) custom-call(s32[3]{0:T(128)} %get-tuple-element.250.refs_7_.refs_0_, bf16[256,2048]{1,0:T(8,128)(2,1)} %bitcast.132, ...), custom_call_target="tpu_custom_call" | custom-call | flops 4294967296 | bytes 11534336 | tf_op jit(solution)/shard_map/attend/pallas_call | solution.py:251
  103.2 12.1 %attend.3 = (bf16[4,128,2048]{2,1,0:T(8,128)(2,1)}, bf16[4,128,2048]{2,1,0:T(8,128)(2,1)}, bf16[2,512,256]{2,1,0:T(8,128)(2,1)}, bf16[2,512,128]{2,1,0:T(8,128)(...) custom-call(s32[3]{0:T(128)} %get-tuple-element.251.refs_8_.refs_0_, bf16[256,2048]{1,0:T(8,128)(2,1)} %bitcast.133, ...), custom_call_target="tpu_custom_call" | custom-call | flops 4294967296 | bytes 11534336 | tf_op jit(solution)/shard_map/attend/pallas_call | solution.py:251
  129.3 22.5 %collective-permute-done.14.refs_5_.refs_9_ = bf16[1,1,2,128,2048]{4,3,2,1,0:T(8,128)(2,1)} collective-permute-done((bf16[1,1,2,128,2048]{4,3,2,1,0:T(8,128)(2,1)}, bf16[1,1,2,128,2048]{4,3,2,1,0:T(8,128)(2,1)}, u32[]{:S(2)}, u32[]{:S(2)}) %collective-permute-start.14) | collective-permute-done | bytes 1048608 | tf_op jit(solution)/shard_map/ppermute | solution.py:21
  158.4 10.5 %collective-permute-done.16.refs_10_ = bf16[1,1,1,128,2048]{4,3,2,1,0:T(8,128)(2,1)} collective-permute-done((bf16[1,1,1,128,2048]{4,3,2,1,0:T(8,128)(2,1)}, bf16[1,1,1,128,2048]{4,3,2,1,0:T(8,128)(2,1)}, u32[]{:S(2)}, u32[]{:S(2)}) %collective-permute-start.16) | collective-permute-done | bytes 524320 | tf_op jit(solution)/shard_map/ppermute | solution.py:21
  180.3 43.9 %collective-permute-done.18.refs_1_ = bf16[512,2048]{1,0:T(8,128)(2,1)} collective-permute-done((bf16[512,2048]{1,0:T(8,128)(2,1)}, bf16[512,2048]{1,0:T(8,128)(2,1)}, u32[]{:S(2)}, u32[]{:S(2)}) %collective-permute-start.18) | collective-permute-done | bytes 2097184 | tf_op jit(solution)/shard_map/ppermute | solution.py:21
  230.7 23.4 %collective-permute-done.23.refs_3_ = bf16[256,2048]{1,0:T(8,128)(2,1)} collective-permute-done((bf16[256,2048]{1,0:T(8,128)(2,1)}, bf16[256,2048]{1,0:T(8,128)(2,1)}, u32[]{:S(2)}, u32[]{:S(2)}) %collective-permute-start.23) | collective-permute-done | bytes 1048608 | tf_op jit(solution)/shard_map/ppermute | solution.py:21
  259.9 20.0 %units.2 = (bf16[16,128,1024]{2,1,0:T(8,128)(2,1)}, bf16[16,128,512]{2,1,0:T(8,128)(2,1)}) custom-call(bf16[512,2048]{1,0:T(8,128)(2,1)} %bitcast.67, bf16[512,2048]{1,0:T(8,128)(2,1)} %get-tuple-element.142.refs_1_.refs_9_.refs_17_.refs_25_, bf16[512,2048]{1,0:T(8,128)(2,1)} %get-tuple-element.143.refs_1_.refs_2_.refs_10_.refs_18_.refs_26_, ...), custom_call_target="tpu_custom_call" | custom-call | flops 12884901888 | bytes 16777216 | tf_op jit(solution)/shard_map/units/pallas_call | solution.py:251
  279.9 13.7 %weight_grads.5.refs_17_ = bf16[8,1536,256]{2,1,0:T(8,128)(2,1)} custom-call(bf16[512,2048]{1,0:T(8,128)(2,1)} %bitcast.71, bf16[512,2048]{1,0:T(8,128)(2,1)} %get-tuple-element.142.refs_1_.refs_9_.refs_17_.refs_25_, bf16[512,2048]{1,0:T(8,128)(2,1)} %get-tuple-element.143.refs_1_.refs_2_.refs_10_.refs_18_.refs_26_, ...), custom_call_target="tpu_custom_call" | custom-call | flops 8589934592 | bytes 8388608 | tf_op jit(solution)/shard_map/weight_grads/pallas_call | solution.py:251
  293.6 9.0 %weight_grads.6.refs_2_ = bf16[8,1536,256]{2,1,0:T(8,128)(2,1)} custom-call(bf16[512,2048]{1,0:T(8,128)(2,1)} %bitcast.73, bf16[512,2048]{1,0:T(8,128)(2,1)} %get-tuple-element.142.refs_1_.refs_9_.refs_17_.refs_25_, bf16[512,2048]{1,0:T(8,128)(2,1)} %get-tuple-element.143.refs_1_.refs_2_.refs_10_.refs_18_.refs_26_, ...), custom_call_target="tpu_custom_call", output_to_operand_aliasing={{}: (17, {})} | custom-call | flops 4294967296 | bytes 8388608 | tf_op jit(solution)/shard_map/weight_grads/pallas_call | solution.py:251
  302.7 14.2 %back.5.refs_33_.refs_2_ = f32[2048,2048]{1,0:T(8,128)} custom-call(bf16[16,128,1024]{2,1,0:T(8,128)(2,1)} %get-tuple-element.153.refs_17_.refs_0_, bf16[2048,1536]{1,0:T(8,128)(2,1)} %bitcast.98, bf16[8,1536,256]{2,1,0:T(8,128)(2,1)} %weight_grads.6.refs_2_), custom_call_target="tpu_custom_call" | custom-call | flops 8589934592 | bytes 16777216 | tf_op jit(solution)/shard_map/back/pallas_call | solution.py:251
  321.9 20.0 %units.3 = (bf16[16,128,1024]{2,1,0:T(8,128)(2,1)}, bf16[16,128,512]{2,1,0:T(8,128)(2,1)}) custom-call(bf16[512,2048]{1,0:T(8,128)(2,1)} %bitcast.75, bf16[512,2048]{1,0:T(8,128)(2,1)} %get-tuple-element.142.refs_1_.refs_9_.refs_17_.refs_25_, bf16[512,2048]{1,0:T(8,128)(2,1)} %get-tuple-element.143.refs_1_.refs_2_.refs_10_.refs_18_.refs_26_, ...), custom_call_target="tpu_custom_call" | custom-call | flops 12884901888 | bytes 16777216 | tf_op jit(solution)/shard_map/units/pallas_call | solution.py:251
  341.9 9.8 %back.6 = (bf16[4,128,2048]{2,1,0:T(8,128)(2,1)}, bf16[4,128,2048]{2,1,0:T(8,128)(2,1)}) custom-call(bf16[16,128,1024]{2,1,0:T(8,128)(2,1)} %get-tuple-element.155.refs_0_, bf16[2048,1536]{1,0:T(8,128)(2,1)} %bitcast.92, f32[2048,2048]{1,0:T(8,128)} %back.5.refs_33_.refs_2_), custom_call_target="tpu_custom_call" | custom-call | flops 4294967296 | bytes 8388608 | tf_op jit(solution)/shard_map/back/pallas_call | solution.py:251
  351.8 9.9 %back.7 = (bf16[4,128,2048]{2,1,0:T(8,128)(2,1)}, bf16[4,128,2048]{2,1,0:T(8,128)(2,1)}) custom-call(bf16[16,128,1024]{2,1,0:T(8,128)(2,1)} %get-tuple-element.155.refs_0_, bf16[2048,1536]{1,0:T(8,128)(2,1)} %bitcast.93, f32[2048,2048]{1,0:T(8,128)} %back.5.refs_33_.refs_2_, bf16[4,128,2048]{2,1,0:T(8,128)(2,1)} %get-tuple-element.156.refs_3_), custom_call_target="tpu_custom_call" | custom-call | flops 4294967296 | bytes 8388608 | tf_op jit(solution)/shard_map/back/pallas_call | solution.py:251
  372.6 13.6 %weight_grads.7.refs_6_.refs_17_ = bf16[8,1536,256]{2,1,0:T(8,128)(2,1)} custom-call(bf16[512,2048]{1,0:T(8,128)(2,1)} %bitcast.79, bf16[512,2048]{1,0:T(8,128)(2,1)} %get-tuple-element.142.refs_1_.refs_9_.refs_17_.refs_25_, bf16[512,2048]{1,0:T(8,128)(2,1)} %get-tuple-element.143.refs_1_.refs_2_.refs_10_.refs_18_.refs_26_, ...), custom_call_target="tpu_custom_call" | custom-call | flops 8589934592 | bytes 8388608 | tf_op jit(solution)/shard_map/weight_grads/pallas_call | solution.py:251
  386.2 9.2 %collective-permute-done.29.refs_5_.refs_8_ = bf16[1,1,2,128,2048]{4,3,2,1,0:T(8,128)(2,1)} collective-permute-done((bf16[1,1,2,128,2048]{4,3,2,1,0:T(8,128)(2,1)}, bf16[1,1,2,128,2048]{4,3,2,1,0:T(8,128)(2,1)}, u32[]{:S(2)}, u32[]{:S(2)}) %collective-permute-start.29) | collective-permute-done | bytes 1048608 | tf_op jit(solution)/shard_map/ppermute | solution.py:21
  401.4 9.0 %weight_grads.8.refs_10_.refs_0_ = bf16[8,1536,256]{2,1,0:T(8,128)(2,1)} custom-call(bf16[512,2048]{1,0:T(8,128)(2,1)} %bitcast.81, bf16[512,2048]{1,0:T(8,128)(2,1)} %get-tuple-element.142.refs_1_.refs_9_.refs_17_.refs_25_, bf16[512,2048]{1,0:T(8,128)(2,1)} %get-tuple-element.143.refs_1_.refs_2_.refs_10_.refs_18_.refs_26_, ...), custom_call_target="tpu_custom_call", output_to_operand_aliasing={{}: (17, {})} | custom-call | flops 4294967296 | bytes 8388608 | tf_op jit(solution)/shard_map/weight_grads/pallas_call | solution.py:251
  414.0 5.8 by_rows.16
  421.1 8.6 %back.8 = (bf16[4,128,2048]{2,1,0:T(8,128)(2,1)}, bf16[4,128,2048]{2,1,0:T(8,128)(2,1)}) custom-call(bf16[16,128,512]{2,1,0:T(8,128)(2,1)} %get-tuple-element.154.refs_0_, bf16[16,128,512]{2,1,0:T(8,128)(2,1)} %get-tuple-element.166.refs_1_, bf16[2048,1536]{1,0:T(8,128)(2,1)} %bitcast.99, bf16[2048,1536]{1,0:T(8,128)(2,1)} %bitcast.94, ...), custom_call_target="tpu_custom_call" | custom-call | flops 4294967296 | bytes 8388608 | tf_op jit(solution)/shard_map/back/pallas_call | solution.py:251
  434.9 10.9 %collective-permute-done.33.refs_1_ = bf16[256,2048]{1,0:T(8,128)(2,1)} collective-permute-done((bf16[256,2048]{1,0:T(8,128)(2,1)}, bf16[256,2048]{1,0:T(8,128)(2,1)}, u32[]{:S(2)}, u32[]{:S(2)}) %collective-permute-start.33) | collective-permute-done | bytes 1048608 | tf_op jit(solution)/shard_map/ppermute | solution.py:21
  452.1 9.1 %back.9 = (bf16[4,128,2048]{2,1,0:T(8,128)(2,1)}, bf16[4,128,2048]{2,1,0:T(8,128)(2,1)}) custom-call(bf16[16,128,512]{2,1,0:T(8,128)(2,1)} %get-tuple-element.154.refs_0_, bf16[16,128,512]{2,1,0:T(8,128)(2,1)} %get-tuple-element.166.refs_1_, bf16[2048,1536]{1,0:T(8,128)(2,1)} %bitcast.100, bf16[2048,1536]{1,0:T(8,128)(2,1)} %bitcast.95, ...), custom_call_target="tpu_custom_call" | custom-call | flops 4294967296 | bytes 8388608 | tf_op jit(solution)/shard_map/back/pallas_call | solution.py:251
  468.9 14.7 %attend_back.2 = (bf16[4,128,2048]{2,1,0:T(8,128)(2,1)}, bf16[4,128,2048]{2,1,0:T(8,128)(2,1)}, bf16[2,512,512]{2,1,0:T(8,128)(2,1)}) custom-call(s32[3]{0:T(128)} %get-tuple-element.250.refs_7_.refs_0_, bf16[256,2048]{1,0:T(8,128)(2,1)} %bitcast.30.refs_1_.refs_16_.refs_24_, bf16[256,2048]{1,0:T(8,128)(2,1)} %get-tuple-element.170.refs_2_.refs_17_.refs_25_, ...), custom_call_target="tpu_custom_call" | custom-call | flops 4831838208 | bytes 11534336 | tf_op jit(solution)/shard_map/attend_back/pallas_call | solution.py:251
  484.4 14.8 %attend_back.3 = (bf16[4,128,2048]{2,1,0:T(8,128)(2,1)}, bf16[4,128,2048]{2,1,0:T(8,128)(2,1)}, bf16[2,512,512]{2,1,0:T(8,128)(2,1)}) custom-call(s32[3]{0:T(128)} %get-tuple-element.251.refs_8_.refs_0_, bf16[256,2048]{1,0:T(8,128)(2,1)} %bitcast.30.refs_1_.refs_16_.refs_24_, bf16[256,2048]{1,0:T(8,128)(2,1)} %get-tuple-element.170.refs_2_.refs_17_.refs_25_, ...), custom_call_target="tpu_custom_call" | custom-call | flops 4831838208 | bytes 11534336 | tf_op jit(solution)/shard_map/attend_back/pallas_call | solution.py:251
  514.7 12.4 %weight_grads.9.refs_2_ = bf16[8,768,256]{2,1,0:T(8,128)(2,1)} custom-call(bf16[256,2048]{1,0:T(8,128)(2,1)} %bitcast.134, bf16[256,2048]{1,0:T(8,128)(2,1)} %get-tuple-element.118.refs_2_.refs_1_.refs_9_, bf16[256,2048]{1,0:T(8,128)(2,1)} %get-tuple-element.119.refs_5_.refs_3_.refs_2_.refs_10_, ...), custom_call_target="tpu_custom_call" | custom-call | flops 6442450944 | bytes 16777216 | tf_op jit(solution)/shard_map/weight_grads/pallas_call | solution.py:251
  533.4 21.3 %reduce-scatter.5.cloned.1.call-done.refs_1_.refs_2_ = bf16[2,1536,256]{2,1,0:T(8,128)(2,1)} async-done(((bf16[2,6144,256]{2,1,0:T(8,128)(2,1)}), bf16[2,1536,256]{2,1,0:T(8,128)(2,1)}) %reduce-scatter.5.cloned.1.call-update) | async-done | bytes 1572880 | tf_op jit(solution)/shard_map/reduce_scatter | solution.py:151
  570.1 8.6 %collective-permute-done.48.refs_0_ = bf16[1536,256]{1,0:T(8,128)(2,1)} collective-permute-done((bf16[1536,256]{1,0:T(8,128)(2,1)}, bf16[1536,256]{1,0:T(8,128)(2,1)}, u32[]{:S(2)}, u32[]{:S(2)}) %collective-permute-start.48) | collective-permute-done | bytes 786464 | tf_op jit(solution)/shard_map/ppermute | solution.py:21
  591.1 7.4 %collective-permute-start.55 = (bf16[2,768,256]{2,1,0:T(8,128)(2,1)}, bf16[2,768,256]{2,1,0:T(8,128)(2,1)}, u32[]{:S(2)}, u32[]{:S(2)}) collective-permute-start(bf16[2,768,256]{2,1,0:T(8,128)(2,1)} %get-tuple-element.212.refs_19_), channel_id=1, source_target_pairs={{0,4},{4,8},{8,12},{1,5},{5,9},{9,13},{2,6},{6,10},{10,14},{3,7},{... | collective-permute-start | bytes 2359304 | tf_op jit(solution)/shard_map/ppermute | solution.py:172
  599.1 8.5 %collective-permute-done.52.refs_10_.refs_18_ = bf16[2,1,1,128,2048]{4,3,2,1,0:T(8,128)(2,1)} collective-permute-done((bf16[2,1,1,128,2048]{4,3,2,1,0:T(8,128)(2,1)}, bf16[2,1,1,128,2048]{4,3,2,1,0:T(8,128)(2,1)}, u32[]{:S(2)}, u32[]{:S(2)}) %collective-permute-start.52) | collective-permute-done | bytes 1048608 | tf_op jit(solution)/shard_map/ppermute | solution.py:21
  608.0 7.7 %by_rows.19 = (bf16[2,128,2048]{2,1,0:T(8,128)(2,1)}, bf16[2,128,2048]{2,1,0:T(8,128)(2,1)}) custom-call(bf16[2,128,2048]{2,1,0:T(8,128)(2,1)} %bitcast.138, f32[2,128,2048]{2,1,0:T(8,128)} %get-tuple-element.167.refs_1_, f32[2,128,2048]{2,1,0:T(8,128)} %get-tuple-element.140.refs_0_.refs_2_, bf16[2,2,128,2048]{3,2,1,0:T(8,128)(2,1)} %bitcast.123, ...), custom_call_target="tpu_custom_call" | custom-call | bytes 69206016 | tf_op jit(solution)/shard_map/by_rows/pallas_call | solution.py:251
  621.3 6.9 %finish_ffn.1 = (f32[256,2048]{1,0:T(8,128)}, f32[256,2048]{1,0:T(8,128)}, f32[2048,256]{1,0:T(8,128)}, f32[1,256]{1,0:T(1,128)}) custom-call(s32[1]{0:T(128)} %bitcast.7.refs_0_, bf16[2,1536,256]{2,1,0:T(8,128)(2,1)} %reduce-scatter.3.cloned.1.call-done.refs_1_, bf16[2,1536,256]{2,1,0:T(8,128)(2,1)} %reduce-scatter.5.cloned.1.call-done.refs_1_.refs_2_, ...), custom_call_target="tpu_custom_call" | custom-call | bytes 12582912 | tf_op jit(solution)/shard_map/finish_ffn/pallas_call | solution.py:251
  (196 shorter events, 201.9 us)
Async XLA Ops:
  7.2 83.9 %all-gather.4.cloned.1.call-start = ((), (), s32[]{:S(2)}) async-start(), calls=%async_computation.2 | async-start | bytes 3932160 | tf_op jit(solution)/shard_map/all_gather | solution.py:113
  26.0 233.9 %all-gather.8.cloned.1.call-start = ((), (), s32[]{:S(2)}) async-start(), calls=%async_computation.4 | async-start | bytes 7864320 | tf_op jit(solution)/shard_map/all_gather | solution.py:113
  26.1 25.9 %collective-permute-start.2 = (bf16[256,2048]{1,0:T(8,128)(2,1)}, bf16[256,2048]{1,0:T(8,128)(2,1)}, u32[]{:S(2)}, u32[]{:S(2)}) collective-permute-start(bf16[256,2048]{1,0:T(8,128)(2,1)} %bitcast.130), channel_id=1, source_target_pairs={{0,16},{16,0},{1,17},{17,1},{2,18},{18,2},{3,19},{19,3},{4,20},{20... | collective-permute-start | bytes 3145736 | tf_op jit(solution)/shard_map/ppermute | solution.py:21
  27.9 25.5 %collective-permute-start.1 = (bf16[256,2048]{1,0:T(8,128)(2,1)}, bf16[256,2048]{1,0:T(8,128)(2,1)}, u32[]{:S(2)}, u32[]{:S(2)}) collective-permute-start(bf16[256,2048]{1,0:T(8,128)(2,1)} %bitcast.131), channel_id=1, source_target_pairs={{0,2},{1,3},{2,0},{3,1},{4,6},{5,7},{6,4},{7,5},{8,10},{9,11},{10,... | collective-permute-start | bytes 3145736 | tf_op jit(solution)/shard_map/ppermute | solution.py:21
  29.4 33.3 %collective-permute-start = (s32[2,1]{0,1:T(1,128)S(1)}, s32[2,1]{0,1:T(1,128)S(1)}, u32[]{:S(2)}, u32[]{:S(2)}) collective-permute-start(s32[2,1]{0,1:T(1,128)S(1)} %copy-done.2), channel_id=1, source_target_pairs={{0,16},{16,0},{1,17},{17,1},{2,18},{18,2},{3,19},{19,3},{4,20},{20... | collective-permute-start | bytes 32 | tf_op jit(solution)/shard_map/ppermute | solution.py:21
  53.5 26.5 %collective-permute-start.7 = (bf16[256,2048]{1,0:T(8,128)(2,1)}, bf16[256,2048]{1,0:T(8,128)(2,1)}, u32[]{:S(2)}, u32[]{:S(2)}) collective-permute-start(bf16[256,2048]{1,0:T(8,128)(2,1)} %get-tuple-element.120.refs_5_.refs_4_.refs_12_), channel_id=1, source_target_pairs={{0,2},{1,3},{2,0},{3,1},{4,6},{5,7},{6,4},{7,5},{8,10},{9,11},{10,... | collective-permute-start | bytes 3145736 | tf_op jit(solution)/shard_map/ppermute | solution.py:21
  55.0 25.0 %collective-permute-start.6 = (bf16[256,2048]{1,0:T(8,128)(2,1)}, bf16[256,2048]{1,0:T(8,128)(2,1)}, u32[]{:S(2)}, u32[]{:S(2)}) collective-permute-start(bf16[256,2048]{1,0:T(8,128)(2,1)} %get-tuple-element.120.refs_5_.refs_4_.refs_12_), channel_id=1, source_target_pairs={{0,1},{1,0},{2,3},{3,2},{4,5},{5,4},{6,7},{7,6},{8,9},{9,8},{10,11... | collective-permute-start | bytes 3145736 | tf_op jit(solution)/shard_map/ppermute | solution.py:21
  55.0 25.0 %collective-permute-start.5 = (bf16[256,2048]{1,0:T(8,128)(2,1)}, bf16[256,2048]{1,0:T(8,128)(2,1)}, u32[]{:S(2)}, u32[]{:S(2)}) collective-permute-start(bf16[256,2048]{1,0:T(8,128)(2,1)} %get-tuple-element.119.refs_5_.refs_3_.refs_2_.refs_10_), channel_id=1, source_target_pairs={{0,1},{1,0},{2,3},{3,2},{4,5},{5,4},{6,7},{7,6},{8,9},{9,8},{10,11... | collective-permute-start | bytes 3145736 | tf_op jit(solution)/shard_map/ppermute | solution.py:21
  82.6 239.2 %all-gather.6.cloned.1.call-start = ((), (), s32[]{:S(2)}) async-start(), calls=%async_computation.3 | async-start | bytes 7864320 | tf_op jit(solution)/shard_map/all_gather | solution.py:113
  89.4 25.9 %collective-permute-start.10 = (bf16[256,1536]{1,0:T(8,128)(2,1)}, bf16[256,1536]{1,0:T(8,128)(2,1)}, u32[]{:S(2)}, u32[]{:S(2)}) collective-permute-start(bf16[256,1536]{1,0:T(8,128)(2,1)} %get-tuple-element.129), channel_id=1, source_target_pairs={{0,16},{16,0},{1,17},{17,1},{2,18},{18,2},{3,19},{19,3},{4,20},{20... | collective-permute-start | bytes 2359304 | tf_op jit(solution)/shard_map/ppermute | solution.py:21
  118.5 314.5 %reduce-scatter.3.cloned.1.call-start = ((), (), s32[]{:S(2)}) async-start(), calls=%async_computation.5 | async-start | bytes 7864320 | tf_op jit(solution)/shard_map/reduce_scatter | solution.py:151
  126.2 25.5 %collective-permute-start.14 = (bf16[1,1,2,128,2048]{4,3,2,1,0:T(8,128)(2,1)}, bf16[1,1,2,128,2048]{4,3,2,1,0:T(8,128)(2,1)}, u32[]{:S(2)}, u32[]{:S(2)}) collective-permute-start(bf16[1,1,2,128,2048]{4,3,2,1,0:T(8,128)(2,1)} %get-tuple-element.137), channel_id=1, source_target_pairs={{0,16},{16,0},{1,17},{17,1},{2,18},{18,2},{3,19},{19,3},{4,20},{20... | collective-permute-start | bytes 3145736 | tf_op jit(solution)/shard_map/ppermute | solution.py:21
  127.8 25.2 %collective-permute-start.13 = (bf16[1,2,1,128,2048]{4,3,2,1,0:T(8,128)(2,1)}, bf16[1,2,1,128,2048]{4,3,2,1,0:T(8,128)(2,1)}, u32[]{:S(2)}, u32[]{:S(2)}) collective-permute-start(bf16[1,2,1,128,2048]{4,3,2,1,0:T(8,128)(2,1)} %get-tuple-element.136.refs_6_), channel_id=1, source_target_pairs={{0,2},{1,3},{2,0},{3,1},{4,6},{5,7},{6,4},{7,5},{8,10},{9,11},{10,... | collective-permute-start | bytes 3145736 | tf_op jit(solution)/shard_map/ppermute | solution.py:21
  175.8 48.4 %collective-permute-start.18 = (bf16[512,2048]{1,0:T(8,128)(2,1)}, bf16[512,2048]{1,0:T(8,128)(2,1)}, u32[]{:S(2)}, u32[]{:S(2)}) collective-permute-start(bf16[512,2048]{1,0:T(8,128)(2,1)} %bitcast.65), channel_id=1, source_target_pairs={{0,16},{16,0},{1,17},{17,1},{2,18},{18,2},{3,19},{19,3},{4,20},{20... | collective-permute-start | bytes 6291464 | tf_op jit(solution)/shard_map/ppermute | solution.py:21
  176.5 48.0 %collective-permute-start.17 = (bf16[512,2048]{1,0:T(8,128)(2,1)}, bf16[512,2048]{1,0:T(8,128)(2,1)}, u32[]{:S(2)}, u32[]{:S(2)}) collective-permute-start(bf16[512,2048]{1,0:T(8,128)(2,1)} %bitcast.66), channel_id=1, source_target_pairs={{0,2},{1,3},{2,0},{3,1},{4,6},{5,7},{6,4},{7,5},{8,10},{9,11},{10,... | collective-permute-start | bytes 6291464 | tf_op jit(solution)/shard_map/ppermute | solution.py:21
  224.5 30.8 %collective-permute-start.20 = (bf16[512,2048]{1,0:T(8,128)(2,1)}, bf16[512,2048]{1,0:T(8,128)(2,1)}, u32[]{:S(2)}, u32[]{:S(2)}) collective-permute-start(bf16[512,2048]{1,0:T(8,128)(2,1)} %get-tuple-element.143.refs_1_.refs_2_.refs_10_.refs_18_.refs_26_), channel_id=1, source_target_pairs={{0,1},{1,0},{2,3},{3,2},{4,5},{5,4},{6,7},{7,6},{8,9},{9,8},{10,11... | collective-permute-start | bytes 6291464 | tf_op jit(solution)/shard_map/ppermute | solution.py:21
  224.5 30.8 %collective-permute-start.21 = (bf16[512,2048]{1,0:T(8,128)(2,1)}, bf16[512,2048]{1,0:T(8,128)(2,1)}, u32[]{:S(2)}, u32[]{:S(2)}) collective-permute-start(bf16[512,2048]{1,0:T(8,128)(2,1)} %get-tuple-element.144.refs_0_.refs_4_.refs_12_.refs_20_.refs_28_), channel_id=1, source_target_pairs={{0,1},{1,0},{2,3},{3,2},{4,5},{5,4},{6,7},{7,6},{8,9},{9,8},{10,11... | collective-permute-start | bytes 6291464 | tf_op jit(solution)/shard_map/ppermute | solution.py:21
  228.8 25.4 %collective-permute-start.23 = (bf16[256,2048]{1,0:T(8,128)(2,1)}, bf16[256,2048]{1,0:T(8,128)(2,1)}, u32[]{:S(2)}, u32[]{:S(2)}) collective-permute-start(bf16[256,2048]{1,0:T(8,128)(2,1)} %get-tuple-element.146), channel_id=1, source_target_pairs={{0,16},{16,0},{1,17},{17,1},{2,18},{18,2},{3,19},{19,3},{4,20},{20... | collective-permute-start | bytes 3145736 | tf_op jit(solution)/shard_map/ppermute | solution.py:21
  230.2 25.1 %collective-permute-start.22 = (bf16[256,2048]{1,0:T(8,128)(2,1)}, bf16[256,2048]{1,0:T(8,128)(2,1)}, u32[]{:S(2)}, u32[]{:S(2)}) collective-permute-start(bf16[256,2048]{1,0:T(8,128)(2,1)} %get-tuple-element.145.refs_4_), channel_id=1, source_target_pairs={{0,2},{1,3},{2,0},{3,1},{4,6},{5,7},{6,4},{7,5},{8,10},{9,11},{10,... | collective-permute-start | bytes 3145736 | tf_op jit(solution)/shard_map/ppermute | solution.py:21
  302.6 252.1 %reduce-scatter.5.cloned.1.call-start = ((), (), s32[]{:S(2)}) async-start(), calls=%async_computation.6 | async-start | bytes 7864320 | tf_op jit(solution)/shard_map/reduce_scatter | solution.py:151
  369.7 25.8 %collective-permute-start.29 = (bf16[1,1,2,128,2048]{4,3,2,1,0:T(8,128)(2,1)}, bf16[1,1,2,128,2048]{4,3,2,1,0:T(8,128)(2,1)}, u32[]{:S(2)}, u32[]{:S(2)}) collective-permute-start(bf16[1,1,2,128,2048]{4,3,2,1,0:T(8,128)(2,1)} %get-tuple-element.163), channel_id=1, source_target_pairs={{0,16},{16,0},{1,17},{17,1},{2,18},{18,2},{3,19},{19,3},{4,20},{20... | collective-permute-start | bytes 3145736 | tf_op jit(solution)/shard_map/ppermute | solution.py:21
  371.1 25.5 %collective-permute-start.28 = (bf16[1,2,1,128,2048]{4,3,2,1,0:T(8,128)(2,1)}, bf16[1,2,1,128,2048]{4,3,2,1,0:T(8,128)(2,1)}, u32[]{:S(2)}, u32[]{:S(2)}) collective-permute-start(bf16[1,2,1,128,2048]{4,3,2,1,0:T(8,128)(2,1)} %get-tuple-element.162.refs_17_), channel_id=1, source_target_pairs={{0,2},{1,3},{2,0},{3,1},{4,6},{5,7},{6,4},{7,5},{8,10},{9,11},{10,... | collective-permute-start | bytes 3145736 | tf_op jit(solution)/shard_map/ppermute | solution.py:21
  419.9 25.9 %collective-permute-start.33 = (bf16[256,2048]{1,0:T(8,128)(2,1)}, bf16[256,2048]{1,0:T(8,128)(2,1)}, u32[]{:S(2)}, u32[]{:S(2)}) collective-permute-start(bf16[256,2048]{1,0:T(8,128)(2,1)} %bitcast.30.refs_1_.refs_16_.refs_24_), channel_id=1, source_target_pairs={{0,16},{16,0},{1,17},{17,1},{2,18},{18,2},{3,19},{19,3},{4,20},{20... | collective-permute-start | bytes 3145736 | tf_op jit(solution)/shard_map/ppermute | solution.py:21
  420.6 25.5 %collective-permute-start.32 = (bf16[256,2048]{1,0:T(8,128)(2,1)}, bf16[256,2048]{1,0:T(8,128)(2,1)}, u32[]{:S(2)}, u32[]{:S(2)}) collective-permute-start(bf16[256,2048]{1,0:T(8,128)(2,1)} %bitcast.30.refs_1_.refs_16_.refs_24_), channel_id=1, source_target_pairs={{0,2},{1,3},{2,0},{3,1},{4,6},{5,7},{6,4},{7,5},{8,10},{9,11},{10,... | collective-permute-start | bytes 3145736 | tf_op jit(solution)/shard_map/ppermute | solution.py:21
  468.4 35.5 %collective-permute-start.43 = (bf16[4,128,2048]{2,1,0:T(8,128)(2,1)}, bf16[4,128,2048]{2,1,0:T(8,128)(2,1)}, u32[]{:S(2)}, u32[]{:S(2)}) collective-permute-start(bf16[4,128,2048]{2,1,0:T(8,128)(2,1)} %get-tuple-element.194), channel_id=1, source_target_pairs={{0,1},{1,0},{2,3},{3,2},{4,5},{5,4},{6,7},{7,6},{8,9},{9,8},{10,11... | collective-permute-start | bytes 6291464 | tf_op jit(solution)/shard_map/ppermute | solution.py:21
  468.5 35.4 %collective-permute-start.44 = (bf16[4,128,2048]{2,1,0:T(8,128)(2,1)}, bf16[4,128,2048]{2,1,0:T(8,128)(2,1)}, u32[]{:S(2)}, u32[]{:S(2)}) collective-permute-start(bf16[4,128,2048]{2,1,0:T(8,128)(2,1)} %get-tuple-element.195), channel_id=1, source_target_pairs={{0,1},{1,0},{2,3},{3,2},{4,5},{5,4},{6,7},{7,6},{8,9},{9,8},{10,11... | collective-permute-start | bytes 6291464 | tf_op jit(solution)/shard_map/ppermute | solution.py:21
  513.9 64.8 %collective-permute-start.47 = (bf16[2,1,2,128,2048]{4,3,2,1,0:T(8,128)(2,1)}, bf16[2,1,2,128,2048]{4,3,2,1,0:T(8,128)(2,1)}, u32[]{:S(2)}, u32[]{:S(2)}) collective-permute-start(bf16[2,1,2,128,2048]{4,3,2,1,0:T(8,128)(2,1)} %get-tuple-element.203), channel_id=1, source_target_pairs={{0,16},{16,0},{1,17},{17,1},{2,18},{18,2},{3,19},{19,3},{4,20},{20... | collective-permute-start | bytes 6291464 | tf_op jit(solution)/shard_map/ppermute | solution.py:21
  514.3 64.4 %collective-permute-start.46 = (bf16[2,2,1,128,2048]{4,3,2,1,0:T(8,128)(2,1)}, bf16[2,2,1,128,2048]{4,3,2,1,0:T(8,128)(2,1)}, u32[]{:S(2)}, u32[]{:S(2)}) collective-permute-start(bf16[2,2,1,128,2048]{4,3,2,1,0:T(8,128)(2,1)} %get-tuple-element.202.refs_36_), channel_id=1, source_target_pairs={{0,2},{1,3},{2,0},{3,1},{4,6},{5,7},{6,4},{7,5},{8,10},{9,11},{10,... | collective-permute-start | bytes 6291464 | tf_op jit(solution)/shard_map/ppermute | solution.py:21
  529.7 29.4 %collective-permute-start.50 = (bf16[2,768,256]{2,1,0:T(8,128)(2,1)}, bf16[2,768,256]{2,1,0:T(8,128)(2,1)}, u32[]{:S(2)}, u32[]{:S(2)}) collective-permute-start(bf16[2,768,256]{2,1,0:T(8,128)(2,1)} %get-tuple-element.241), channel_id=1, source_target_pairs={{12,8},{13,9},{14,10},{15,11},{28,24},{29,25},{30,26},{31,27}} | collective-permute-start | bytes 2359304 | tf_op jit(solution)/shard_map/ppermute | solution.py:173
  531.3 28.8 %collective-permute-start.49 = (bf16[2,768,256]{2,1,0:T(8,128)(2,1)}, bf16[2,768,256]{2,1,0:T(8,128)(2,1)}, u32[]{:S(2)}, u32[]{:S(2)}) collective-permute-start(bf16[2,768,256]{2,1,0:T(8,128)(2,1)} %get-tuple-element.242), channel_id=1, source_target_pairs={{0,4},{1,5},{2,6},{3,7},{16,20},{17,21},{18,22},{19,23}} | collective-permute-start | bytes 2359304 | tf_op jit(solution)/shard_map/ppermute | solution.py:172
  582.9 24.7 %collective-permute-start.52 = (bf16[2,1,1,128,2048]{4,3,2,1,0:T(8,128)(2,1)}, bf16[2,1,1,128,2048]{4,3,2,1,0:T(8,128)(2,1)}, u32[]{:S(2)}, u32[]{:S(2)}) collective-permute-start(bf16[2,1,1,128,2048]{4,3,2,1,0:T(8,128)(2,1)} %get-tuple-element.210), channel_id=1, source_target_pairs={{0,2},{1,3},{2,0},{3,1},{4,6},{5,7},{6,4},{7,5},{8,10},{9,11},{10,... | collective-permute-start | bytes 3145736 | tf_op jit(solution)/shard_map/ppermute | solution.py:21
  589.8 25.8 %collective-permute-start.56 = (bf16[2,768,256]{2,1,0:T(8,128)(2,1)}, bf16[2,768,256]{2,1,0:T(8,128)(2,1)}, u32[]{:S(2)}, u32[]{:S(2)}) collective-permute-start(bf16[2,768,256]{2,1,0:T(8,128)(2,1)} %get-tuple-element.215), channel_id=1, source_target_pairs={{4,0},{8,4},{12,8},{5,1},{9,5},{13,9},{6,2},{10,6},{14,10},{7,3},{... | collective-permute-start | bytes 2359304 | tf_op jit(solution)/shard_map/ppermute | solution.py:173
  (42 other events, 466.9 us)
Sparse Core Ops, SparseCore 0:
  26.1 64.9 all-gather.3
  92.6 114.0 all-gather.7
  208.3 113.5 all-gather.5
  324.0 108.9 reduce-scatter.2
  435.2 119.5 reduce-scatter.4

commit v5 on v4

--- a/solution.py
+++ b/solution.py
@@ -149,63 +149,6 @@
     grad = start_scatter(grad)
     grad = grad.reshape(2, -1, grad.shape[-1])
     return lax.psum_scatter(grad, "row", scatter_dimension=1, tiled=True)
-
-
-class Chain:
-    def __init__(self, grad):
-        self.grad = start_scatter(grad)
-        self.rows = lax.axis_size("row")
-        self.step = 1
-        self.came = ()
-        far = self.rows - 1
-        self.send(self.block(far), self.block(-far))
-
-    def place(self, offset):
-        return jnp.clip(lax.axis_index("row") + offset, 0, self.rows - 1).astype(jnp.int32)
-
-    def block(self, offset):
-        return lax.dynamic_index_in_dim(self.grad, self.place(offset), 1, keepdims=False)
-
-    def send(self, up, down):
-        far = self.rows - self.step
-        self.came = (
-            lax.ppermute(up, "row", [(i, i + 1) for i in range(self.step)]),
-            lax.ppermute(down, "row", [(i, i - 1) for i in range(far, self.rows)]),
-        )
-
-    def advance(self, order):
-        self.step += 1
-        far = self.rows - self.step
-        places = jnp.stack((self.place(far), self.place(-far)))
-        _, _, n, d = self.grad.shape
-        part = pl.BlockSpec((1, n, d), lambda p, at: (p, 0, 0))
-
-        def picked(which):
-            return pl.BlockSpec((1, 1, n, d), lambda p, at: (p, at[which], 0, 0))
-
-        def kernel(at_ref, up_ref, down_ref, first_ref, second_ref, *out_refs):
-            if far:
-                out_refs[0][...] = add(first_ref[0], up_ref[...]).astype(BF)
-                out_refs[1][...] = add(second_ref[0], down_ref[...]).astype(BF)
-            else:
-                out_refs[0][...] = (add(first_ref[0], up_ref[...]) + down_ref[...].astype(F32)).astype(BF)
-
-        count = 2 if far else 1
-        outs = order.call(
-            "advance",
-            kernel,
-            (2,),
-            [part, part, picked(0), picked(1)],
-            [part] * count,
-            [shaped(2, n, d)] * count,
-            (places, *self.came, self.grad, self.grad),
-            prefetch=1,
-            moved=24 * n * d,
-        )
-        if far:
-            self.send(*outs)
-            return None
-        return outs[0]
 
 
 def sum_over_col(value):
@@ -931,7 +874,7 @@
     ffn_parts = [(ffn_grads[0], came)]
     out_parts = [(keep, item) for (keep, _), item in zip(out_sent, values)]
     attn_parts = [(behind[0][0], first_came), (behind[1][0], xchg(second_sent, "col", 1))]
-    scatter = Scatter(attn_parts, out_parts)
+    scatter, out_scatter = Scatter(attn_parts), Scatter(out_parts)
     scatter.first(order)
     attn_grads = weight_grads(
         [
@@ -942,18 +885,19 @@
         owners,
         order,
     )
-    chain = Chain(attn_grads)
+    out_scatter.first(order)
+    scatter.second(order)
+    attn_pair = scatter_weight(order.fence(attn_grads)[0])
     sent = for_partner(ffn_grads[1], low, order)
-    chain.advance(order)
+    out_scatter.second(order)
     (came,) = order.fence(xchg(sent, "dp", 1))
     ffn_parts.append((ffn_grads[1], came))
-    scatter.second(order)
-    chain.advance(order)
-    source_grad, result = finished(inputs, residual_grad, residual, scatter.terms(), order)
-    attn_pair = chain.advance(order)
-    attn_came = xchg(for_partner(attn_pair, low, order), "dp", 1)
     w1_grad, w3_grad, w2_grad, ffn_sum = finish_ffn(low, ffn_parts, w1, w3, w2, ffn_gain, order)
     ffn_sum = sum_over_col(ffn_sum)[0]
+    terms = scatter.terms() + out_scatter.terms()
+    sent = for_partner(attn_pair, low, order)
+    source_grad, result = finished(inputs, residual_grad, residual, terms, order)
+    attn_came = xchg(sent, "dp", 1)
     wqkv_grad, wo_grad, attn_sum = finish_attn(low, attn_pair, attn_came, wqkv, wo, attn_gain, order)
     attn_sum = sum_over_col(attn_sum)[0]
     return (

time: 652 us -> 643 us (0.986)
  waiting for transfers between devices: 260 us -> 277 us
  starting transfers between devices: 59 us -> 45.4 us
  Pallas kernels: 297 us -> 289 us
    ppermute x58 -> x62, waiting for transfers between devices: 226 us -> 245 us  [xchg(): return lax.ppermute(value, axis, [(i, i ^ bit) for i in range(size)])]
    ppermute x6 -> x0, starting transfers between devices: 19 us -> none  [the longest x3 14.6 us: send(): lax.ppermute(up, 'row', [(i, i + 1) for i in range(self.step)])]
    pallas_call x56, Pallas kernels: 297 us -> 289 us  [call(): pl.pallas_call(run, grid_spec=pltpu.PrefetchScalarGridSpec(num_scalar_pre...]
    ppermute x58 -> x62, starting transfers between devices: 38.9 us -> 44.3 us  [xchg(): return lax.ppermute(value, axis, [(i, i ^ bit) for i in range(size)])]
    reduce_scatter x2 -> x3, waiting for transfers between devices: 24.6 us -> 25.5 us  [scatter_weight(): return lax.psum_scatter(grad, 'row', scatter_dimension=1, tiled=True)]
  transfers between devices with their start and end apart: 69 -> 68, of which waited for: 43 -> 44; matrix products, arithmetic and copies ran while one was open for 2% -> 1% of each run, Pallas kernels for 44% -> 45%
where the time goes in v5:
time: 643 us; the launch traced here: 639 us
  Pallas kernels  289 us (45%)
  waiting for transfers between devices  277 us (43%)
  starting transfers between devices  45.4 us (7%)
  between operations  14.6 us (2%)
  other arithmetic  8.37 us (1%)
    pallas_call x56, Pallas kernels, call(): pl.pallas_call(run, grid_spec=pltpu.PrefetchScalarGridSpec(num_scalar_pre...  289 us
    ppermute x62, waiting for transfers between devices, xchg(): return lax.ppermute(value, axis, [(i, i ^ bit) for i in range(size)])  245 us
    ppermute x62, starting transfers between devices, xchg(): return lax.ppermute(value, axis, [(i, i ^ bit) for i in range(size)])  44.3 us
    reduce_scatter x3, waiting for transfers between devices, scatter_weight(): return lax.psum_scatter(grad, 'row', scatter_dimension=1, tiled=True)  25.5 us
  transfers between devices with their start and end apart: 68, of which 44 were waited for; matrix products, arithmetic and copies ran while one was open for 1% of the time, Pallas kernels for 45%

profile of v5, /device:TPU:0, one launch (start us, length us, event | category | flops | bytes accessed | tf_op | source)
XLA Modules:
  0.0 638.8 jit_solution(2653767616225886040)
XLA Ops:
  17.5 5.7 collective-permute-done.4.refs_2_
  30.0 22.1 %collective-permute-done.2.refs_1_ = bf16[256,2048]{1,0:T(8,128)(2,1)} collective-permute-done((bf16[256,2048]{1,0:T(8,128)(2,1)}, bf16[256,2048]{1,0:T(8,128)(2,1)}, u32[]{:S(2)}, u32[]{:S(2)}) %collective-permute-start.2) | collective-permute-done | bytes 1048608 | tf_op jit(solution)/shard_map/ppermute | solution.py:21
  66.6 13.4 %collective-permute-done.8.refs_3_ = bf16[256,1536]{1,0:T(8,128)(2,1)} collective-permute-done((bf16[256,1536]{1,0:T(8,128)(2,1)}, bf16[256,1536]{1,0:T(8,128)(2,1)}, u32[]{:S(2)}, u32[]{:S(2)}) %collective-permute-start.8) | collective-permute-done | bytes 786464 | tf_op jit(solution)/shard_map/ppermute | solution.py:21
  91.1 12.1 %attend.2 = (bf16[4,128,2048]{2,1,0:T(8,128)(2,1)}, bf16[4,128,2048]{2,1,0:T(8,128)(2,1)}, bf16[2,512,256]{2,1,0:T(8,128)(2,1)}, bf16[2,512,128]{2,1,0:T(8,128)(...) custom-call(s32[3]{0:T(128)} %get-tuple-element.248.refs_7_.refs_0_, bf16[256,2048]{1,0:T(8,128)(2,1)} %bitcast.117, ...), custom_call_target="tpu_custom_call" | custom-call | flops 4294967296 | bytes 11534336 | tf_op jit(solution)/shard_map/attend/pallas_call | solution.py:194
  103.2 12.1 %attend.3 = (bf16[4,128,2048]{2,1,0:T(8,128)(2,1)}, bf16[4,128,2048]{2,1,0:T(8,128)(2,1)}, bf16[2,512,256]{2,1,0:T(8,128)(2,1)}, bf16[2,512,128]{2,1,0:T(8,128)(...) custom-call(s32[3]{0:T(128)} %get-tuple-element.249.refs_8_.refs_0_, bf16[256,2048]{1,0:T(8,128)(2,1)} %bitcast.118, ...), custom_call_target="tpu_custom_call" | custom-call | flops 4294967296 | bytes 11534336 | tf_op jit(solution)/shard_map/attend/pallas_call | solution.py:194
  129.3 22.5 %collective-permute-done.14.refs_5_.refs_9_ = bf16[1,1,2,128,2048]{4,3,2,1,0:T(8,128)(2,1)} collective-permute-done((bf16[1,1,2,128,2048]{4,3,2,1,0:T(8,128)(2,1)}, bf16[1,1,2,128,2048]{4,3,2,1,0:T(8,128)(2,1)}, u32[]{:S(2)}, u32[]{:S(2)}) %collective-permute-start.14) | collective-permute-done | bytes 1048608 | tf_op jit(solution)/shard_map/ppermute | solution.py:21
  158.4 10.5 %collective-permute-done.16.refs_10_ = bf16[1,1,1,128,2048]{4,3,2,1,0:T(8,128)(2,1)} collective-permute-done((bf16[1,1,1,128,2048]{4,3,2,1,0:T(8,128)(2,1)}, bf16[1,1,1,128,2048]{4,3,2,1,0:T(8,128)(2,1)}, u32[]{:S(2)}, u32[]{:S(2)}) %collective-permute-start.16) | collective-permute-done | bytes 524320 | tf_op jit(solution)/shard_map/ppermute | solution.py:21
  180.3 43.9 %collective-permute-done.18.refs_1_ = bf16[512,2048]{1,0:T(8,128)(2,1)} collective-permute-done((bf16[512,2048]{1,0:T(8,128)(2,1)}, bf16[512,2048]{1,0:T(8,128)(2,1)}, u32[]{:S(2)}, u32[]{:S(2)}) %collective-permute-start.18) | collective-permute-done | bytes 2097184 | tf_op jit(solution)/shard_map/ppermute | solution.py:21
  230.7 23.4 %collective-permute-done.23.refs_3_ = bf16[256,2048]{1,0:T(8,128)(2,1)} collective-permute-done((bf16[256,2048]{1,0:T(8,128)(2,1)}, bf16[256,2048]{1,0:T(8,128)(2,1)}, u32[]{:S(2)}, u32[]{:S(2)}) %collective-permute-start.23) | collective-permute-done | bytes 1048608 | tf_op jit(solution)/shard_map/ppermute | solution.py:21
  259.9 20.0 %units.2 = (bf16[16,128,1024]{2,1,0:T(8,128)(2,1)}, bf16[16,128,512]{2,1,0:T(8,128)(2,1)}) custom-call(bf16[512,2048]{1,0:T(8,128)(2,1)} %bitcast.58, bf16[512,2048]{1,0:T(8,128)(2,1)} %get-tuple-element.142.refs_1_.refs_9_.refs_17_.refs_25_, bf16[512,2048]{1,0:T(8,128)(2,1)} %get-tuple-element.143.refs_1_.refs_2_.refs_10_.refs_18_.refs_26_, ...), custom_call_target="tpu_custom_call" | custom-call | flops 12884901888 | bytes 16777216 | tf_op jit(solution)/shard_map/units/pallas_call | solution.py:194
  279.9 13.7 %weight_grads.5.refs_17_ = bf16[8,1536,256]{2,1,0:T(8,128)(2,1)} custom-call(bf16[512,2048]{1,0:T(8,128)(2,1)} %bitcast.62, bf16[512,2048]{1,0:T(8,128)(2,1)} %get-tuple-element.142.refs_1_.refs_9_.refs_17_.refs_25_, bf16[512,2048]{1,0:T(8,128)(2,1)} %get-tuple-element.143.refs_1_.refs_2_.refs_10_.refs_18_.refs_26_, ...), custom_call_target="tpu_custom_call" | custom-call | flops 8589934592 | bytes 8388608 | tf_op jit(solution)/shard_map/weight_grads/pallas_call | solution.py:194
  293.6 8.9 %weight_grads.6.refs_2_ = bf16[8,1536,256]{2,1,0:T(8,128)(2,1)} custom-call(bf16[512,2048]{1,0:T(8,128)(2,1)} %bitcast.64, bf16[512,2048]{1,0:T(8,128)(2,1)} %get-tuple-element.142.refs_1_.refs_9_.refs_17_.refs_25_, bf16[512,2048]{1,0:T(8,128)(2,1)} %get-tuple-element.143.refs_1_.refs_2_.refs_10_.refs_18_.refs_26_, ...), custom_call_target="tpu_custom_call", output_to_operand_aliasing={{}: (17, {})} | custom-call | flops 4294967296 | bytes 8388608 | tf_op jit(solution)/shard_map/weight_grads/pallas_call | solution.py:194
  302.7 14.2 %back.5.refs_33_.refs_2_ = f32[2048,2048]{1,0:T(8,128)} custom-call(bf16[16,128,1024]{2,1,0:T(8,128)(2,1)} %get-tuple-element.153.refs_17_.refs_0_, bf16[2048,1536]{1,0:T(8,128)(2,1)} %bitcast.82, bf16[8,1536,256]{2,1,0:T(8,128)(2,1)} %weight_grads.6.refs_2_), custom_call_target="tpu_custom_call" | custom-call | flops 8589934592 | bytes 16777216 | tf_op jit(solution)/shard_map/back/pallas_call | solution.py:194
  321.9 20.0 %units.3 = (bf16[16,128,1024]{2,1,0:T(8,128)(2,1)}, bf16[16,128,512]{2,1,0:T(8,128)(2,1)}) custom-call(bf16[512,2048]{1,0:T(8,128)(2,1)} %bitcast.66, bf16[512,2048]{1,0:T(8,128)(2,1)} %get-tuple-element.142.refs_1_.refs_9_.refs_17_.refs_25_, bf16[512,2048]{1,0:T(8,128)(2,1)} %get-tuple-element.143.refs_1_.refs_2_.refs_10_.refs_18_.refs_26_, ...), custom_call_target="tpu_custom_call" | custom-call | flops 12884901888 | bytes 16777216 | tf_op jit(solution)/shard_map/units/pallas_call | solution.py:194
  341.9 9.8 %back.6 = (bf16[4,128,2048]{2,1,0:T(8,128)(2,1)}, bf16[4,128,2048]{2,1,0:T(8,128)(2,1)}) custom-call(bf16[16,128,1024]{2,1,0:T(8,128)(2,1)} %get-tuple-element.155.refs_0_, bf16[2048,1536]{1,0:T(8,128)(2,1)} %bitcast.76, f32[2048,2048]{1,0:T(8,128)} %back.5.refs_33_.refs_2_), custom_call_target="tpu_custom_call" | custom-call | flops 4294967296 | bytes 8388608 | tf_op jit(solution)/shard_map/back/pallas_call | solution.py:194
  351.8 9.8 %back.7 = (bf16[4,128,2048]{2,1,0:T(8,128)(2,1)}, bf16[4,128,2048]{2,1,0:T(8,128)(2,1)}) custom-call(bf16[16,128,1024]{2,1,0:T(8,128)(2,1)} %get-tuple-element.155.refs_0_, bf16[2048,1536]{1,0:T(8,128)(2,1)} %bitcast.77, f32[2048,2048]{1,0:T(8,128)} %back.5.refs_33_.refs_2_, bf16[4,128,2048]{2,1,0:T(8,128)(2,1)} %get-tuple-element.156.refs_3_), custom_call_target="tpu_custom_call" | custom-call | flops 4294967296 | bytes 8388608 | tf_op jit(solution)/shard_map/back/pallas_call | solution.py:194
  372.6 13.6 %weight_grads.7.refs_6_.refs_17_ = bf16[8,1536,256]{2,1,0:T(8,128)(2,1)} custom-call(bf16[512,2048]{1,0:T(8,128)(2,1)} %bitcast.70, bf16[512,2048]{1,0:T(8,128)(2,1)} %get-tuple-element.142.refs_1_.refs_9_.refs_17_.refs_25_, bf16[512,2048]{1,0:T(8,128)(2,1)} %get-tuple-element.143.refs_1_.refs_2_.refs_10_.refs_18_.refs_26_, ...), custom_call_target="tpu_custom_call" | custom-call | flops 8589934592 | bytes 8388608 | tf_op jit(solution)/shard_map/weight_grads/pallas_call | solution.py:194
  386.2 9.2 %collective-permute-done.29.refs_5_.refs_8_ = bf16[1,1,2,128,2048]{4,3,2,1,0:T(8,128)(2,1)} collective-permute-done((bf16[1,1,2,128,2048]{4,3,2,1,0:T(8,128)(2,1)}, bf16[1,1,2,128,2048]{4,3,2,1,0:T(8,128)(2,1)}, u32[]{:S(2)}, u32[]{:S(2)}) %collective-permute-start.29) | collective-permute-done | bytes 1048608 | tf_op jit(solution)/shard_map/ppermute | solution.py:21
  401.4 9.0 %weight_grads.8.refs_10_.refs_0_ = bf16[8,1536,256]{2,1,0:T(8,128)(2,1)} custom-call(bf16[512,2048]{1,0:T(8,128)(2,1)} %bitcast.72, bf16[512,2048]{1,0:T(8,128)(2,1)} %get-tuple-element.142.refs_1_.refs_9_.refs_17_.refs_25_, bf16[512,2048]{1,0:T(8,128)(2,1)} %get-tuple-element.143.refs_1_.refs_2_.refs_10_.refs_18_.refs_26_, ...), custom_call_target="tpu_custom_call", output_to_operand_aliasing={{}: (17, {})} | custom-call | flops 4294967296 | bytes 8388608 | tf_op jit(solution)/shard_map/weight_grads/pallas_call | solution.py:194
  414.0 5.8 by_rows.18
  421.2 8.6 %back.8 = (bf16[4,128,2048]{2,1,0:T(8,128)(2,1)}, bf16[4,128,2048]{2,1,0:T(8,128)(2,1)}) custom-call(bf16[16,128,512]{2,1,0:T(8,128)(2,1)} %get-tuple-element.154.refs_0_, bf16[16,128,512]{2,1,0:T(8,128)(2,1)} %get-tuple-element.166.refs_1_, bf16[2048,1536]{1,0:T(8,128)(2,1)} %bitcast.83, bf16[2048,1536]{1,0:T(8,128)(2,1)} %bitcast.78, ...), custom_call_target="tpu_custom_call" | custom-call | flops 4294967296 | bytes 8388608 | tf_op jit(solution)/shard_map/back/pallas_call | solution.py:194
  435.0 10.9 %collective-permute-done.33.refs_1_ = bf16[256,2048]{1,0:T(8,128)(2,1)} collective-permute-done((bf16[256,2048]{1,0:T(8,128)(2,1)}, bf16[256,2048]{1,0:T(8,128)(2,1)}, u32[]{:S(2)}, u32[]{:S(2)}) %collective-permute-start.33) | collective-permute-done | bytes 1048608 | tf_op jit(solution)/shard_map/ppermute | solution.py:21
  452.1 9.1 %back.9 = (bf16[4,128,2048]{2,1,0:T(8,128)(2,1)}, bf16[4,128,2048]{2,1,0:T(8,128)(2,1)}) custom-call(bf16[16,128,512]{2,1,0:T(8,128)(2,1)} %get-tuple-element.154.refs_0_, bf16[16,128,512]{2,1,0:T(8,128)(2,1)} %get-tuple-element.166.refs_1_, bf16[2048,1536]{1,0:T(8,128)(2,1)} %bitcast.84, bf16[2048,1536]{1,0:T(8,128)(2,1)} %bitcast.79, ...), custom_call_target="tpu_custom_call" | custom-call | flops 4294967296 | bytes 8388608 | tf_op jit(solution)/shard_map/back/pallas_call | solution.py:194
  469.0 14.7 %attend_back.2 = (bf16[4,128,2048]{2,1,0:T(8,128)(2,1)}, bf16[4,128,2048]{2,1,0:T(8,128)(2,1)}, bf16[2,512,512]{2,1,0:T(8,128)(2,1)}) custom-call(s32[3]{0:T(128)} %get-tuple-element.248.refs_7_.refs_0_, bf16[256,2048]{1,0:T(8,128)(2,1)} %bitcast.30.refs_1_.refs_16_.refs_24_, bf16[256,2048]{1,0:T(8,128)(2,1)} %get-tuple-element.170.refs_2_.refs_17_.refs_25_, ...), custom_call_target="tpu_custom_call" | custom-call | flops 4831838208 | bytes 11534336 | tf_op jit(solution)/shard_map/attend_back/pallas_call | solution.py:194
  484.4 14.9 %attend_back.3 = (bf16[4,128,2048]{2,1,0:T(8,128)(2,1)}, bf16[4,128,2048]{2,1,0:T(8,128)(2,1)}, bf16[2,512,512]{2,1,0:T(8,128)(2,1)}) custom-call(s32[3]{0:T(128)} %get-tuple-element.249.refs_8_.refs_0_, bf16[256,2048]{1,0:T(8,128)(2,1)} %bitcast.30.refs_1_.refs_16_.refs_24_, bf16[256,2048]{1,0:T(8,128)(2,1)} %get-tuple-element.170.refs_2_.refs_17_.refs_25_, ...), custom_call_target="tpu_custom_call" | custom-call | flops 4831838208 | bytes 11534336 | tf_op jit(solution)/shard_map/attend_back/pallas_call | solution.py:194
  513.1 12.4 %weight_grads.9.refs_4_.refs_0_ = bf16[8,768,256]{2,1,0:T(8,128)(2,1)} custom-call(bf16[256,2048]{1,0:T(8,128)(2,1)} %bitcast.119, bf16[256,2048]{1,0:T(8,128)(2,1)} %get-tuple-element.118.refs_2_.refs_1_.refs_9_, bf16[256,2048]{1,0:T(8,128)(2,1)} %get-tuple-element.119.refs_5_.refs_3_.refs_2_.refs_10_, ...), custom_call_target="tpu_custom_call" | custom-call | flops 6442450944 | bytes 16777216 | tf_op jit(solution)/shard_map/weight_grads/pallas_call | solution.py:194
  528.9 8.7 %collective-permute-done.47.refs_5_.refs_9_ = bf16[1,1,2,128,2048]{4,3,2,1,0:T(8,128)(2,1)} collective-permute-done((bf16[1,1,2,128,2048]{4,3,2,1,0:T(8,128)(2,1)}, bf16[1,1,2,128,2048]{4,3,2,1,0:T(8,128)(2,1)}, u32[]{:S(2)}, u32[]{:S(2)}) %collective-permute-start.47) | collective-permute-done | bytes 1048608 | tf_op jit(solution)/shard_map/ppermute | solution.py:21
  551.9 15.1 %collective-permute-done.51.refs_5_.refs_17_ = bf16[1,1,2,128,2048]{4,3,2,1,0:T(8,128)(2,1)} collective-permute-done((bf16[1,1,2,128,2048]{4,3,2,1,0:T(8,128)(2,1)}, bf16[1,1,2,128,2048]{4,3,2,1,0:T(8,128)(2,1)}, u32[]{:S(2)}, u32[]{:S(2)}) %collective-permute-start.51) | collective-permute-done | bytes 1048608 | tf_op jit(solution)/shard_map/ppermute | solution.py:21
  572.4 11.4 %collective-permute-done.54.refs_0_ = bf16[1536,256]{1,0:T(8,128)(2,1)} collective-permute-done((bf16[1536,256]{1,0:T(8,128)(2,1)}, bf16[1536,256]{1,0:T(8,128)(2,1)}, u32[]{:S(2)}, u32[]{:S(2)}) %collective-permute-start.54) | collective-permute-done | bytes 786464 | tf_op jit(solution)/shard_map/ppermute | solution.py:21
  583.9 7.0 %finish_ffn.1 = (f32[256,2048]{1,0:T(8,128)}, f32[256,2048]{1,0:T(8,128)}, f32[2048,256]{1,0:T(8,128)}, f32[1,256]{1,0:T(1,128)}) custom-call(s32[1]{0:T(128)} %bitcast.7.refs_0_, bf16[2,1536,256]{2,1,0:T(8,128)(2,1)} %reduce-scatter.4.cloned.1.call-done.refs_1_, bf16[2,1536,256]{2,1,0:T(8,128)(2,1)} %reduce-scatter.6.cloned.1.call-done.refs_1_.refs_2_, ...), custom_call_target="tpu_custom_call" | custom-call | bytes 12582912 | tf_op jit(solution)/shard_map/finish_ffn/pallas_call | solution.py:194
  590.8 18.6 %reduce-scatter.8.cloned.1.call-done.refs_1_ = bf16[2,768,256]{2,1,0:T(8,128)(2,1)} async-done(((bf16[2,3072,256]{2,1,0:T(8,128)(2,1)}), bf16[2,768,256]{2,1,0:T(8,128)(2,1)}) %reduce-scatter.8.cloned.1.call-update) | async-done | bytes 786448 | tf_op jit(solution)/shard_map/reduce_scatter | solution.py:151
  614.5 7.5 %by_rows.23 = (bf16[2,128,2048]{2,1,0:T(8,128)(2,1)}, bf16[2,128,2048]{2,1,0:T(8,128)(2,1)}) custom-call(bf16[2,128,2048]{2,1,0:T(8,128)(2,1)} %bitcast.123, f32[2,128,2048]{2,1,0:T(8,128)} %get-tuple-element.167.refs_1_, f32[2,128,2048]{2,1,0:T(8,128)} %get-tuple-element.140.refs_0_.refs_2_, bf16[2,2,128,2048]{3,2,1,0:T(8,128)(2,1)} %bitcast.108, ...), custom_call_target="tpu_custom_call" | custom-call | bytes 56623104 | tf_op jit(solution)/shard_map/by_rows/pallas_call | solution.py:194
  (191 shorter events, 185.6 us)
Async XLA Ops:
  7.2 83.9 %all-gather.4.cloned.1.call-start = ((), (), s32[]{:S(2)}) async-start(), calls=%async_computation.3 | async-start | bytes 3932160 | tf_op jit(solution)/shard_map/all_gather | solution.py:113
  26.0 233.9 %all-gather.8.cloned.1.call-start = ((), (), s32[]{:S(2)}) async-start(), calls=%async_computation.5 | async-start | bytes 7864320 | tf_op jit(solution)/shard_map/all_gather | solution.py:113
  26.1 25.9 %collective-permute-start.2 = (bf16[256,2048]{1,0:T(8,128)(2,1)}, bf16[256,2048]{1,0:T(8,128)(2,1)}, u32[]{:S(2)}, u32[]{:S(2)}) collective-permute-start(bf16[256,2048]{1,0:T(8,128)(2,1)} %bitcast.115), channel_id=1, source_target_pairs={{0,16},{16,0},{1,17},{17,1},{2,18},{18,2},{3,19},{19,3},{4,20},{20... | collective-permute-start | bytes 3145736 | tf_op jit(solution)/shard_map/ppermute | solution.py:21
  27.9 25.5 %collective-permute-start.1 = (bf16[256,2048]{1,0:T(8,128)(2,1)}, bf16[256,2048]{1,0:T(8,128)(2,1)}, u32[]{:S(2)}, u32[]{:S(2)}) collective-permute-start(bf16[256,2048]{1,0:T(8,128)(2,1)} %bitcast.116), channel_id=1, source_target_pairs={{0,2},{1,3},{2,0},{3,1},{4,6},{5,7},{6,4},{7,5},{8,10},{9,11},{10,... | collective-permute-start | bytes 3145736 | tf_op jit(solution)/shard_map/ppermute | solution.py:21
  29.4 33.3 %collective-permute-start = (s32[2,1]{0,1:T(1,128)S(1)}, s32[2,1]{0,1:T(1,128)S(1)}, u32[]{:S(2)}, u32[]{:S(2)}) collective-permute-start(s32[2,1]{0,1:T(1,128)S(1)} %copy-done.2), channel_id=1, source_target_pairs={{0,16},{16,0},{1,17},{17,1},{2,18},{18,2},{3,19},{19,3},{4,20},{20... | collective-permute-start | bytes 32 | tf_op jit(solution)/shard_map/ppermute | solution.py:21
  53.5 26.5 %collective-permute-start.7 = (bf16[256,2048]{1,0:T(8,128)(2,1)}, bf16[256,2048]{1,0:T(8,128)(2,1)}, u32[]{:S(2)}, u32[]{:S(2)}) collective-permute-start(bf16[256,2048]{1,0:T(8,128)(2,1)} %get-tuple-element.120.refs_5_.refs_4_.refs_12_), channel_id=1, source_target_pairs={{0,2},{1,3},{2,0},{3,1},{4,6},{5,7},{6,4},{7,5},{8,10},{9,11},{10,... | collective-permute-start | bytes 3145736 | tf_op jit(solution)/shard_map/ppermute | solution.py:21
  82.7 239.2 %all-gather.6.cloned.1.call-start = ((), (), s32[]{:S(2)}) async-start(), calls=%async_computation.4 | async-start | bytes 7864320 | tf_op jit(solution)/shard_map/all_gather | solution.py:113
  89.4 25.9 %collective-permute-start.10 = (bf16[256,1536]{1,0:T(8,128)(2,1)}, bf16[256,1536]{1,0:T(8,128)(2,1)}, u32[]{:S(2)}, u32[]{:S(2)}) collective-permute-start(bf16[256,1536]{1,0:T(8,128)(2,1)} %get-tuple-element.129), channel_id=1, source_target_pairs={{0,16},{16,0},{1,17},{17,1},{2,18},{18,2},{3,19},{19,3},{4,20},{20... | collective-permute-start | bytes 2359304 | tf_op jit(solution)/shard_map/ppermute | solution.py:21
  118.5 314.5 %reduce-scatter.4.cloned.1.call-start = ((), (), s32[]{:S(2)}) async-start(), calls=%async_computation.6 | async-start | bytes 7864320 | tf_op jit(solution)/shard_map/reduce_scatter | solution.py:151
  126.2 25.5 %collective-permute-start.14 = (bf16[1,1,2,128,2048]{4,3,2,1,0:T(8,128)(2,1)}, bf16[1,1,2,128,2048]{4,3,2,1,0:T(8,128)(2,1)}, u32[]{:S(2)}, u32[]{:S(2)}) collective-permute-start(bf16[1,1,2,128,2048]{4,3,2,1,0:T(8,128)(2,1)} %get-tuple-element.137), channel_id=1, source_target_pairs={{0,16},{16,0},{1,17},{17,1},{2,18},{18,2},{3,19},{19,3},{4,20},{20... | collective-permute-start | bytes 3145736 | tf_op jit(solution)/shard_map/ppermute | solution.py:21
  127.8 25.2 %collective-permute-start.13 = (bf16[1,2,1,128,2048]{4,3,2,1,0:T(8,128)(2,1)}, bf16[1,2,1,128,2048]{4,3,2,1,0:T(8,128)(2,1)}, u32[]{:S(2)}, u32[]{:S(2)}) collective-permute-start(bf16[1,2,1,128,2048]{4,3,2,1,0:T(8,128)(2,1)} %get-tuple-element.136.refs_6_), channel_id=1, source_target_pairs={{0,2},{1,3},{2,0},{3,1},{4,6},{5,7},{6,4},{7,5},{8,10},{9,11},{10,... | collective-permute-start | bytes 3145736 | tf_op jit(solution)/shard_map/ppermute | solution.py:21
  175.8 48.4 %collective-permute-start.18 = (bf16[512,2048]{1,0:T(8,128)(2,1)}, bf16[512,2048]{1,0:T(8,128)(2,1)}, u32[]{:S(2)}, u32[]{:S(2)}) collective-permute-start(bf16[512,2048]{1,0:T(8,128)(2,1)} %bitcast.56), channel_id=1, source_target_pairs={{0,16},{16,0},{1,17},{17,1},{2,18},{18,2},{3,19},{19,3},{4,20},{20... | collective-permute-start | bytes 6291464 | tf_op jit(solution)/shard_map/ppermute | solution.py:21
  176.5 48.0 %collective-permute-start.17 = (bf16[512,2048]{1,0:T(8,128)(2,1)}, bf16[512,2048]{1,0:T(8,128)(2,1)}, u32[]{:S(2)}, u32[]{:S(2)}) collective-permute-start(bf16[512,2048]{1,0:T(8,128)(2,1)} %bitcast.57), channel_id=1, source_target_pairs={{0,2},{1,3},{2,0},{3,1},{4,6},{5,7},{6,4},{7,5},{8,10},{9,11},{10,... | collective-permute-start | bytes 6291464 | tf_op jit(solution)/shard_map/ppermute | solution.py:21
  224.5 30.8 %collective-permute-start.20 = (bf16[512,2048]{1,0:T(8,128)(2,1)}, bf16[512,2048]{1,0:T(8,128)(2,1)}, u32[]{:S(2)}, u32[]{:S(2)}) collective-permute-start(bf16[512,2048]{1,0:T(8,128)(2,1)} %get-tuple-element.143.refs_1_.refs_2_.refs_10_.refs_18_.refs_26_), channel_id=1, source_target_pairs={{0,1},{1,0},{2,3},{3,2},{4,5},{5,4},{6,7},{7,6},{8,9},{9,8},{10,11... | collective-permute-start | bytes 6291464 | tf_op jit(solution)/shard_map/ppermute | solution.py:21
  224.5 30.8 %collective-permute-start.21 = (bf16[512,2048]{1,0:T(8,128)(2,1)}, bf16[512,2048]{1,0:T(8,128)(2,1)}, u32[]{:S(2)}, u32[]{:S(2)}) collective-permute-start(bf16[512,2048]{1,0:T(8,128)(2,1)} %get-tuple-element.144.refs_0_.refs_4_.refs_12_.refs_20_.refs_28_), channel_id=1, source_target_pairs={{0,1},{1,0},{2,3},{3,2},{4,5},{5,4},{6,7},{7,6},{8,9},{9,8},{10,11... | collective-permute-start | bytes 6291464 | tf_op jit(solution)/shard_map/ppermute | solution.py:21
  228.8 25.4 %collective-permute-start.23 = (bf16[256,2048]{1,0:T(8,128)(2,1)}, bf16[256,2048]{1,0:T(8,128)(2,1)}, u32[]{:S(2)}, u32[]{:S(2)}) collective-permute-start(bf16[256,2048]{1,0:T(8,128)(2,1)} %get-tuple-element.146), channel_id=1, source_target_pairs={{0,16},{16,0},{1,17},{17,1},{2,18},{18,2},{3,19},{19,3},{4,20},{20... | collective-permute-start | bytes 3145736 | tf_op jit(solution)/shard_map/ppermute | solution.py:21
  302.6 243.8 %reduce-scatter.6.cloned.1.call-start = ((), (), s32[]{:S(2)}) async-start(), calls=%async_computation.7 | async-start | bytes 7864320 | tf_op jit(solution)/shard_map/reduce_scatter | solution.py:151
  369.7 25.8 %collective-permute-start.29 = (bf16[1,1,2,128,2048]{4,3,2,1,0:T(8,128)(2,1)}, bf16[1,1,2,128,2048]{4,3,2,1,0:T(8,128)(2,1)}, u32[]{:S(2)}, u32[]{:S(2)}) collective-permute-start(bf16[1,1,2,128,2048]{4,3,2,1,0:T(8,128)(2,1)} %get-tuple-element.163), channel_id=1, source_target_pairs={{0,16},{16,0},{1,17},{17,1},{2,18},{18,2},{3,19},{19,3},{4,20},{20... | collective-permute-start | bytes 3145736 | tf_op jit(solution)/shard_map/ppermute | solution.py:21
  371.1 25.5 %collective-permute-start.28 = (bf16[1,2,1,128,2048]{4,3,2,1,0:T(8,128)(2,1)}, bf16[1,2,1,128,2048]{4,3,2,1,0:T(8,128)(2,1)}, u32[]{:S(2)}, u32[]{:S(2)}) collective-permute-start(bf16[1,2,1,128,2048]{4,3,2,1,0:T(8,128)(2,1)} %get-tuple-element.162.refs_17_), channel_id=1, source_target_pairs={{0,2},{1,3},{2,0},{3,1},{4,6},{5,7},{6,4},{7,5},{8,10},{9,11},{10,... | collective-permute-start | bytes 3145736 | tf_op jit(solution)/shard_map/ppermute | solution.py:21
  419.8 189.6 %reduce-scatter.8.cloned.1.call-start = ((), (), s32[]{:S(2)}) async-start(), calls=%async_computation.8 | async-start | bytes 3932160 | tf_op jit(solution)/shard_map/reduce_scatter | solution.py:151
  420.0 25.9 %collective-permute-start.33 = (bf16[256,2048]{1,0:T(8,128)(2,1)}, bf16[256,2048]{1,0:T(8,128)(2,1)}, u32[]{:S(2)}, u32[]{:S(2)}) collective-permute-start(bf16[256,2048]{1,0:T(8,128)(2,1)} %bitcast.30.refs_1_.refs_16_.refs_24_), channel_id=1, source_target_pairs={{0,16},{16,0},{1,17},{17,1},{2,18},{18,2},{3,19},{19,3},{4,20},{20... | collective-permute-start | bytes 3145736 | tf_op jit(solution)/shard_map/ppermute | solution.py:21
  420.6 25.5 %collective-permute-start.32 = (bf16[256,2048]{1,0:T(8,128)(2,1)}, bf16[256,2048]{1,0:T(8,128)(2,1)}, u32[]{:S(2)}, u32[]{:S(2)}) collective-permute-start(bf16[256,2048]{1,0:T(8,128)(2,1)} %bitcast.30.refs_1_.refs_16_.refs_24_), channel_id=1, source_target_pairs={{0,2},{1,3},{2,0},{3,1},{4,6},{5,7},{6,4},{7,5},{8,10},{9,11},{10,... | collective-permute-start | bytes 3145736 | tf_op jit(solution)/shard_map/ppermute | solution.py:21
  468.5 35.5 %collective-permute-start.43 = (bf16[4,128,2048]{2,1,0:T(8,128)(2,1)}, bf16[4,128,2048]{2,1,0:T(8,128)(2,1)}, u32[]{:S(2)}, u32[]{:S(2)}) collective-permute-start(bf16[4,128,2048]{2,1,0:T(8,128)(2,1)} %get-tuple-element.194), channel_id=1, source_target_pairs={{0,1},{1,0},{2,3},{3,2},{4,5},{5,4},{6,7},{7,6},{8,9},{9,8},{10,11... | collective-permute-start | bytes 6291464 | tf_op jit(solution)/shard_map/ppermute | solution.py:21
  468.6 35.4 %collective-permute-start.44 = (bf16[4,128,2048]{2,1,0:T(8,128)(2,1)}, bf16[4,128,2048]{2,1,0:T(8,128)(2,1)}, u32[]{:S(2)}, u32[]{:S(2)}) collective-permute-start(bf16[4,128,2048]{2,1,0:T(8,128)(2,1)} %get-tuple-element.195), channel_id=1, source_target_pairs={{0,1},{1,0},{2,3},{3,2},{4,5},{5,4},{6,7},{7,6},{8,9},{9,8},{10,11... | collective-permute-start | bytes 6291464 | tf_op jit(solution)/shard_map/ppermute | solution.py:21
  512.0 25.5 %collective-permute-start.47 = (bf16[1,1,2,128,2048]{4,3,2,1,0:T(8,128)(2,1)}, bf16[1,1,2,128,2048]{4,3,2,1,0:T(8,128)(2,1)}, u32[]{:S(2)}, u32[]{:S(2)}) collective-permute-start(bf16[1,1,2,128,2048]{4,3,2,1,0:T(8,128)(2,1)} %get-tuple-element.201), channel_id=1, source_target_pairs={{0,16},{16,0},{1,17},{17,1},{2,18},{18,2},{3,19},{19,3},{4,20},{20... | collective-permute-start | bytes 3145736 | tf_op jit(solution)/shard_map/ppermute | solution.py:21
  540.5 26.5 %collective-permute-start.51 = (bf16[1,1,2,128,2048]{4,3,2,1,0:T(8,128)(2,1)}, bf16[1,1,2,128,2048]{4,3,2,1,0:T(8,128)(2,1)}, u32[]{:S(2)}, u32[]{:S(2)}) collective-permute-start(bf16[1,1,2,128,2048]{4,3,2,1,0:T(8,128)(2,1)} %get-tuple-element.211), channel_id=1, source_target_pairs={{0,16},{16,0},{1,17},{17,1},{2,18},{18,2},{3,19},{19,3},{4,20},{20... | collective-permute-start | bytes 3145736 | tf_op jit(solution)/shard_map/ppermute | solution.py:21
  542.2 26.4 %collective-permute-start.50 = (bf16[1,2,1,128,2048]{4,3,2,1,0:T(8,128)(2,1)}, bf16[1,2,1,128,2048]{4,3,2,1,0:T(8,128)(2,1)}, u32[]{:S(2)}, u32[]{:S(2)}) collective-permute-start(bf16[1,2,1,128,2048]{4,3,2,1,0:T(8,128)(2,1)} %get-tuple-element.208.refs_6_), channel_id=1, source_target_pairs={{0,2},{1,3},{2,0},{3,1},{4,6},{5,7},{6,4},{7,5},{8,10},{9,11},{10,... | collective-permute-start | bytes 3145736 | tf_op jit(solution)/shard_map/ppermute | solution.py:21
  548.3 35.5 %collective-permute-start.54 = (bf16[1536,256]{1,0:T(8,128)(2,1)}, bf16[1536,256]{1,0:T(8,128)(2,1)}, u32[]{:S(2)}, u32[]{:S(2)}) collective-permute-start(bf16[1536,256]{1,0:T(8,128)(2,1)} %for_partner.4.refs_6_), channel_id=1, source_target_pairs={{0,16},{16,0},{1,17},{17,1},{2,18},{18,2},{3,19},{19,3},{4,20},{20... | collective-permute-start | bytes 2359304 | tf_op jit(solution)/shard_map/ppermute | solution.py:21
  549.8 63.3 %collective-permute-start.48 = (bf16[1,1,1,128,2048]{4,3,2,1,0:T(8,128)(2,1)}, bf16[1,1,1,128,2048]{4,3,2,1,0:T(8,128)(2,1)}, u32[]{:S(2)}, u32[]{:S(2)}) collective-permute-start(bf16[1,1,1,128,2048]{4,3,2,1,0:T(8,128)(2,1)} %get-tuple-element.209.refs_1_), channel_id=1, source_target_pairs={{0,16},{16,0},{1,17},{17,1},{2,18},{18,2},{3,19},{19,3},{4,20},{20... | collective-permute-start | bytes 1572872 | tf_op jit(solution)/shard_map/ppermute | solution.py:21
  550.4 62.3 %collective-permute-start.49 = (bf16[1,1,1,128,2048]{4,3,2,1,0:T(8,128)(2,1)}, bf16[1,1,1,128,2048]{4,3,2,1,0:T(8,128)(2,1)}, u32[]{:S(2)}, u32[]{:S(2)}) collective-permute-start(bf16[1,1,1,128,2048]{4,3,2,1,0:T(8,128)(2,1)} %get-tuple-element.210), channel_id=1, source_target_pairs={{0,2},{1,3},{2,0},{3,1},{4,6},{5,7},{6,4},{7,5},{8,10},{9,11},{10,... | collective-permute-start | bytes 1572872 | tf_op jit(solution)/shard_map/ppermute | solution.py:21
  571.3 42.9 %collective-permute-start.53 = (bf16[1,1,1,128,2048]{4,3,2,1,0:T(8,128)(2,1)}, bf16[1,1,1,128,2048]{4,3,2,1,0:T(8,128)(2,1)}, u32[]{:S(2)}, u32[]{:S(2)}) collective-permute-start(bf16[1,1,1,128,2048]{4,3,2,1,0:T(8,128)(2,1)} %get-tuple-element.213), channel_id=1, source_target_pairs={{0,2},{1,3},{2,0},{3,1},{4,6},{5,7},{6,4},{7,5},{8,10},{9,11},{10,... | collective-permute-start | bytes 1572872 | tf_op jit(solution)/shard_map/ppermute | solution.py:21
  571.9 42.6 %collective-permute-start.52 = (bf16[1,1,1,128,2048]{4,3,2,1,0:T(8,128)(2,1)}, bf16[1,1,1,128,2048]{4,3,2,1,0:T(8,128)(2,1)}, u32[]{:S(2)}, u32[]{:S(2)}) collective-permute-start(bf16[1,1,1,128,2048]{4,3,2,1,0:T(8,128)(2,1)} %get-tuple-element.212.refs_1_), channel_id=1, source_target_pairs={{0,16},{16,0},{1,17},{17,1},{2,18},{18,2},{3,19},{19,3},{4,20},{20... | collective-permute-start | bytes 1572872 | tf_op jit(solution)/shard_map/ppermute | solution.py:21
  (41 other events, 491.2 us)
Sparse Core Ops, SparseCore 0:
  26.1 64.9 all-gather.3
  92.7 114.0 all-gather.7
  208.3 113.5 all-gather.5
  324.0 108.9 reduce-scatter.3
  435.2 111.2 reduce-scatter.5
  548.6 60.7 reduce-scatter.7

commit v6 on v5

--- a/solution.py
+++ b/solution.py
@@ -11,7 +11,7 @@
 THETA = 1000000.0
 NEGATIVE = -1e30
 CHUNKS = 2
-VMEM = 127 * 2**19
+VMEM = 64 * 2**20
 BF = jnp.bfloat16
 F32 = jnp.float32
 
@@ -230,16 +230,16 @@
 SCALARS = pl.BlockSpec(memory_space=pltpu.SMEM)
 
 
-def prepare_attn_kernel(low_ref, qkv_ref, out_ref, gain_ref, mine_ref, sent_ref):
+def prepare_attn_kernel(part_ref, qkv_ref, out_ref, gain_ref, half_ref):
     wide = qkv_ref.shape[1] // 2
     tall = out_ref.shape[0] // 2
-    for part, ref in ((low_ref[0], mine_ref), (1 - low_ref[0], sent_ref)):
-        columns = qkv_ref[:, pl.ds(pl.multiple_of(part * wide, wide), wide)]
-        ref[:, :wide] = (columns.astype(F32) * gain_ref[...]).astype(BF)
-        ref[:, wide:] = out_ref[pl.ds(pl.multiple_of(part * tall, tall), tall), :].T
-
-
-def prepare_attn(low, wqkv, wo, gain, order):
+    part = part_ref[0]
+    columns = qkv_ref[:, pl.ds(pl.multiple_of(part * wide, wide), wide)]
+    half_ref[:, :wide] = (columns.astype(F32) * gain_ref[...]).astype(BF)
+    half_ref[:, wide:] = out_ref[pl.ds(pl.multiple_of(part * tall, tall), tall), :].T
+
+
+def prepare_attn(part, wqkv, wo, gain, order):
     d = wqkv.shape[0]
     out = shaped(d, wqkv.shape[1] // 2 + wo.shape[0] // 2)
     return order.call(
@@ -247,10 +247,10 @@
         prepare_attn_kernel,
         (1,),
         [SCALARS] + [whole(item.shape) for item in (wqkv, wo, gain)],
-        [whole(out.shape)] * 2,
-        [out, out],
-        (low, wqkv, wo, gain),
-        moved=4 * (wqkv.size + wo.size),
+        whole(out.shape),
+        out,
+        (part, wqkv, wo, gain),
+        moved=2 * (wqkv.size + wo.size),
     )
 
 
@@ -790,9 +790,10 @@
     ]
     own_scalars = jnp.concatenate(((me * rows).astype(jnp.int32)[None], lengths.reshape(micro)))
 
-    mine, sent = prepare_attn(low, wqkv, wo, attn_gain, order)
+    came = xchg(prepare_attn(1 - low, wqkv, wo, attn_gain, order), "dp", 1)
+    mine = prepare_attn(low, wqkv, wo, attn_gain, order)
     normed1 = first_norm(inputs, order)
-    attn_w = gather_weight(mine, xchg(sent, "dp", 1), low, order)
+    attn_w = gather_weight(mine, came, low, order)
     attn_gather = Gather(normed1.reshape(-1, width), rows, False)
     attn_gather.cross(order)
     ((mine, sent),) = prepared(0)

time: 643 us -> 641 us (level)
  waiting for transfers between devices: 277 us -> 270 us
    pallas_call x56 -> x57, Pallas kernels: 289 us -> 291 us  [call(): pl.pallas_call(run, grid_spec=pltpu.PrefetchScalarGridSpec(num_scalar_pre...]
  transfers between devices with their start and end apart: 68 -> 68, of which waited for: 44 -> 43; matrix products, arithmetic and copies ran while one was open for 1% -> 2% of each run, Pallas kernels for 45% -> 45%
where the time goes in v6:
time: 641 us; the launch traced here: 637 us
  Pallas kernels  291 us (45%)
  waiting for transfers between devices  270 us (42%)
  starting transfers between devices  45.1 us (7%)
  between operations  14.6 us (2%)
  other arithmetic  12.7 us (2%)
    pallas_call x57, Pallas kernels, call(): pl.pallas_call(run, grid_spec=pltpu.PrefetchScalarGridSpec(num_scalar_pre...  291 us
    ppermute x62, waiting for transfers between devices, xchg(): return lax.ppermute(value, axis, [(i, i ^ bit) for i in range(size)])  239 us
    ppermute x62, starting transfers between devices, xchg(): return lax.ppermute(value, axis, [(i, i ^ bit) for i in range(size)])  44 us
    reduce_scatter x3, waiting for transfers between devices, scatter_weight(): return lax.psum_scatter(grad, 'row', scatter_dimension=1, tiled=True)  25.6 us
  transfers between devices with their start and end apart: 68, of which 43 were waited for; matrix products, arithmetic and copies ran while one was open for 2% of the time, Pallas kernels for 45%

profile of v6, /device:TPU:0, one launch (start us, length us, event | category | flops | bytes accessed | tf_op | source)
XLA Modules:
  0.0 637.3 jit_solution(17275446894268456316)
XLA Ops:
  29.1 22.1 %collective-permute-done.2.refs_1_ = bf16[256,2048]{1,0:T(8,128)(2,1)} collective-permute-done((bf16[256,2048]{1,0:T(8,128)(2,1)}, bf16[256,2048]{1,0:T(8,128)(2,1)}, u32[]{:S(2)}, u32[]{:S(2)}) %collective-permute-start.2) | collective-permute-done | bytes 1048608 | tf_op jit(solution)/shard_map/ppermute | solution.py:21
  70.2 11.3 %collective-permute-done.8.refs_3_ = bf16[256,1536]{1,0:T(8,128)(2,1)} collective-permute-done((bf16[256,1536]{1,0:T(8,128)(2,1)}, bf16[256,1536]{1,0:T(8,128)(2,1)}, u32[]{:S(2)}, u32[]{:S(2)}) %collective-permute-start.8) | collective-permute-done | bytes 786464 | tf_op jit(solution)/shard_map/ppermute | solution.py:21
  91.4 12.1 %attend.2 = (bf16[4,128,2048]{2,1,0:T(8,128)(2,1)}, bf16[4,128,2048]{2,1,0:T(8,128)(2,1)}, bf16[2,512,256]{2,1,0:T(8,128)(2,1)}, bf16[2,512,128]{2,1,0:T(8,128)(...) custom-call(s32[3]{0:T(128)} %get-tuple-element.244.refs_7_.refs_0_, bf16[256,2048]{1,0:T(8,128)(2,1)} %bitcast.117, ...), custom_call_target="tpu_custom_call" | custom-call | flops 4294967296 | bytes 11534336 | tf_op jit(solution)/shard_map/attend/pallas_call | solution.py:194
  103.5 12.1 %attend.3 = (bf16[4,128,2048]{2,1,0:T(8,128)(2,1)}, bf16[4,128,2048]{2,1,0:T(8,128)(2,1)}, bf16[2,512,256]{2,1,0:T(8,128)(2,1)}, bf16[2,512,128]{2,1,0:T(8,128)(...) custom-call(s32[3]{0:T(128)} %get-tuple-element.245.refs_8_.refs_0_, bf16[256,2048]{1,0:T(8,128)(2,1)} %bitcast.118, ...), custom_call_target="tpu_custom_call" | custom-call | flops 4294967296 | bytes 11534336 | tf_op jit(solution)/shard_map/attend/pallas_call | solution.py:194
  128.7 23.4 %collective-permute-done.14.refs_5_.refs_9_ = bf16[1,1,2,128,2048]{4,3,2,1,0:T(8,128)(2,1)} collective-permute-done((bf16[1,1,2,128,2048]{4,3,2,1,0:T(8,128)(2,1)}, bf16[1,1,2,128,2048]{4,3,2,1,0:T(8,128)(2,1)}, u32[]{:S(2)}, u32[]{:S(2)}) %collective-permute-start.14) | collective-permute-done | bytes 1048608 | tf_op jit(solution)/shard_map/ppermute | solution.py:21
  158.2 11.0 %collective-permute-done.16.refs_10_ = bf16[1,1,1,128,2048]{4,3,2,1,0:T(8,128)(2,1)} collective-permute-done((bf16[1,1,1,128,2048]{4,3,2,1,0:T(8,128)(2,1)}, bf16[1,1,1,128,2048]{4,3,2,1,0:T(8,128)(2,1)}, u32[]{:S(2)}, u32[]{:S(2)}) %collective-permute-start.16) | collective-permute-done | bytes 524320 | tf_op jit(solution)/shard_map/ppermute | solution.py:21
  169.5 5.7 by_rows.15
  179.7 43.9 %collective-permute-done.18.refs_1_ = bf16[512,2048]{1,0:T(8,128)(2,1)} collective-permute-done((bf16[512,2048]{1,0:T(8,128)(2,1)}, bf16[512,2048]{1,0:T(8,128)(2,1)}, u32[]{:S(2)}, u32[]{:S(2)}) %collective-permute-start.18) | collective-permute-done | bytes 2097184 | tf_op jit(solution)/shard_map/ppermute | solution.py:21
  231.0 22.5 %collective-permute-done.23.refs_3_ = bf16[256,2048]{1,0:T(8,128)(2,1)} collective-permute-done((bf16[256,2048]{1,0:T(8,128)(2,1)}, bf16[256,2048]{1,0:T(8,128)(2,1)}, u32[]{:S(2)}, u32[]{:S(2)}) %collective-permute-start.23) | collective-permute-done | bytes 1048608 | tf_op jit(solution)/shard_map/ppermute | solution.py:21
  259.3 20.0 %units.2 = (bf16[16,128,1024]{2,1,0:T(8,128)(2,1)}, bf16[16,128,512]{2,1,0:T(8,128)(2,1)}) custom-call(bf16[512,2048]{1,0:T(8,128)(2,1)} %bitcast.58, bf16[512,2048]{1,0:T(8,128)(2,1)} %get-tuple-element.138.refs_1_.refs_9_.refs_17_.refs_25_, bf16[512,2048]{1,0:T(8,128)(2,1)} %get-tuple-element.139.refs_1_.refs_2_.refs_10_.refs_18_.refs_26_, ...), custom_call_target="tpu_custom_call" | custom-call | flops 12884901888 | bytes 16777216 | tf_op jit(solution)/shard_map/units/pallas_call | solution.py:194
  279.3 13.7 %weight_grads.5.refs_17_ = bf16[8,1536,256]{2,1,0:T(8,128)(2,1)} custom-call(bf16[512,2048]{1,0:T(8,128)(2,1)} %bitcast.62, bf16[512,2048]{1,0:T(8,128)(2,1)} %get-tuple-element.138.refs_1_.refs_9_.refs_17_.refs_25_, bf16[512,2048]{1,0:T(8,128)(2,1)} %get-tuple-element.139.refs_1_.refs_2_.refs_10_.refs_18_.refs_26_, ...), custom_call_target="tpu_custom_call" | custom-call | flops 8589934592 | bytes 8388608 | tf_op jit(solution)/shard_map/weight_grads/pallas_call | solution.py:194
  293.0 8.9 %weight_grads.6.refs_2_ = bf16[8,1536,256]{2,1,0:T(8,128)(2,1)} custom-call(bf16[512,2048]{1,0:T(8,128)(2,1)} %bitcast.64, bf16[512,2048]{1,0:T(8,128)(2,1)} %get-tuple-element.138.refs_1_.refs_9_.refs_17_.refs_25_, bf16[512,2048]{1,0:T(8,128)(2,1)} %get-tuple-element.139.refs_1_.refs_2_.refs_10_.refs_18_.refs_26_, ...), custom_call_target="tpu_custom_call", output_to_operand_aliasing={{}: (17, {})} | custom-call | flops 4294967296 | bytes 8388608 | tf_op jit(solution)/shard_map/weight_grads/pallas_call | solution.py:194
  302.0 14.2 %back.5.refs_33_.refs_2_ = f32[2048,2048]{1,0:T(8,128)} custom-call(bf16[16,128,1024]{2,1,0:T(8,128)(2,1)} %get-tuple-element.149.refs_17_.refs_0_, bf16[2048,1536]{1,0:T(8,128)(2,1)} %bitcast.82, bf16[8,1536,256]{2,1,0:T(8,128)(2,1)} %weight_grads.6.refs_2_), custom_call_target="tpu_custom_call" | custom-call | flops 8589934592 | bytes 16777216 | tf_op jit(solution)/shard_map/back/pallas_call | solution.py:194
  321.1 20.0 %units.3 = (bf16[16,128,1024]{2,1,0:T(8,128)(2,1)}, bf16[16,128,512]{2,1,0:T(8,128)(2,1)}) custom-call(bf16[512,2048]{1,0:T(8,128)(2,1)} %bitcast.66, bf16[512,2048]{1,0:T(8,128)(2,1)} %get-tuple-element.138.refs_1_.refs_9_.refs_17_.refs_25_, bf16[512,2048]{1,0:T(8,128)(2,1)} %get-tuple-element.139.refs_1_.refs_2_.refs_10_.refs_18_.refs_26_, ...), custom_call_target="tpu_custom_call" | custom-call | flops 12884901888 | bytes 16777216 | tf_op jit(solution)/shard_map/units/pallas_call | solution.py:194
  341.1 9.8 %back.6 = (bf16[4,128,2048]{2,1,0:T(8,128)(2,1)}, bf16[4,128,2048]{2,1,0:T(8,128)(2,1)}) custom-call(bf16[16,128,1024]{2,1,0:T(8,128)(2,1)} %get-tuple-element.151.refs_0_, bf16[2048,1536]{1,0:T(8,128)(2,1)} %bitcast.76, f32[2048,2048]{1,0:T(8,128)} %back.5.refs_33_.refs_2_), custom_call_target="tpu_custom_call" | custom-call | flops 4294967296 | bytes 8388608 | tf_op jit(solution)/shard_map/back/pallas_call | solution.py:194
  351.0 9.8 %back.7 = (bf16[4,128,2048]{2,1,0:T(8,128)(2,1)}, bf16[4,128,2048]{2,1,0:T(8,128)(2,1)}) custom-call(bf16[16,128,1024]{2,1,0:T(8,128)(2,1)} %get-tuple-element.151.refs_0_, bf16[2048,1536]{1,0:T(8,128)(2,1)} %bitcast.77, f32[2048,2048]{1,0:T(8,128)} %back.5.refs_33_.refs_2_, bf16[4,128,2048]{2,1,0:T(8,128)(2,1)} %get-tuple-element.152.refs_3_), custom_call_target="tpu_custom_call" | custom-call | flops 4294967296 | bytes 8388608 | tf_op jit(solution)/shard_map/back/pallas_call | solution.py:194
  371.8 13.6 %weight_grads.7.refs_6_.refs_17_ = bf16[8,1536,256]{2,1,0:T(8,128)(2,1)} custom-call(bf16[512,2048]{1,0:T(8,128)(2,1)} %bitcast.70, bf16[512,2048]{1,0:T(8,128)(2,1)} %get-tuple-element.138.refs_1_.refs_9_.refs_17_.refs_25_, bf16[512,2048]{1,0:T(8,128)(2,1)} %get-tuple-element.139.refs_1_.refs_2_.refs_10_.refs_18_.refs_26_, ...), custom_call_target="tpu_custom_call" | custom-call | flops 8589934592 | bytes 8388608 | tf_op jit(solution)/shard_map/weight_grads/pallas_call | solution.py:194
  385.4 9.2 %collective-permute-done.29.refs_5_.refs_8_ = bf16[1,1,2,128,2048]{4,3,2,1,0:T(8,128)(2,1)} collective-permute-done((bf16[1,1,2,128,2048]{4,3,2,1,0:T(8,128)(2,1)}, bf16[1,1,2,128,2048]{4,3,2,1,0:T(8,128)(2,1)}, u32[]{:S(2)}, u32[]{:S(2)}) %collective-permute-start.29) | collective-permute-done | bytes 1048608 | tf_op jit(solution)/shard_map/ppermute | solution.py:21
  400.6 9.0 %weight_grads.8.refs_10_.refs_0_ = bf16[8,1536,256]{2,1,0:T(8,128)(2,1)} custom-call(bf16[512,2048]{1,0:T(8,128)(2,1)} %bitcast.72, bf16[512,2048]{1,0:T(8,128)(2,1)} %get-tuple-element.138.refs_1_.refs_9_.refs_17_.refs_25_, bf16[512,2048]{1,0:T(8,128)(2,1)} %get-tuple-element.139.refs_1_.refs_2_.refs_10_.refs_18_.refs_26_, ...), custom_call_target="tpu_custom_call", output_to_operand_aliasing={{}: (17, {})} | custom-call | flops 4294967296 | bytes 8388608 | tf_op jit(solution)/shard_map/weight_grads/pallas_call | solution.py:194
  413.2 5.8 by_rows.18
  420.3 8.6 %back.8 = (bf16[4,128,2048]{2,1,0:T(8,128)(2,1)}, bf16[4,128,2048]{2,1,0:T(8,128)(2,1)}) custom-call(bf16[16,128,512]{2,1,0:T(8,128)(2,1)} %get-tuple-element.150.refs_0_, bf16[16,128,512]{2,1,0:T(8,128)(2,1)} %get-tuple-element.162.refs_1_, bf16[2048,1536]{1,0:T(8,128)(2,1)} %bitcast.83, bf16[2048,1536]{1,0:T(8,128)(2,1)} %bitcast.78, ...), custom_call_target="tpu_custom_call" | custom-call | flops 4294967296 | bytes 8388608 | tf_op jit(solution)/shard_map/back/pallas_call | solution.py:194
  434.2 10.9 %collective-permute-done.33.refs_1_ = bf16[256,2048]{1,0:T(8,128)(2,1)} collective-permute-done((bf16[256,2048]{1,0:T(8,128)(2,1)}, bf16[256,2048]{1,0:T(8,128)(2,1)}, u32[]{:S(2)}, u32[]{:S(2)}) %collective-permute-start.33) | collective-permute-done | bytes 1048608 | tf_op jit(solution)/shard_map/ppermute | solution.py:21
  451.3 9.2 %back.9 = (bf16[4,128,2048]{2,1,0:T(8,128)(2,1)}, bf16[4,128,2048]{2,1,0:T(8,128)(2,1)}) custom-call(bf16[16,128,512]{2,1,0:T(8,128)(2,1)} %get-tuple-element.150.refs_0_, bf16[16,128,512]{2,1,0:T(8,128)(2,1)} %get-tuple-element.162.refs_1_, bf16[2048,1536]{1,0:T(8,128)(2,1)} %bitcast.84, bf16[2048,1536]{1,0:T(8,128)(2,1)} %bitcast.79, ...), custom_call_target="tpu_custom_call" | custom-call | flops 4294967296 | bytes 8388608 | tf_op jit(solution)/shard_map/back/pallas_call | solution.py:194
  468.1 14.7 %attend_back.2 = (bf16[4,128,2048]{2,1,0:T(8,128)(2,1)}, bf16[4,128,2048]{2,1,0:T(8,128)(2,1)}, bf16[2,512,512]{2,1,0:T(8,128)(2,1)}) custom-call(s32[3]{0:T(128)} %get-tuple-element.244.refs_7_.refs_0_, bf16[256,2048]{1,0:T(8,128)(2,1)} %bitcast.30.refs_1_.refs_16_.refs_24_, bf16[256,2048]{1,0:T(8,128)(2,1)} %get-tuple-element.166.refs_2_.refs_17_.refs_25_, ...), custom_call_target="tpu_custom_call" | custom-call | flops 4831838208 | bytes 11534336 | tf_op jit(solution)/shard_map/attend_back/pallas_call | solution.py:194
  483.6 14.9 %attend_back.3 = (bf16[4,128,2048]{2,1,0:T(8,128)(2,1)}, bf16[4,128,2048]{2,1,0:T(8,128)(2,1)}, bf16[2,512,512]{2,1,0:T(8,128)(2,1)}) custom-call(s32[3]{0:T(128)} %get-tuple-element.245.refs_8_.refs_0_, bf16[256,2048]{1,0:T(8,128)(2,1)} %bitcast.30.refs_1_.refs_16_.refs_24_, bf16[256,2048]{1,0:T(8,128)(2,1)} %get-tuple-element.166.refs_2_.refs_17_.refs_25_, ...), custom_call_target="tpu_custom_call" | custom-call | flops 4831838208 | bytes 11534336 | tf_op jit(solution)/shard_map/attend_back/pallas_call | solution.py:194
  512.2 12.4 %weight_grads.9.refs_4_.refs_0_ = bf16[8,768,256]{2,1,0:T(8,128)(2,1)} custom-call(bf16[256,2048]{1,0:T(8,128)(2,1)} %bitcast.119, bf16[256,2048]{1,0:T(8,128)(2,1)} %get-tuple-element.114.refs_2_.refs_1_.refs_9_, bf16[256,2048]{1,0:T(8,128)(2,1)} %get-tuple-element.115.refs_5_.refs_3_.refs_2_.refs_10_, ...), custom_call_target="tpu_custom_call" | custom-call | flops 6442450944 | bytes 16777216 | tf_op jit(solution)/shard_map/weight_grads/pallas_call | solution.py:194
  528.0 8.7 %collective-permute-done.47.refs_5_.refs_9_ = bf16[1,1,2,128,2048]{4,3,2,1,0:T(8,128)(2,1)} collective-permute-done((bf16[1,1,2,128,2048]{4,3,2,1,0:T(8,128)(2,1)}, bf16[1,1,2,128,2048]{4,3,2,1,0:T(8,128)(2,1)}, u32[]{:S(2)}, u32[]{:S(2)}) %collective-permute-start.47) | collective-permute-done | bytes 1048608 | tf_op jit(solution)/shard_map/ppermute | solution.py:21
  551.1 15.1 %collective-permute-done.51.refs_5_.refs_17_ = bf16[1,1,2,128,2048]{4,3,2,1,0:T(8,128)(2,1)} collective-permute-done((bf16[1,1,2,128,2048]{4,3,2,1,0:T(8,128)(2,1)}, bf16[1,1,2,128,2048]{4,3,2,1,0:T(8,128)(2,1)}, u32[]{:S(2)}, u32[]{:S(2)}) %collective-permute-start.51) | collective-permute-done | bytes 1048608 | tf_op jit(solution)/shard_map/ppermute | solution.py:21
  571.5 11.5 %collective-permute-done.54.refs_0_ = bf16[1536,256]{1,0:T(8,128)(2,1)} collective-permute-done((bf16[1536,256]{1,0:T(8,128)(2,1)}, bf16[1536,256]{1,0:T(8,128)(2,1)}, u32[]{:S(2)}, u32[]{:S(2)}) %collective-permute-start.54) | collective-permute-done | bytes 786464 | tf_op jit(solution)/shard_map/ppermute | solution.py:21
  583.0 7.0 %finish_ffn.1 = (f32[256,2048]{1,0:T(8,128)}, f32[256,2048]{1,0:T(8,128)}, f32[2048,256]{1,0:T(8,128)}, f32[1,256]{1,0:T(1,128)}) custom-call(s32[1]{0:T(128)} %bitcast.7.refs_0_, bf16[2,1536,256]{2,1,0:T(8,128)(2,1)} %reduce-scatter.4.cloned.1.call-done.refs_1_, bf16[2,1536,256]{2,1,0:T(8,128)(2,1)} %reduce-scatter.6.cloned.1.call-done.refs_1_.refs_2_, ...), custom_call_target="tpu_custom_call" | custom-call | bytes 12582912 | tf_op jit(solution)/shard_map/finish_ffn/pallas_call | solution.py:194
  590.0 18.6 %reduce-scatter.8.cloned.1.call-done.refs_1_ = bf16[2,768,256]{2,1,0:T(8,128)(2,1)} async-done(((bf16[2,3072,256]{2,1,0:T(8,128)(2,1)}), bf16[2,768,256]{2,1,0:T(8,128)(2,1)}) %reduce-scatter.8.cloned.1.call-update) | async-done | bytes 786448 | tf_op jit(solution)/shard_map/reduce_scatter | solution.py:151
  613.7 7.5 %by_rows.23 = (bf16[2,128,2048]{2,1,0:T(8,128)(2,1)}, bf16[2,128,2048]{2,1,0:T(8,128)(2,1)}) custom-call(bf16[2,128,2048]{2,1,0:T(8,128)(2,1)} %bitcast.123, f32[2,128,2048]{2,1,0:T(8,128)} %get-tuple-element.163.refs_1_, f32[2,128,2048]{2,1,0:T(8,128)} %get-tuple-element.136.refs_0_.refs_2_, bf16[2,2,128,2048]{3,2,1,0:T(8,128)(2,1)} %bitcast.108, ...), custom_call_target="tpu_custom_call" | custom-call | bytes 56623104 | tf_op jit(solution)/shard_map/by_rows/pallas_call | solution.py:194
  (182 shorter events, 185.4 us)
Async XLA Ops:
  7.2 84.3 %all-gather.4.cloned.1.call-start = ((), (), s32[]{:S(2)}) async-start(), calls=%async_computation.3 | async-start | bytes 3932160 | tf_op jit(solution)/shard_map/all_gather | solution.py:113
  25.2 234.1 %all-gather.8.cloned.1.call-start = ((), (), s32[]{:S(2)}) async-start(), calls=%async_computation.5 | async-start | bytes 7864320 | tf_op jit(solution)/shard_map/all_gather | solution.py:113
  25.3 25.9 %collective-permute-start.2 = (bf16[256,2048]{1,0:T(8,128)(2,1)}, bf16[256,2048]{1,0:T(8,128)(2,1)}, u32[]{:S(2)}, u32[]{:S(2)}) collective-permute-start(bf16[256,2048]{1,0:T(8,128)(2,1)} %bitcast.115), channel_id=1, source_target_pairs={{0,16},{16,0},{1,17},{17,1},{2,18},{18,2},{3,19},{19,3},{4,20},{20... | collective-permute-start | bytes 3145736 | tf_op jit(solution)/shard_map/ppermute | solution.py:21
  27.1 25.5 %collective-permute-start.1 = (bf16[256,2048]{1,0:T(8,128)(2,1)}, bf16[256,2048]{1,0:T(8,128)(2,1)}, u32[]{:S(2)}, u32[]{:S(2)}) collective-permute-start(bf16[256,2048]{1,0:T(8,128)(2,1)} %bitcast.116), channel_id=1, source_target_pairs={{0,2},{1,3},{2,0},{3,1},{4,6},{5,7},{6,4},{7,5},{8,10},{9,11},{10,... | collective-permute-start | bytes 3145736 | tf_op jit(solution)/shard_map/ppermute | solution.py:21
  28.6 37.0 %collective-permute-start = (s32[2,1]{0,1:T(1,128)}, s32[2,1]{0,1:T(1,128)}, u32[]{:S(2)}, u32[]{:S(2)}) collective-permute-start(s32[2,1]{0,1:T(1,128)} %param.11), channel_id=1, source_target_pairs={{0,16},{16,0},{1,17},{17,1},{2,18},{18,2},{3,19},{19,3},{4,20},{20... | collective-permute-start | bytes 32 | tf_op jit(solution)/shard_map/ppermute | solution.py:21
  52.7 28.8 %collective-permute-start.7 = (bf16[256,2048]{1,0:T(8,128)(2,1)}, bf16[256,2048]{1,0:T(8,128)(2,1)}, u32[]{:S(2)}, u32[]{:S(2)}) collective-permute-start(bf16[256,2048]{1,0:T(8,128)(2,1)} %get-tuple-element.116.refs_5_.refs_4_.refs_12_), channel_id=1, source_target_pairs={{0,2},{1,3},{2,0},{3,1},{4,6},{5,7},{6,4},{7,5},{8,10},{9,11},{10,... | collective-permute-start | bytes 3145736 | tf_op jit(solution)/shard_map/ppermute | solution.py:21
  54.2 27.4 %collective-permute-start.6 = (bf16[256,2048]{1,0:T(8,128)(2,1)}, bf16[256,2048]{1,0:T(8,128)(2,1)}, u32[]{:S(2)}, u32[]{:S(2)}) collective-permute-start(bf16[256,2048]{1,0:T(8,128)(2,1)} %get-tuple-element.116.refs_5_.refs_4_.refs_12_), channel_id=1, source_target_pairs={{0,1},{1,0},{2,3},{3,2},{4,5},{5,4},{6,7},{7,6},{8,9},{9,8},{10,11... | collective-permute-start | bytes 3145736 | tf_op jit(solution)/shard_map/ppermute | solution.py:21
  54.2 27.3 %collective-permute-start.5 = (bf16[256,2048]{1,0:T(8,128)(2,1)}, bf16[256,2048]{1,0:T(8,128)(2,1)}, u32[]{:S(2)}, u32[]{:S(2)}) collective-permute-start(bf16[256,2048]{1,0:T(8,128)(2,1)} %get-tuple-element.115.refs_5_.refs_3_.refs_2_.refs_10_), channel_id=1, source_target_pairs={{0,1},{1,0},{2,3},{3,2},{4,5},{5,4},{6,7},{7,6},{8,9},{9,8},{10,11... | collective-permute-start | bytes 3145736 | tf_op jit(solution)/shard_map/ppermute | solution.py:21
  84.2 236.9 %all-gather.6.cloned.1.call-start = ((), (), s32[]{:S(2)}) async-start(), calls=%async_computation.4 | async-start | bytes 7864320 | tf_op jit(solution)/shard_map/all_gather | solution.py:113
  118.9 313.4 %reduce-scatter.4.cloned.1.call-start = ((), (), s32[]{:S(2)}) async-start(), calls=%async_computation.6 | async-start | bytes 7864320 | tf_op jit(solution)/shard_map/reduce_scatter | solution.py:151
  126.6 25.5 %collective-permute-start.14 = (bf16[1,1,2,128,2048]{4,3,2,1,0:T(8,128)(2,1)}, bf16[1,1,2,128,2048]{4,3,2,1,0:T(8,128)(2,1)}, u32[]{:S(2)}, u32[]{:S(2)}) collective-permute-start(bf16[1,1,2,128,2048]{4,3,2,1,0:T(8,128)(2,1)} %get-tuple-element.133), channel_id=1, source_target_pairs={{0,16},{16,0},{1,17},{17,1},{2,18},{18,2},{3,19},{19,3},{4,20},{20... | collective-permute-start | bytes 3145736 | tf_op jit(solution)/shard_map/ppermute | solution.py:21
  175.2 48.4 %collective-permute-start.18 = (bf16[512,2048]{1,0:T(8,128)(2,1)}, bf16[512,2048]{1,0:T(8,128)(2,1)}, u32[]{:S(2)}, u32[]{:S(2)}) collective-permute-start(bf16[512,2048]{1,0:T(8,128)(2,1)} %bitcast.56), channel_id=1, source_target_pairs={{0,16},{16,0},{1,17},{17,1},{2,18},{18,2},{3,19},{19,3},{4,20},{20... | collective-permute-start | bytes 6291464 | tf_op jit(solution)/shard_map/ppermute | solution.py:21
  175.9 48.0 %collective-permute-start.17 = (bf16[512,2048]{1,0:T(8,128)(2,1)}, bf16[512,2048]{1,0:T(8,128)(2,1)}, u32[]{:S(2)}, u32[]{:S(2)}) collective-permute-start(bf16[512,2048]{1,0:T(8,128)(2,1)} %bitcast.57), channel_id=1, source_target_pairs={{0,2},{1,3},{2,0},{3,1},{4,6},{5,7},{6,4},{7,5},{8,10},{9,11},{10,... | collective-permute-start | bytes 6291464 | tf_op jit(solution)/shard_map/ppermute | solution.py:21
  223.9 30.8 %collective-permute-start.20 = (bf16[512,2048]{1,0:T(8,128)(2,1)}, bf16[512,2048]{1,0:T(8,128)(2,1)}, u32[]{:S(2)}, u32[]{:S(2)}) collective-permute-start(bf16[512,2048]{1,0:T(8,128)(2,1)} %get-tuple-element.139.refs_1_.refs_2_.refs_10_.refs_18_.refs_26_), channel_id=1, source_target_pairs={{0,1},{1,0},{2,3},{3,2},{4,5},{5,4},{6,7},{7,6},{8,9},{9,8},{10,11... | collective-permute-start | bytes 6291464 | tf_op jit(solution)/shard_map/ppermute | solution.py:21
  223.9 30.8 %collective-permute-start.21 = (bf16[512,2048]{1,0:T(8,128)(2,1)}, bf16[512,2048]{1,0:T(8,128)(2,1)}, u32[]{:S(2)}, u32[]{:S(2)}) collective-permute-start(bf16[512,2048]{1,0:T(8,128)(2,1)} %get-tuple-element.140.refs_0_.refs_4_.refs_12_.refs_20_.refs_28_), channel_id=1, source_target_pairs={{0,1},{1,0},{2,3},{3,2},{4,5},{5,4},{6,7},{7,6},{8,9},{9,8},{10,11... | collective-permute-start | bytes 6291464 | tf_op jit(solution)/shard_map/ppermute | solution.py:21
  228.2 25.4 %collective-permute-start.23 = (bf16[256,2048]{1,0:T(8,128)(2,1)}, bf16[256,2048]{1,0:T(8,128)(2,1)}, u32[]{:S(2)}, u32[]{:S(2)}) collective-permute-start(bf16[256,2048]{1,0:T(8,128)(2,1)} %get-tuple-element.142), channel_id=1, source_target_pairs={{0,16},{16,0},{1,17},{17,1},{2,18},{18,2},{3,19},{19,3},{4,20},{20... | collective-permute-start | bytes 3145736 | tf_op jit(solution)/shard_map/ppermute | solution.py:21
  302.0 243.7 %reduce-scatter.6.cloned.1.call-start = ((), (), s32[]{:S(2)}) async-start(), calls=%async_computation.7 | async-start | bytes 7864320 | tf_op jit(solution)/shard_map/reduce_scatter | solution.py:151
  368.8 25.8 %collective-permute-start.29 = (bf16[1,1,2,128,2048]{4,3,2,1,0:T(8,128)(2,1)}, bf16[1,1,2,128,2048]{4,3,2,1,0:T(8,128)(2,1)}, u32[]{:S(2)}, u32[]{:S(2)}) collective-permute-start(bf16[1,1,2,128,2048]{4,3,2,1,0:T(8,128)(2,1)} %get-tuple-element.159), channel_id=1, source_target_pairs={{0,16},{16,0},{1,17},{17,1},{2,18},{18,2},{3,19},{19,3},{4,20},{20... | collective-permute-start | bytes 3145736 | tf_op jit(solution)/shard_map/ppermute | solution.py:21
  370.3 25.5 %collective-permute-start.28 = (bf16[1,2,1,128,2048]{4,3,2,1,0:T(8,128)(2,1)}, bf16[1,2,1,128,2048]{4,3,2,1,0:T(8,128)(2,1)}, u32[]{:S(2)}, u32[]{:S(2)}) collective-permute-start(bf16[1,2,1,128,2048]{4,3,2,1,0:T(8,128)(2,1)} %get-tuple-element.158.refs_17_), channel_id=1, source_target_pairs={{0,2},{1,3},{2,0},{3,1},{4,6},{5,7},{6,4},{7,5},{8,10},{9,11},{10,... | collective-permute-start | bytes 3145736 | tf_op jit(solution)/shard_map/ppermute | solution.py:21
  419.0 189.6 %reduce-scatter.8.cloned.1.call-start = ((), (), s32[]{:S(2)}) async-start(), calls=%async_computation.8 | async-start | bytes 3932160 | tf_op jit(solution)/shard_map/reduce_scatter | solution.py:151
  419.1 25.9 %collective-permute-start.33 = (bf16[256,2048]{1,0:T(8,128)(2,1)}, bf16[256,2048]{1,0:T(8,128)(2,1)}, u32[]{:S(2)}, u32[]{:S(2)}) collective-permute-start(bf16[256,2048]{1,0:T(8,128)(2,1)} %bitcast.30.refs_1_.refs_16_.refs_24_), channel_id=1, source_target_pairs={{0,16},{16,0},{1,17},{17,1},{2,18},{18,2},{3,19},{19,3},{4,20},{20... | collective-permute-start | bytes 3145736 | tf_op jit(solution)/shard_map/ppermute | solution.py:21
  419.8 25.5 %collective-permute-start.32 = (bf16[256,2048]{1,0:T(8,128)(2,1)}, bf16[256,2048]{1,0:T(8,128)(2,1)}, u32[]{:S(2)}, u32[]{:S(2)}) collective-permute-start(bf16[256,2048]{1,0:T(8,128)(2,1)} %bitcast.30.refs_1_.refs_16_.refs_24_), channel_id=1, source_target_pairs={{0,2},{1,3},{2,0},{3,1},{4,6},{5,7},{6,4},{7,5},{8,10},{9,11},{10,... | collective-permute-start | bytes 3145736 | tf_op jit(solution)/shard_map/ppermute | solution.py:21
  467.6 35.5 %collective-permute-start.43 = (bf16[4,128,2048]{2,1,0:T(8,128)(2,1)}, bf16[4,128,2048]{2,1,0:T(8,128)(2,1)}, u32[]{:S(2)}, u32[]{:S(2)}) collective-permute-start(bf16[4,128,2048]{2,1,0:T(8,128)(2,1)} %get-tuple-element.190), channel_id=1, source_target_pairs={{0,1},{1,0},{2,3},{3,2},{4,5},{5,4},{6,7},{7,6},{8,9},{9,8},{10,11... | collective-permute-start | bytes 6291464 | tf_op jit(solution)/shard_map/ppermute | solution.py:21
  467.8 35.4 %collective-permute-start.44 = (bf16[4,128,2048]{2,1,0:T(8,128)(2,1)}, bf16[4,128,2048]{2,1,0:T(8,128)(2,1)}, u32[]{:S(2)}, u32[]{:S(2)}) collective-permute-start(bf16[4,128,2048]{2,1,0:T(8,128)(2,1)} %get-tuple-element.191), channel_id=1, source_target_pairs={{0,1},{1,0},{2,3},{3,2},{4,5},{5,4},{6,7},{7,6},{8,9},{9,8},{10,11... | collective-permute-start | bytes 6291464 | tf_op jit(solution)/shard_map/ppermute | solution.py:21
  511.2 25.5 %collective-permute-start.47 = (bf16[1,1,2,128,2048]{4,3,2,1,0:T(8,128)(2,1)}, bf16[1,1,2,128,2048]{4,3,2,1,0:T(8,128)(2,1)}, u32[]{:S(2)}, u32[]{:S(2)}) collective-permute-start(bf16[1,1,2,128,2048]{4,3,2,1,0:T(8,128)(2,1)} %get-tuple-element.197), channel_id=1, source_target_pairs={{0,16},{16,0},{1,17},{17,1},{2,18},{18,2},{3,19},{19,3},{4,20},{20... | collective-permute-start | bytes 3145736 | tf_op jit(solution)/shard_map/ppermute | solution.py:21
  539.7 26.5 %collective-permute-start.51 = (bf16[1,1,2,128,2048]{4,3,2,1,0:T(8,128)(2,1)}, bf16[1,1,2,128,2048]{4,3,2,1,0:T(8,128)(2,1)}, u32[]{:S(2)}, u32[]{:S(2)}) collective-permute-start(bf16[1,1,2,128,2048]{4,3,2,1,0:T(8,128)(2,1)} %get-tuple-element.207), channel_id=1, source_target_pairs={{0,16},{16,0},{1,17},{17,1},{2,18},{18,2},{3,19},{19,3},{4,20},{20... | collective-permute-start | bytes 3145736 | tf_op jit(solution)/shard_map/ppermute | solution.py:21
  541.3 26.4 %collective-permute-start.50 = (bf16[1,2,1,128,2048]{4,3,2,1,0:T(8,128)(2,1)}, bf16[1,2,1,128,2048]{4,3,2,1,0:T(8,128)(2,1)}, u32[]{:S(2)}, u32[]{:S(2)}) collective-permute-start(bf16[1,2,1,128,2048]{4,3,2,1,0:T(8,128)(2,1)} %get-tuple-element.204.refs_6_), channel_id=1, source_target_pairs={{0,2},{1,3},{2,0},{3,1},{4,6},{5,7},{6,4},{7,5},{8,10},{9,11},{10,... | collective-permute-start | bytes 3145736 | tf_op jit(solution)/shard_map/ppermute | solution.py:21
  547.5 35.5 %collective-permute-start.54 = (bf16[1536,256]{1,0:T(8,128)(2,1)}, bf16[1536,256]{1,0:T(8,128)(2,1)}, u32[]{:S(2)}, u32[]{:S(2)}) collective-permute-start(bf16[1536,256]{1,0:T(8,128)(2,1)} %for_partner.4.refs_6_), channel_id=1, source_target_pairs={{0,16},{16,0},{1,17},{17,1},{2,18},{18,2},{3,19},{19,3},{4,20},{20... | collective-permute-start | bytes 2359304 | tf_op jit(solution)/shard_map/ppermute | solution.py:21
  549.0 63.3 %collective-permute-start.48 = (bf16[1,1,1,128,2048]{4,3,2,1,0:T(8,128)(2,1)}, bf16[1,1,1,128,2048]{4,3,2,1,0:T(8,128)(2,1)}, u32[]{:S(2)}, u32[]{:S(2)}) collective-permute-start(bf16[1,1,1,128,2048]{4,3,2,1,0:T(8,128)(2,1)} %get-tuple-element.205.refs_1_), channel_id=1, source_target_pairs={{0,16},{16,0},{1,17},{17,1},{2,18},{18,2},{3,19},{19,3},{4,20},{20... | collective-permute-start | bytes 1572872 | tf_op jit(solution)/shard_map/ppermute | solution.py:21
  549.6 62.3 %collective-permute-start.49 = (bf16[1,1,1,128,2048]{4,3,2,1,0:T(8,128)(2,1)}, bf16[1,1,1,128,2048]{4,3,2,1,0:T(8,128)(2,1)}, u32[]{:S(2)}, u32[]{:S(2)}) collective-permute-start(bf16[1,1,1,128,2048]{4,3,2,1,0:T(8,128)(2,1)} %get-tuple-element.206), channel_id=1, source_target_pairs={{0,2},{1,3},{2,0},{3,1},{4,6},{5,7},{6,4},{7,5},{8,10},{9,11},{10,... | collective-permute-start | bytes 1572872 | tf_op jit(solution)/shard_map/ppermute | solution.py:21
  570.5 42.9 %collective-permute-start.53 = (bf16[1,1,1,128,2048]{4,3,2,1,0:T(8,128)(2,1)}, bf16[1,1,1,128,2048]{4,3,2,1,0:T(8,128)(2,1)}, u32[]{:S(2)}, u32[]{:S(2)}) collective-permute-start(bf16[1,1,1,128,2048]{4,3,2,1,0:T(8,128)(2,1)} %get-tuple-element.209), channel_id=1, source_target_pairs={{0,2},{1,3},{2,0},{3,1},{4,6},{5,7},{6,4},{7,5},{8,10},{9,11},{10,... | collective-permute-start | bytes 1572872 | tf_op jit(solution)/shard_map/ppermute | solution.py:21
  571.1 42.6 %collective-permute-start.52 = (bf16[1,1,1,128,2048]{4,3,2,1,0:T(8,128)(2,1)}, bf16[1,1,1,128,2048]{4,3,2,1,0:T(8,128)(2,1)}, u32[]{:S(2)}, u32[]{:S(2)}) collective-permute-start(bf16[1,1,1,128,2048]{4,3,2,1,0:T(8,128)(2,1)} %get-tuple-element.208.refs_1_), channel_id=1, source_target_pairs={{0,16},{16,0},{1,17},{17,1},{2,18},{18,2},{3,19},{19,3},{4,20},{20... | collective-permute-start | bytes 1572872 | tf_op jit(solution)/shard_map/ppermute | solution.py:21
  (36 other events, 424.3 us)
Sparse Core Ops, SparseCore 0:
  25.3 64.9 all-gather.3
  91.8 114.0 all-gather.7
  207.5 113.5 all-gather.5
  323.2 108.9 reduce-scatter.3
  434.4 111.2 reduce-scatter.5
  547.8 60.7 reduce-scatter.7
